TPU v7x, 32 devices: a whole 2x2x4 slice. The times are simulated.
32 devices in a mesh: seq: 8 (over z, y), mp: 4 (over x, core).
Axes of the slice: x: 2, y: 2, z: 4, core: 2. Of those that a mesh axis runs over, the one named last changes fastest.
Arguments:
- block_input: bfloat16 [2, 16384, 512], P(None, ('seq', 'mp')), may hold values from -6 to 6
- cotangent: bfloat16 [2, 16384, 512], P(None, 'seq'), may hold values from -6 to 6
- span_offset: int32 [2], replicated, may hold values from 1 to 127
- doc_lengths: int32 [2, 8], replicated, may hold values from 1 to 15360, 16384 in all within a row
- ln1_gain: float32 [512], replicated, may hold values from 0.5 to 1.5
- ln1_bias: float32 [512], replicated, may hold values from -3 to 3
- w_query: bfloat16 [512, 512], P('seq', 'mp'), may hold values from -0.25 to 0.25
- w_key: bfloat16 [512, 512], P('seq', 'mp'), may hold values from -0.25 to 0.25
- w_value: bfloat16 [512, 512], P('seq', 'mp'), may hold values from -0.25 to 0.25
- query_bias: float32 [512], replicated, may hold values from -3 to 3
- value_bias: float32 [512], replicated, may hold values from -3 to 3
- w_out: bfloat16 [512, 512], P('mp', 'seq'), may hold values from -2 to 2
- out_bias: float32 [512], replicated, may hold values from -3 to 3
- ln2_gain: float32 [512], replicated, may hold values from 0.5 to 1.5
- ln2_bias: float32 [512], replicated, may hold values from -3 to 3
- w_up: bfloat16 [512, 2048], P('seq', 'mp'), may hold values from -0.25 to 0.25
- up_bias: float32 [2048], replicated, may hold values from -3 to 3
- w_down: bfloat16 [2048, 512], P('mp', 'seq'), may hold values from -0.75 to 0.75
- down_bias: float32 [512], replicated, may hold values from -3 to 3
Outputs:
- result: bfloat16 [2, 16384, 512], P(None, ('seq', 'mp'))
- input_grad: float32 [2, 16384, 512], P(None, ('seq', 'mp'))
- grad_ln1_gain: float32 [512], replicated
- grad_ln1_bias: float32 [512], replicated
- grad_w_query: float32 [512, 512], P('seq', 'mp')
- grad_w_key: float32 [512, 512], P('seq', 'mp')
- grad_w_value: float32 [512, 512], P('seq', 'mp')
- grad_query_bias: float32 [512], replicated
- grad_value_bias: float32 [512], replicated
- grad_w_out: float32 [512, 512], P('mp', 'seq')
- grad_out_bias: float32 [512], replicated
- grad_ln2_gain: float32 [512], replicated
- grad_ln2_bias: float32 [512], replicated
- grad_w_up: float32 [512, 2048], P('seq', 'mp')
- grad_up_bias: float32 [2048], replicated
- grad_w_down: float32 [2048, 512], P('mp', 'seq')
- grad_down_bias: float32 [512], replicated
Inputs may be any that keep to these rules, and one draw needn't show every extreme that they name: `doc_lengths`: each row's 8 lengths add up to 16384, and one document of each row has exactly 15360 positions.
All inputs are finite; a program needn't handle non-finite values.
Results may differ from a plain program's by a relative error of at most 0.012.
The roundings to bfloat16 on the way count: a program that leaves them out, or rounds other values in their place, can miss the bound.
Values may be sent and summed in bfloat16 or wider, within the bound.
No kernel may reach another device: no remote copies, remote signals or barrier semaphores. Data moves between devices by JAX's collectives and lax.ppermute only.
A program may use at most 128 MiB of HBM per device.

v0:
```python
from functools import partial
import math

import jax
import jax.numpy as jnp
from jax import lax
from jax.experimental import pallas as pl
from jax.experimental.pallas import tpu as pltpu
from jax.sharding import PartitionSpec as P

D = 512
FF = 2048
HEAD_DIM = 64
SPAN = 128
LANES = 128
STEP = 256
EPSILON = 1e-05
NEGATIVE = -1e30
SCALE = 1.0 / math.sqrt(HEAD_DIM)
F32 = jnp.float32
BF16 = jnp.bfloat16
AXES = ("seq", "mp")
MIB = 1 << 20
VMEM = pl.BlockSpec(memory_space=pltpu.VMEM)
SMEM = pl.BlockSpec(memory_space=pltpu.SMEM)
ANY = pl.BlockSpec(memory_space=pl.ANY)
HBM = pl.BlockSpec(memory_space=pltpu.HBM)


def dot(left, right):
    return lax.dot_general(left, right, (((1,), (0,)), ((), ())), preferred_element_type=F32)


def dot_cols(left, right):
    return lax.dot_general(left, right, (((1,), (1,)), ((), ())), preferred_element_type=F32)


def unit(rows):
    centred = rows - jnp.mean(rows, axis=-1, keepdims=True)
    inverse = lax.rsqrt(jnp.mean(centred * centred, axis=-1, keepdims=True) + EPSILON)
    return centred * inverse, inverse


def unit_back(grad, hat, inverse):
    shift = jnp.mean(grad, axis=-1, keepdims=True)
    slope = jnp.mean(grad * hat, axis=-1, keepdims=True)
    return (grad - shift - hat * slope) * inverse


def row_info(place, offsets, lengths, mi):
    ends = []
    for c in range(lengths.shape[1]):
        ends.append(lengths[mi, c] + (ends[-1] if ends else 0))
    return place[0], offsets[mi], ends


def doc_start(positions, ends):
    start = jnp.zeros_like(positions)
    for end in ends:
        start = jnp.where(positions >= end, end, start)
    return start


def summary_range(summary_ids, offset, ends):
    last = offset - 1 + SPAN * summary_ids
    first = jnp.maximum(doc_start(last, ends), last - (SPAN - 1))
    return first, last


def iota(shape, dim):
    return lax.broadcasted_iota(jnp.int32, shape, dim)


def roll_rows(ref, by):
    whole = pl.multiple_of((by // 8) * 8, 8)
    return pltpu.roll(ref[pl.ds(whole, SPAN + 8), :], SPAN + 8 - (by - whole), axis=0)[:SPAN]


def prepare_kernel(
    place, offsets, lengths, x_ref, cot_ref, wq_ref, wk_ref, wv_ref, wo_ref, wu_ref, wd_ref,
    out_ref, rest_ref, edge_ref, rows_ref, sem
):
    rows = x_ref.shape[1]
    last_rows = pl.multiple_of(place[1] * rows + (rows - SPAN), SPAN)
    shard = wq_ref.shape[0]
    copies = [pltpu.make_async_copy(x_ref.at[mi], rows_ref.at[mi], sem.at[mi]) for mi in range(2)]
    copies += [
        pltpu.make_async_copy(ref, out_ref.at[0, 0:shard, i * LANES : (i + 1) * LANES], sem.at[2 + i])
        for i, ref in enumerate((wq_ref, wk_ref, wv_ref))
    ]
    copies.append(pltpu.make_async_copy(cot_ref.at[:, pl.ds(last_rows, SPAN), :], edge_ref, sem.at[5]))
    copies.append(pltpu.make_async_copy(wo_ref, rest_ref.at[0, :, 0:128], sem.at[6]))
    for i, (ref, first) in enumerate(((wu_ref, 0), (wd_ref, 0), (wu_ref, 256), (wd_ref, 256))):
        target = rest_ref.at[0, :, 128 + 256 * i : 384 + 256 * i]
        copies.append(pltpu.make_async_copy(ref.at[:, first : first + 256], target, sem.at[7 + i]))
    for copy in copies:
        copy.start()
    sums = []
    for mi in range(2):
        dev, offset, ends = row_info(place, offsets, lengths, mi)
        first, last = summary_range(dev * (rows // SPAN) + iota((8, 1), 0), offset, ends)
        pos = dev * rows + iota((1, rows), 1)
        member = jnp.where((pos >= first) & (pos <= last), 1.0, 0.0).astype(BF16)
        copies[mi].wait()
        hat, _ = unit(rows_ref[mi].astype(F32))
        high = hat.astype(BF16)
        rest = (hat - high.astype(F32)).astype(BF16)
        total = dot(member, high) + dot(member, rest)
        sums.append(total * lax.rsqrt((last - first + 1).astype(F32)))
    both = jnp.concatenate(sums, axis=0).astype(BF16)
    for copy in copies[2:]:
        copy.wait()
    for lane in range(D // LANES):
        out_ref[0, 16 * lane : 16 * lane + 16, 384:512] = both[:, lane * LANES : (lane + 1) * LANES]


def fill_masks(place, offsets, lengths, mi, bias_ref, tiles, summaries, length):
    dev, offset, ends = row_info(place, offsets, lengths, mi)
    ends_col = offset - 1 + SPAN * iota((summaries, 1), 0)
    for t in range(tiles):
        base = SPAN * (dev * tiles + t) + offset - SPAN
        qpos = base + iota((1, SPAN), 1)
        qpos = jnp.where(qpos < 0, qpos + length, qpos)
        kpos = base + iota((SPAN, 1), 0)
        kpos = jnp.where(kpos < 0, kpos + length, kpos)
        span_first = jnp.where(qpos >= base + SPAN, base + length, base)
        doc_first = doc_start(qpos, ends)
        local_ok = (kpos >= jnp.maximum(doc_first, span_first)) & (kpos <= qpos)
        summary_ok = (ends_col >= doc_first) & (ends_col < span_first)
        bias_ref[t, 0:SPAN, :] = jnp.where(local_ok, 0.0, NEGATIVE)
        bias_ref[t, SPAN : SPAN + summaries, :] = jnp.where(summary_ok, 0.0, NEGATIVE)


def split_heads(pair):
    low = iota(pair.shape, 1) < HEAD_DIM
    zero = jnp.zeros_like(pair)
    return jnp.concatenate((jnp.where(low, pair, zero), jnp.where(low, zero, pair)), axis=0)


def join_heads(turned):
    half = turned.shape[1] // 2
    return jnp.concatenate((turned[:HEAD_DIM, :half], turned[HEAD_DIM:, half:]), axis=0).T


def project_kernel(
    apart, place_ref, offsets, lengths, block_of, row_of, slots_ref, x_ref, left_ref, gain, shift, qbias, vbias,
    near_ref, far_ref, *refs
):
    if apart:
        all_ref, *refs = refs
    xs_ref, qkv_ref, skv_ref, sums_ref, w_ref, stack_ref, wide_ref, rows_ref, sem = refs
    rows = x_ref.shape[1]
    tiles = rows // SPAN
    summaries = skv_ref.shape[1]
    half, shard, _ = near_ref.shape

    def place(d, carry):
        for source, slot in ((near_ref, d), (far_ref, half + d)):
            here = pl.ds(pl.multiple_of(row_of[slot] * shard, 16), shard)
            cols = pl.ds(pl.multiple_of(block_of[slot] * 384, 128), 384)
            pltpu.make_async_copy(source.at[d, :, 0:384], w_ref.at[here, cols], sem.at[0]).start()
            if not apart:
                pltpu.make_async_copy(
                    source.at[d, 0:64, 384:512], stack_ref.at[slot], sem.at[1]
                ).start()
        return carry

    lax.fori_loop(0, half, place, 0)
    if apart:
        pltpu.make_async_copy(all_ref, stack_ref, sem.at[1]).start()
    for mi in range(2):
        wide_ref[0:SPAN, :] = left_ref[mi].astype(F32)
        wide_ref[SPAN : SPAN + rows, :] = x_ref[mi].astype(F32)
        for t in range(tiles):
            here = slice(t * SPAN, (t + 1) * SPAN)
            rolled = roll_rows(wide_ref, t * SPAN + offsets[mi])
            xs_ref[mi, here, :] = rolled.astype(BF16)
            hat, _ = unit(rolled)
            rows_ref[mi, here, :] = (hat * gain[...] + shift[...]).astype(BF16)
    pltpu.make_async_copy(stack_ref, stack_ref, sem.at[1]).wait()
    roots = []
    for mi in range(2):
        _, offset, ends = row_info(place_ref, offsets, lengths, mi)
        first, last = summary_range(iota((summaries, 1), 0), offset, ends)
        root = jnp.sqrt((last - first + 1).astype(F32))
        roots.append(root)
        for base in range(0, stack_ref.shape[0], 32):
            named = slots_ref[mi : mi + 1, 16 * base : 16 * base + 512]
            pick = jnp.where(iota((summaries, 1), 0) == named, 1.0, 0.0).astype(BF16)
            piece = jnp.concatenate(
                [
                    stack_ref[base : base + 32, 16 * lane : 16 * lane + 16, :].reshape(512, LANES)
                    for lane in range(D // LANES)
                ],
                axis=1,
            )
            found = dot(pick, piece)
            sums_ref[mi] = found if base == 0 else sums_ref[mi] + found
        summed = sums_ref[mi] * gain[...] + root * shift[...]
        high = summed.astype(BF16)
        rows_ref[mi, rows : rows + summaries, :] = high
        rows_ref[mi, rows + summaries : rows + 2 * summaries, :] = (summed - high.astype(F32)).astype(BF16)
    pltpu.make_async_copy(w_ref, w_ref, sem.at[0]).wait()
    none = jnp.zeros((1, LANES), F32)
    for m in range(4):
        lanes = slice(m * LANES, (m + 1) * LANES)
        cols = slice(m * 384, (m + 1) * 384)
        bias = jnp.concatenate((qbias[:, lanes], none, vbias[:, lanes]), axis=1)
        for mi in range(2):
            projected = dot(rows_ref[mi], w_ref[:, cols])
            qkv_ref[mi, :, cols] = (projected[:rows] + bias).astype(BF16)
            pooled = projected[rows : rows + summaries] + projected[rows + summaries :]
            skv_ref[mi, :, cols] = (pooled + roots[mi] * bias).astype(BF16)


def pair_of(ref, here, pair):
    def part(i):
        return ref[0, here, pl.ds(pl.multiple_of(pair * 384 + i * LANES, LANES), LANES)]

    return part(0), part(1), part(2)


def attend_kernel(mi, place, offsets, lengths, qkv_ref, skv_ref, *refs):
    att_ref, lse_ref, bias_ref = refs[-3:]
    rows = qkv_ref.shape[1]
    tiles = rows // SPAN
    summaries = skv_ref.shape[1]
    fill_masks(place, offsets, lengths, mi, bias_ref, tiles, summaries, summaries * SPAN)

    def heads(pair, carry):
        lanes = pl.ds(pl.multiple_of(pair * LANES, LANES), LANES)
        _, skeys, svalues = pair_of(skv_ref, slice(None), pair)
        svalues = svalues.T
        spans = [pair_of(qkv_ref, slice(t * SPAN, (t + 1) * SPAN), pair) for t in range(tiles)]
        scores = []
        for t, (queries, keys, _) in enumerate(spans):
            bias = bias_ref[t]
            keys = jnp.concatenate((keys, skeys), axis=0)
            scores.append(dot_cols(keys, split_heads(queries * SCALE)) + jnp.concatenate((bias, bias), axis=1))
        probs = []
        for t in range(tiles):
            top = jnp.max(scores[t], axis=0, keepdims=True)
            grown = jnp.exp(scores[t] - top)
            total = jnp.sum(grown, axis=0, keepdims=True)
            probs.append((grown * (1.0 / total)).astype(BF16))
            lse_ref[0, pair, t] = top + jnp.log(total)
        for t, (_, _, values) in enumerate(spans):
            values = jnp.concatenate((values.T, svalues), axis=1)
            att_ref[0, t * SPAN : (t + 1) * SPAN, lanes] = join_heads(dot(values, probs[t])).astype(BF16)
        return carry

    lax.fori_loop(0, 4, heads, 0)


def gelu_pair(u):
    c0 = math.sqrt(2.0 / math.pi)
    square = u * u
    t = jnp.tanh(c0 * u * (1.0 + 0.044715 * square))
    half = 0.5 * (1.0 + t)
    slope = half + (0.5 * c0) * u * (1.0 - t * t) * (1.0 + (3 * 0.044715) * square)
    return u * half, slope


def columns(block, width):
    return pl.ds(pl.multiple_of(block * width, 128), width)


def mlp_half(half_id, ubias, n_ref, c_ref, nt_ref, ct_ref, wu_ref, wd_ref, gu_ref, gd_ref, gub_ref, act_ref, grad_ref, add):
    bias = jnp.concatenate([ubias[:, m * 512 + half_id * 256 : m * 512 + half_id * 256 + 256] for m in range(4)], axis=1)
    step = STEP
    gub_ref[...] = jnp.zeros_like(gub_ref)

    def block(r, carry):
        here = pl.ds(pl.multiple_of(r * step, step), step)
        w_up, w_down = wu_ref[...], wd_ref[...]
        act, slope = gelu_pair(dot(n_ref[here, :], w_up) + bias)
        act = act.astype(BF16)
        grad = dot(c_ref[here, :], w_down) * slope
        gub_ref[...] += jnp.sum(grad, axis=0, keepdims=True)
        grad = grad.astype(BF16)
        act_ref[here, :] = act
        grad_ref[here, :] = grad
        add(r, here, dot_cols(act, w_down), dot_cols(grad, w_up))
        return carry

    lax.fori_loop(0, n_ref.shape[0] // step, block, 0)
    gu_ref[...] = dot(nt_ref[...], grad_ref[...]).astype(BF16)
    gd_ref[...] = dot(ct_ref[...], act_ref[...]).astype(BF16)


def pull(block_of, row_of, near_ref, far_ref, parts):
    half, shard, _ = near_ref.shape

    def body(d, carry):
        for source, slot in ((near_ref, d), (far_ref, half + d)):
            here = pl.ds(pl.multiple_of(row_of[slot] * shard, 16), shard)
            for target, first, width, sem in parts:
                pltpu.make_async_copy(
                    source.at[d, :, first : first + width], target.at[here, columns(block_of[slot], width)], sem
                ).start()
        return carry

    lax.fori_loop(0, half, body, 0)


def push(block_of, row_of, keep_ref, send_ref, parts):
    half, shard, _ = keep_ref.shape

    def body(d, carry):
        for target, slot in ((keep_ref, d), (send_ref, half + d)):
            here = pl.ds(pl.multiple_of(row_of[slot] * shard, 16), shard)
            for source, first, width, sem in parts:
                pltpu.make_async_copy(
                    source.at[here, columns(block_of[slot], width)], target.at[d, :, first : first + width], sem
                ).start()
        return carry

    lax.fori_loop(0, half, body, 0)


def mlp_first_kernel(
    place_ref, offsets, block_of, row_of, xs_ref, att_ref, left_ref, obias, gain, shift, ubias, dbias, cot_ref,
    near_ref, far_ref,
    resid_ref, acc_ref, gn_ref, n_ref, c_ref, wo_ref, gub_ref, down_ref, keep_ref, send_ref,
    nt_ref, ct_ref, wu_ref, wd_ref, gu_ref, gd_ref, act_ref, grad_ref, wide_ref, low_ref, sem, out_sem,
):
    rows = xs_ref.shape[1]
    own = pl.ds(pl.multiple_of(place_ref[1] * rows, SPAN), rows)
    own_copy = pltpu.make_async_copy(cot_ref.at[:, own, :], low_ref, sem.at[3])
    own_copy.start()
    pull(block_of, row_of, near_ref, far_ref, ((wo_ref, 0, 128, sem.at[0]),))
    pull(block_of, row_of, near_ref, far_ref, ((wu_ref, 128, 256, sem.at[1]), (wd_ref, 384, 256, sem.at[2])))
    down_ref[...] = jnp.zeros_like(down_ref)
    own_copy.wait()
    pltpu.make_async_copy(wo_ref, wo_ref, sem.at[0]).wait()
    for mi in range(2):
        all_rows = slice(mi * rows, (mi + 1) * rows)
        wide_ref[0:SPAN, :] = left_ref[mi].astype(F32)
        wide_ref[SPAN : SPAN + rows, :] = low_ref[mi].astype(F32)
        for t in range(rows // SPAN):
            rolled = roll_rows(wide_ref, t * SPAN + offsets[mi])
            down_ref[...] += jnp.sum(rolled, axis=0, keepdims=True)
            c_ref[mi * rows + t * SPAN : mi * rows + (t + 1) * SPAN, :] = rolled.astype(BF16)
        resid = xs_ref[mi].astype(F32) + dot_cols(att_ref[mi], wo_ref[...]) + obias[...]
        resid_ref[all_rows, :] = resid
        hat, _ = unit(resid)
        normed = (hat * gain[...] + shift[...]).astype(BF16)
        n_ref[all_rows, :] = normed
        nt_ref[:, all_rows] = normed.T
        ct_ref[:, all_rows] = c_ref[all_rows, :].T
    pltpu.make_async_copy(wu_ref, wu_ref, sem.at[1]).wait()
    pltpu.make_async_copy(wd_ref, wd_ref, sem.at[2]).wait()

    def add(r, here, down, back):
        acc_ref[here, :] = (down + dbias[...]).astype(BF16)
        gn_ref[here, :] = back.astype(BF16)

    mlp_half(
        0, ubias, n_ref, c_ref, nt_ref, ct_ref, wu_ref, wd_ref, gu_ref, gd_ref, gub_ref, act_ref, grad_ref, add
    )
    push(block_of, row_of, keep_ref, send_ref, ((gu_ref, 0, 256, out_sem.at[0]), (gd_ref, 256, 256, out_sem.at[1])))
    pltpu.make_async_copy(gu_ref, gu_ref, out_sem.at[0]).wait()
    pltpu.make_async_copy(gd_ref, gd_ref, out_sem.at[1]).wait()


def mlp_second_kernel(
    block_of, row_of, att_ref, gain, ubias, resid_ref, acc_ref, gn_ref, n_ref, c_ref, wo_ref,
    near_ref, far_ref,
    result_ref, gmid_ref, gatt_ref, small_ref, gub_ref, keep_ref, send_ref,
    nt_ref, ct_ref, wu_ref, wd_ref, gu_ref, gd_ref, act_ref, grad_ref, go_ref, turned_ref, sem, out_sem,
):
    rows = att_ref.shape[1]
    pull(block_of, row_of, near_ref, far_ref, ((wu_ref, 0, 256, sem.at[0]), (wd_ref, 256, 256, sem.at[1])))
    small_ref[...] = jnp.zeros_like(small_ref)
    for mi in range(2):
        here = slice(mi * rows, (mi + 1) * rows)
        nt_ref[:, here] = n_ref[here, :].T
        ct_ref[:, here] = c_ref[here, :].T
    pltpu.make_async_copy(wu_ref, wu_ref, sem.at[0]).wait()
    pltpu.make_async_copy(wd_ref, wd_ref, sem.at[1]).wait()

    def add(r, here, down, back):
        mi = r // (rows // STEP)
        own = pl.ds(pl.multiple_of((r % (rows // STEP)) * STEP, STEP), STEP)
        result_ref[mi, own, :] = (resid_ref[here, :] + (acc_ref[here, :].astype(F32) + down)).astype(BF16)
        hat, inverse = unit(resid_ref[here, :])
        grad = gn_ref[here, :].astype(F32) + back
        small_ref[0:1, :] += jnp.sum(grad * hat, axis=0, keepdims=True)
        small_ref[1:2, :] += jnp.sum(grad, axis=0, keepdims=True)
        branch = (c_ref[here, :].astype(F32) + unit_back(grad * gain[...], hat, inverse)).astype(BF16)
        gmid_ref[mi, own, :] = branch
        small_ref[2:3, :] += jnp.sum(branch.astype(F32), axis=0, keepdims=True)
        gatt_ref[mi, own, :] = dot(branch, wo_ref[...]).astype(BF16)
        turned_ref[:, here] = branch.T

    mlp_half(
        1, ubias, n_ref, c_ref, nt_ref, ct_ref, wu_ref, wd_ref, gu_ref, gd_ref, gub_ref, act_ref, grad_ref, add
    )
    push(block_of, row_of, keep_ref, send_ref, ((gu_ref, 0, 256, out_sem.at[0]), (gd_ref, 256, 256, out_sem.at[1])))
    both = jnp.concatenate((att_ref[0], att_ref[1]), axis=0)
    go_ref[...] = dot(turned_ref[...], both).astype(BF16)
    push(block_of, row_of, keep_ref, send_ref, ((go_ref, 512, 128, out_sem.at[2]),))
    pltpu.make_async_copy(gu_ref, gu_ref, out_sem.at[0]).wait()
    pltpu.make_async_copy(gd_ref, gd_ref, out_sem.at[1]).wait()
    pltpu.make_async_copy(go_ref, go_ref, out_sem.at[2]).wait()


def attend_back_kernel(mi, place, offsets, lengths, qkv_ref, skv_ref, lse_ref, gatt_ref, *refs):
    grad_ref, pooled_ref, bias_ref = refs[-3:]
    rows = qkv_ref.shape[1]
    tiles = rows // SPAN
    summaries = skv_ref.shape[1]
    fill_masks(place, offsets, lengths, mi, bias_ref, tiles, summaries, summaries * SPAN)

    def heads(pair, carry):
        lanes = pl.ds(pl.multiple_of(pair * LANES, LANES), LANES)

        def columns(i):
            return pl.ds(pl.multiple_of(pair * 384 + i * LANES, LANES), LANES)

        _, skeys, svalues = pair_of(skv_ref, slice(None), pair)
        skeys_t = skeys.T
        sum_k = jnp.zeros((summaries, LANES), F32)
        sum_v = jnp.zeros((summaries, LANES), F32)
        held = []
        for t in range(tiles):
            here = slice(t * SPAN, (t + 1) * SPAN)
            queries, keys, values = pair_of(qkv_ref, here, pair)
            queries = split_heads(queries * SCALE)
            grads = split_heads(gatt_ref[0, here, lanes])
            bias = bias_ref[t]
            scores = dot_cols(jnp.concatenate((keys, skeys), axis=0), queries)
            gprobs = dot_cols(jnp.concatenate((values, svalues), axis=0), grads)
            held.append((queries, keys, grads, scores + jnp.concatenate((bias, bias), axis=1), gprobs))
        for t, (queries, keys, grads, scores, gprobs) in enumerate(held):
            here = slice(t * SPAN, (t + 1) * SPAN)
            probs = jnp.exp(scores - lse_ref[0, pair, t])
            delta = jnp.sum(probs * gprobs, axis=0, keepdims=True)
            gscores = (probs * (gprobs - delta)).astype(BF16)
            keys_t = jnp.concatenate((keys.T, skeys_t), axis=1)
            grad_q = join_heads(dot(keys_t, gscores)) * SCALE
            grad_k = dot(gscores, queries)
            grad_v = dot(probs.astype(BF16), grads)
            grad_ref[0, here, columns(0)] = grad_q.astype(BF16)
            grad_ref[0, here, columns(1)] = grad_k[:SPAN].astype(BF16)
            grad_ref[0, here, columns(2)] = grad_v[:SPAN].astype(BF16)
            sum_k += grad_k[SPAN:]
            sum_v += grad_v[SPAN:]
        pooled_ref[0, :, columns(0)] = jnp.zeros((summaries, LANES), BF16)
        pooled_ref[0, :, columns(1)] = sum_k.astype(BF16)
        pooled_ref[0, :, columns(2)] = sum_v.astype(BF16)
        return carry

    lax.fori_loop(0, 4, heads, 0)


def weights_back_kernel(
    apart, place, offsets, lengths, block_of, row_of, slots_ref, xs_ref, grad_ref, pooled_ref, sums_ref, w_ref,
    gain, shift, small_ref, down_ref, gub1_ref, gub2_ref, line_ref, keep_ref, send_ref, *refs
):
    if apart:
        all_ref, *refs = refs
    gwb_ref, back_ref, stack_ref, pad_ref, sem = refs
    rows = xs_ref.shape[1]
    summaries = pooled_ref.shape[1]
    half = block_of.shape[0] // 2
    shard = keep_ref.shape[0] // half
    turned = []
    column = jnp.zeros((1, 3 * D), F32)
    for mi in range(2):
        _, offset, ends = row_info(place, offsets, lengths, mi)
        first, last = summary_range(iota((summaries, 1), 0), offset, ends)
        root = jnp.sqrt((last - first + 1).astype(F32))
        hat, _ = unit(xs_ref[mi].astype(F32))
        turned += [hat.astype(BF16).T, sums_ref[mi].astype(BF16).T]
        column += jnp.sum(grad_ref[mi].astype(F32), axis=0, keepdims=True)
        column += jnp.sum(root * pooled_ref[mi].astype(F32), axis=0, keepdims=True)
        back_ref[mi] = dot_cols(pooled_ref[mi], w_ref[...]).astype(BF16)
    turned = jnp.concatenate(turned, axis=1)
    gain_col, shift_col = gain[...].T, shift[...].T
    grad_gain = jnp.zeros((D, 1), F32)
    grad_shift = jnp.zeros((D, 1), F32)
    for m in range(4):
        cols = slice(m * 384, (m + 1) * 384)
        lanes = slice(m * LANES, (m + 1) * LANES)
        grads = jnp.concatenate([ref[mi, :, cols] for mi in range(2) for ref in (grad_ref, pooled_ref)], axis=0)
        hats, w, sums = dot(turned, grads), w_ref[:, cols].astype(F32), column[:, cols]
        grad_gain += jnp.sum(hats * w, axis=1, keepdims=True)
        grad_shift += jnp.sum(sums * w, axis=1, keepdims=True)
        gwb_ref[:, cols] = (hats * gain_col + shift_col * sums).astype(BF16)
        line_ref[10:11, lanes] = sums[:, :128]
        line_ref[11:12, lanes] = sums[:, 256:]
    line_ref[8:9, :] = grad_gain.T
    line_ref[9:10, :] = grad_shift.T
    line_ref[0:3, :] = small_ref[0:3, :]
    line_ref[3:4, :] = down_ref[...]
    for i in range(4):
        for j, ref in enumerate((gub1_ref, gub2_ref)):
            line_ref[4 + i : 5 + i, j * 256 : (j + 1) * 256] = ref[:, i * 256 : (i + 1) * 256]
    line_ref[12:16, :] = jnp.zeros((4, D), F32)
    for base in range(0, stack_ref.shape[0], 32):
        names = [slots_ref[mi : mi + 1, 16 * base : 16 * base + 512] for mi in range(2)]
        spread = [
            jnp.where(iota((summaries, 1), 0) == named, 1.0, 0.0).astype(BF16).T for named in names
        ]
        piece = (dot(spread[0], back_ref[0]) + dot(spread[1], back_ref[1])).astype(BF16)
        for lane in range(D // LANES):
            part = piece[:, lane * LANES : (lane + 1) * LANES]
            stack_ref[base : base + 32, 16 * lane : 16 * lane + 16, :] = part.reshape(32, 16, LANES)

    def emit(d, carry):
        for target, slot in ((keep_ref, d), (send_ref, half + d)):
            first_row = pl.multiple_of(row_of[slot] * shard, 16)
            cols = pl.ds(pl.multiple_of(block_of[slot] * 384, 128), 384)
            here = target.at[pl.ds(pl.multiple_of(d * shard, 16), shard), :]
            pltpu.make_async_copy(
                gwb_ref.at[pl.ds(first_row, shard), cols], here.at[:, 0:384], sem.at[0]
            ).start()
            if not apart:
                pltpu.make_async_copy(stack_ref.at[slot], here.at[:, 384:512], sem.at[1]).start()
        return carry

    lax.fori_loop(0, half, emit, 0)
    if apart:
        pltpu.make_async_copy(stack_ref, all_ref, sem.at[1]).start()
    else:
        high = line_ref[...].astype(BF16)
        pad_ref[0:16, :] = high
        pad_ref[16:32, :] = (line_ref[...] - high.astype(F32)).astype(BF16)
        size = half * shard
        copy = pltpu.make_async_copy(pad_ref, send_ref.at[size : size + 32, :], sem.at[2])
        copy.start()
        copy.wait()
    pltpu.make_async_copy(gwb_ref, gwb_ref, sem.at[0]).wait()
    pltpu.make_async_copy(stack_ref, stack_ref, sem.at[1]).wait()


def rows_back_kernel(grad_ref, w_ref, xs_ref, gmid_ref, result_ref, gain, part_ref, edge_ref):
    grad = dot_cols(grad_ref[0], w_ref[...]) * gain[...]
    hat, inverse = unit(xs_ref[0].astype(F32))
    part = gmid_ref[0].astype(F32) + unit_back(grad, hat, inverse)
    part_ref[0] = part
    edge_ref[0, 0] = part[0:SPAN].astype(BF16)
    edge_ref[1, 0] = result_ref[0]


def fold_kernel(keep_ref, mine_ref, got_ref, next_ref, *send_refs):
    size = keep_ref.shape[0]
    part = size // (1 + len(send_refs))
    mine = mine_ref[0:16, :].astype(F32) + mine_ref[16:32, :].astype(F32)
    lines = mine + (got_ref[size : size + 16, :].astype(F32) + got_ref[size + 16 : size + 32, :].astype(F32))
    high = lines.astype(BF16)
    rest = (lines - high.astype(F32)).astype(BF16)
    next_ref[...] = keep_ref[0:part, :].astype(F32) + got_ref[0:part, :].astype(F32)
    for i, send_ref in enumerate(send_refs):
        here = slice((i + 1) * part, (i + 2) * part)
        send_ref[0:part, :] = (keep_ref[here, :].astype(F32) + got_ref[here, :].astype(F32)).astype(BF16)
        send_ref[part : part + 16, :] = high
        if len(send_refs) == 1:
            send_ref[part + 16 : part + 32, :] = rest


def lines_of(ref):
    return ref[ref.shape[0] - 16 :, :].astype(F32)


def two_tiles(ref, right, mi, t):
    if (t + 2) * SPAN <= ref.shape[1]:
        return ref[mi, t * SPAN : (t + 2) * SPAN, :]
    return jnp.concatenate((ref[mi, t * SPAN :, :], right[mi].astype(ref.dtype)), axis=0)


def unroll_kernel(offsets, result_ref, right_ref, x_ref, out_ref, hat_ref, inverse_ref, wide_ref):
    mi = pl.program_id(0)
    for t in range(result_ref.shape[1] // SPAN):
        here = slice(t * SPAN, (t + 1) * SPAN)
        wide_ref[...] = two_tiles(result_ref, right_ref.at[0], 0, t).astype(F32)
        out_ref[0, here, :] = roll_rows(wide_ref, SPAN - offsets[mi]).astype(BF16)
        hat, inverse = unit(x_ref[0, here, :].astype(F32))
        hat_ref[0, here, :] = hat.astype(BF16)
        inverse_ref[0, here, :] = jnp.broadcast_to(inverse, (SPAN, LANES))


def finish_rest_kernel(keep_ref, got_ref, wo_ref, wu_ref, wd_ref):
    total = keep_ref[0] + got_ref[0].astype(F32)
    for i in range(2):
        wu_ref[:, i * 256 : (i + 1) * 256] = total[:, i * 512 : i * 512 + 256]
        wd_ref[:, i * 256 : (i + 1) * 256] = total[:, i * 512 + 256 : i * 512 + 512]
    wo_ref[...] = total[:, 1024:]


def finish_kernel(
    direct, place, offsets, lengths, hat_ref, inverse_ref, part_ref, right_ref, gain, *refs
):
    if direct:
        keep_ref, mine_ref, a_ref, b_ref, c_ref, out_ref, wq_ref, wk_ref, wv_ref, *line_refs, wide_ref = refs
        size = keep_ref.shape[0]
        total = (keep_ref[...] + a_ref[0:size, :].astype(F32)) + (
            b_ref[0:size, :].astype(F32) + c_ref[0:size, :].astype(F32)
        )
        wq_ref[...], wk_ref[...], wv_ref[...] = total[:, :128], total[:, 128:256], total[:, 256:384]
        pooled = total[:, 384:]
        lines = (lines_of(mine_ref) + lines_of(a_ref)) + (lines_of(b_ref) + lines_of(c_ref))
        ub_ref, *line_refs = line_refs
        for i in range(4):
            ub_ref[:, i * D : (i + 1) * D] = lines[4 + i : 5 + i, :]
        for ref, i in zip(line_refs, (0, 1, 2, 3, 8, 9, 10, 11)):
            ref[...] = lines[i : i + 1, :]
    else:
        pooled_ref, out_ref, wide_ref = refs
        pooled = pooled_ref[...]
    rows = hat_ref.shape[1]
    for mi in range(2):
        dev, offset, ends = row_info(place, offsets, lengths, mi)
        first, last = summary_range(dev * (rows // SPAN) + iota((8, 1), 0), offset, ends)
        lows = jnp.concatenate(
            [pooled[16 * i + 8 * mi : 16 * i + 8 * mi + 8, :] for i in range(D // LANES)], axis=1
        )
        lows = lows * gain[...] * lax.rsqrt((last - first + 1).astype(F32))
        level = (lows - jnp.mean(lows, axis=-1, keepdims=True)).astype(BF16)
        lows = lows.astype(BF16)
        first, last = summary_range(dev * (rows // SPAN) + iota((1, 8), 1), offset, ends)
        for t in range(rows // SPAN):
            here = slice(t * SPAN, (t + 1) * SPAN)
            pos = dev * rows + t * SPAN + iota((SPAN, 1), 0)
            member = jnp.where((pos >= first) & (pos <= last), 1.0, 0.0)
            hat = hat_ref[mi, here, :]
            slope = jnp.sum(member * dot_cols(hat, lows), axis=1, keepdims=True) * (1.0 / D)
            inverse = inverse_ref[mi, here, 0:1]
            wide_ref[...] = two_tiles(part_ref, right_ref.at[0], mi, t)
            own = roll_rows(wide_ref, SPAN - offset)
            out_ref[mi, here, :] = own + (dot(member.astype(BF16), level) - hat.astype(F32) * slope) * inverse


def call(kernel, outs, in_specs, out_specs=None, scratch=(), limit=8, **more):
    return pl.pallas_call(
        kernel,
        out_shape=outs,
        in_specs=in_specs,
        out_specs=out_specs if out_specs is not None else [VMEM] * len(outs),
        scratch_shapes=list(scratch),
        compiler_params=pltpu.CompilerParams(vmem_limit_bytes=limit * MIB),
        cost_estimate=pl.CostEstimate(flops=1, bytes_accessed=1, transcendentals=0),
        **more,
    )


def call_row(kernel, mi, facts, arrays, outs, before, scratch, **more):
    def block(dims):
        return pl.BlockSpec((1,) + dims[1:], lambda i: (mi,) + (0,) * (len(dims) - 1))

    aliases = {3 + len(arrays) + i: i for i in range(len(before))}
    return call(
        partial(kernel, mi), outs, [SMEM] * 3 + [block(a.shape) for a in arrays] + [ANY] * len(before),
        [block(o.shape) for o in outs], scratch, grid=(1,), input_output_aliases=aliases, **more,
    )(*facts, *arrays, *before)


def tie(value, *others):
    return lax.optimization_barrier((value,) + others)[0]


def per_device(
    block_input, cotangent, span_offset, doc_lengths, ln1_gain, ln1_bias, w_query, w_key, w_value,
    query_bias, value_bias, w_out, out_bias, ln2_gain, ln2_bias, w_up, up_bias, w_down, down_bias,
):
    groups, ranks = lax.axis_size("seq"), lax.axis_size("mp")
    count = groups * ranks
    mp_index = lax.axis_index("mp")
    dev = lax.axis_index("seq") * ranks + mp_index
    rows = block_input.shape[1]
    tiles = rows // SPAN
    summaries = tiles * count
    shard = w_query.shape[0]
    bits = count.bit_length() - 1
    stages = [(b, b) for b in range(bits - 1, 2, -1)] + [(1, 2), (2, 1)]
    direct = shard == 64

    def swap(value, stage):
        pairs = [(i, i ^ (1 << stage[i & 1])) for i in range(count)]
        return lax.ppermute(value, AXES, pairs)

    def turn(value, by):
        return lax.ppermute(value, AXES, [(i, (i + by) % count) for i in range(count)])

    core = dev & 1
    slot = jnp.arange(count, dtype=jnp.int32)
    far = slot // (count // 2)
    mask = far
    for i, (even, odd) in enumerate(stages):
        where = jnp.where((core ^ far) == 0, even, odd)
        mask = mask | (((slot >> i) & 1) << where)
    owner = dev ^ mask
    if not direct:
        owner = slot
    member_slot = jnp.arange(16, dtype=jnp.int32)
    slots = owner[:, None] * tiles + (member_slot % 8)[None, :]
    valid = (member_slot % 8 <= tiles)[None, :]
    slots = jnp.stack(
        [
            jnp.where(valid & (member_slot // 8 == mi)[None, :], slots, -1).reshape(-1)
            for mi in range(2)
        ]
    )
    block_of, row_of = owner % ranks, owner // ranks
    facts = (jnp.stack((dev, mp_index)), span_offset, doc_lengths)

    def reach(value, flip):
        return lax.ppermute(value, AXES, [(i, i ^ flip) for i in range(count)])

    def spread(values):
        return [reach(value, flip) for value, flip in zip(values, (16, 8, 24))]

    def join(near, far):
        return jnp.concatenate((near, far), axis=0)

    def fold(keep, got):
        total = keep + got.astype(F32)
        half = total.shape[0] // 2
        return total[:half], total[half:].astype(BF16)

    def whole_blocks(arrays):
        return [pl.BlockSpec(a.shape, lambda i, n=len(a.shape): (0,) * n) for a in arrays]

    def fold_lines(keep, sent, got, sends=1):
        size = keep.shape[0]
        part = size // (1 + sends)
        outs = [shape((part, D), F32)] + [shape((part + (32 if sends == 1 else 16), D), BF16)] * sends
        mine = pl.BlockSpec((32, D), lambda i: (size // 32, 0))
        both = whole_blocks((keep, got))
        return call(fold_kernel, outs, [both[0], mine, both[1]], whole_blocks(outs), grid=(1,))(keep, sent, got)

    def gather_whole(value):
        both = lax.all_gather(value, "seq", axis=0, tiled=True)
        both = lax.all_gather(both, "mp", axis=0)
        return both[: ranks // 2], both[ranks // 2 :]

    def scatter_whole(keep, send):
        both = jnp.concatenate((keep, send), axis=0).astype(F32)
        total = lax.psum_scatter(both, "mp", scatter_dimension=0, tiled=True)[0]
        return lax.psum_scatter(total, "seq", scatter_dimension=0, tiled=True)

    def row(vector):
        return vector[None, :]

    def shape(dims, kind):
        return jax.ShapeDtypeStruct(dims, kind)

    half, tall = (count // 2, shard) if direct else (ranks // 2, shard * groups)
    width = 4 * LANES if direct else 3 * LANES
    apart = not direct
    wide, three = (2, rows, D), (2, rows, 3 * D)
    flat, pooled_dims = (2 * rows, D), (2, summaries, D)
    room = 12 if direct else 56
    masks = [pltpu.VMEM((tiles, SPAN + summaries, SPAN), F32)]

    def prepare():
        return call(
            prepare_kernel, [shape((1, max(shard, 64), D), BF16), shape((1, shard, 1152), BF16), shape((2, SPAN, D), BF16)],
            [SMEM] * 3 + [HBM] * 8, [VMEM] * 3,
            scratch=[pltpu.VMEM(wide, BF16), pltpu.SemaphoreType.DMA((11,))],
            limit=56,
        )(*facts, block_input, cotangent, w_query, w_key, w_value, w_out.T, w_up, w_down.T)

    part_a, w_rest, cot_edge = prepare()
    x_edge = block_input[:, rows - SPAN :]
    if direct:
        got_a = spread([part_a] * 3)
        part_b = tie(w_rest, got_a[0])
        got_b = swap(part_b, stages[0])
        part_a = jnp.concatenate([part_a] + got_a, axis=0)
        x_left = turn(tie(x_edge, part_a), 1)
        got_a = swap(part_a, stages[2])
        part_a = join(part_a, got_a)
        part_b = join(part_b, tie(got_b, part_a))
        got_a, got_b = swap(part_a, stages[3]), swap(part_b, stages[1])
        near_a = join(part_a, tie(got_a, x_left))
        far_a = swap(near_a, (0, 0))
        part_b = join(part_b, tie(got_b, near_a))
        got_b = swap(part_b, stages[2])
        more = ()
    else:
        x_left, cot_left = turn(x_edge, 1), turn(cot_edge, 1)
        near_a, far_a = gather_whole(part_a[0, :shard, :384])
        near_b, far_b = gather_whole(w_rest[0])
        near_1, near_2, far_1, far_2 = (a[:, :, i : i + w] for a in (near_b, far_b) for i, w in ((0, 640), (640, 512)))
        more = (lax.all_gather(part_a[0, :64, 384:], AXES, axis=0),)
        block_of, row_of = jnp.arange(ranks, dtype=jnp.int32), jnp.zeros((ranks,), jnp.int32)

    xs, qkv, skv, sums, w_full = call(
        partial(project_kernel, apart),
        [shape(wide, BF16), shape(three, BF16), shape((2, summaries, 3 * D), BF16), shape(pooled_dims, F32)]
        + [shape((D, 3 * D), BF16)],
        [SMEM] * 5 + [VMEM] * 7 + [ANY] * (2 + len(more)),
        scratch=[
            pltpu.VMEM((count, 64, LANES), BF16),
            pltpu.VMEM((rows + SPAN, D), F32),
            pltpu.VMEM((2, rows + 2 * summaries, D), BF16),
            pltpu.SemaphoreType.DMA((2,)),
        ],
        limit=24 if direct else 56,
    )(
        *facts, block_of, row_of, slots, block_input, x_left, row(ln1_gain), row(ln1_bias),
        row(query_bias), row(value_bias), near_a, far_a, *more,
    )
    outs = [shape(wide, BF16), shape((2, 4, tiles, 1, 2 * SPAN), F32)]
    if direct:
        cot_left = turn(tie(cot_edge, near_a), 1)
        part_b = join(part_b, tie(got_b, skv, cot_left))
        part_1, part_2 = part_b[:, :, :640], part_b[:, :, 640:]
        got_1 = swap(part_1, stages[3])
        qkv = tie(qkv, part_1)
    seen = call_row(attend_kernel, 0, facts, (qkv, skv), outs, (), masks, limit=room)
    att, lse = call_row(attend_kernel, 1, facts, (qkv, skv), outs, tuple(seen), masks, limit=room)
    if direct:
        near_1 = join(part_1, tie(got_1, att))
        far_1 = swap(near_1, (0, 0))
        got_2 = swap(tie(part_2, near_1), stages[3])
    tall_low, tall_float = shape(flat, BF16), shape(flat, F32)
    weights = [pltpu.VMEM((D, 2 * rows), BF16)] * 2 + [pltpu.VMEM((D, FF // 2), BF16)] * 4
    weights += [pltpu.VMEM((2 * rows, FF // 2), BF16)] * 2
    *kept, gub_1, down_b, keep_1, send_1 = call(
        mlp_first_kernel,
        [tall_float] + [tall_low] * 4 + [shape((D, D), BF16)]
        + [shape((1, FF // 2), F32), shape((1, D), F32)] + [shape((half, tall, 512), BF16)] * 2,
        [SMEM] * 4 + [VMEM] * 8 + [HBM] + [ANY] * 2,
        [VMEM] * 8 + [ANY] * 2,
        scratch=weights
        + [pltpu.VMEM((rows + SPAN, D), F32), pltpu.VMEM(wide, BF16)]
        + [pltpu.SemaphoreType.DMA((4,)), pltpu.SemaphoreType.DMA((2,))],
        limit=28,
    )(
        facts[0], span_offset, block_of, row_of, xs, att, cot_left, row(out_bias), row(ln2_gain), row(ln2_bias),
        row(up_bias), row(down_bias), cotangent, near_1, far_1,
    )
    if direct:
        near_2 = join(part_2, tie(got_2, kept[0]))
        far_2 = swap(near_2, (0, 0))
        got_1 = swap(tie(send_1, near_2), (0, 0))
        keep_1, send_1 = fold(keep_1.astype(F32), got_1)
        got_1 = swap(send_1, stages[3])
        near_2 = tie(near_2, send_1)
    result, gmid, gatt, small_b, gub_2, keep_2, send_2 = call(
        mlp_second_kernel,
        [shape(wide, BF16)] * 3 + [shape((8, D), F32)]
        + [shape((1, FF // 2), F32)] + [shape((half, tall, 640), BF16)] * 2,
        [SMEM] * 2 + [VMEM] * 9 + [ANY] * 2,
        [VMEM] * 5 + [ANY] * 2,
        scratch=weights
        + [pltpu.VMEM((D, D), BF16), pltpu.VMEM((D, 2 * rows), BF16)]
        + [pltpu.SemaphoreType.DMA((2,)), pltpu.SemaphoreType.DMA((3,))],
        limit=28,
    )(block_of, row_of, att, row(ln2_gain), row(up_bias), *kept, near_2, far_2)
    gubs = (gub_1, gub_2)
    arrays = (qkv, skv, lse, gatt)
    outs = [shape(three, BF16), shape((2, summaries, 3 * D), BF16)]
    if direct:
        keep_1, send_1 = fold(keep_1, tie(got_1, send_2))
        got_2 = swap(tie(send_2, send_1), (0, 0))
        got_1 = swap(send_1, stages[2])
    grads = call_row(attend_back_kernel, 0, facts, arrays, outs, (), masks, limit=room)
    if direct:
        keep_2, send_2 = fold(keep_2.astype(F32), tie(got_2, grads[0]))
        got_2 = swap(send_2, stages[3])
        grads = [tie(grads[0], send_2)] + list(grads[1:])
    grads = call_row(attend_back_kernel, 1, facts, arrays, outs, tuple(grads), masks, limit=room)
    if direct:
        keep_1, send_1 = fold(keep_1, tie(got_1, grads[0]))
        grads = [tie(grads[0], send_1), grads[1]]
    lines, keep_a, send_a, *more = call(
        partial(weights_back_kernel, apart),
        [shape((16, D), F32)]
        + [shape((half * tall, width), BF16), shape((half * tall + (32 if direct else 0), width), BF16)]
        + [shape((count, 64, LANES), BF16)] * apart,
        [SMEM] * 5 + [VMEM] * 12,
        [VMEM] + [ANY] * (2 + apart),
        scratch=[
            pltpu.VMEM((D, 3 * D), BF16), pltpu.VMEM(pooled_dims, BF16), pltpu.VMEM((count, 64, LANES), BF16),
            pltpu.VMEM((32, D), BF16), pltpu.SemaphoreType.DMA((3,)),
        ],
        limit=24 if direct else 56,
    )(
        *facts, block_of, row_of, slots, xs, *grads, sums, w_full, row(ln1_gain), row(ln1_bias), small_b, down_b, *gubs,
    )

    def by_row(dims):
        return pl.BlockSpec((1,) + dims[1:], lambda i: (i,) + (0,) * (len(dims) - 1))

    once = pl.BlockSpec((1, D), lambda i: (0, 0))
    edge_dims = (2, SPAN, D)

    def rows_back(*after):
        return call(
            rows_back_kernel, [shape(wide, F32), shape((2,) + edge_dims, BF16)],
            [by_row(three), pl.BlockSpec((D, 3 * D), lambda i: (0, 0)), by_row(wide), by_row(wide)]
            + [by_row(edge_dims), once],
            [by_row(wide), pl.BlockSpec((2, 1, SPAN, D), lambda i: (0, i, 0, 0))], grid=(2,), limit=16,
        )(grads[0], tie(w_full, *after), xs, gmid, result, row(ln1_gain))

    def unroll(back):
        return call(
            unroll_kernel, [shape(wide, BF16)] * 2 + [shape((2, rows, LANES), F32)],
            [SMEM, by_row(wide), pl.BlockSpec((1, 1, SPAN, D), lambda i: (1, i, 0, 0)), by_row(wide)], [by_row(wide)] * 2 + [by_row((2, rows, LANES))],
            [pltpu.VMEM((2 * SPAN, D), F32)], grid=(2,),
        )(span_offset, result, back, block_input)

    final = [SMEM] * 3 + [VMEM] * 5
    rolled = [pltpu.VMEM((2 * SPAN, D), F32)]
    if direct:
        got_a = swap(send_a, (0, 0))
        keep_2, send_2 = fold(keep_2, tie(got_2, send_a))
        got_2 = swap(send_2, stages[2])
        keep_a, send_a = fold_lines(keep_a, send_a, tie(got_a, send_2))
        got_a = swap(send_a, stages[3])
        part, edge = rows_back(send_a)
        keep_2, send_2 = fold(keep_2, tie(got_2, part))
        keep_b, send_b = (jnp.concatenate(a, axis=2) for a in ((keep_1, keep_2), (send_1, send_2)))
        got_b = swap(send_b, stages[1])
        back = turn(tie(edge, send_b), -1)
        keep_a, send_a = fold_lines(keep_a, send_a, tie(got_a, send_b))
        got_a = swap(send_a, stages[2])
        keep_b, send_b = fold(keep_b, tie(got_b, send_a))
        got_b = swap(send_b, stages[0])
        keep_a, *send_a = fold_lines(keep_a, send_a, tie(got_a, send_b), 3)
        got_a = spread(send_a)
        result_own, *hats = unroll(tie(back, send_a[0]))
        grad_wo, grad_wu, grad_wd = call(
            finish_rest_kernel, [shape((shard, LANES), F32), shape((shard, 512), F32), shape((shard, 512), F32)],
            [VMEM] * 2,
        )(keep_b, tie(got_b, send_a[0]))
        input_grad, grad_wq, grad_wk, grad_wv, grad_ub, *small = call(
            partial(finish_kernel, True),
            [shape(wide, F32)] + [shape((shard, LANES), F32)] * 3 + [shape((1, FF), F32)] + [shape((1, D), F32)] * 8,
            final + [VMEM] * 5, scratch=rolled, limit=16,
        )(*facts, *hats, part, back, row(ln1_gain), keep_a, send_a[0], *(tie(got, grad_wo) for got in got_a))
        grad_wo, grad_wd = grad_wo.T, grad_wd.T
        small = [a.reshape(D) for a in small]
        grad_ub = grad_ub.reshape(FF)
    else:
        keep_a, send_a = (a.reshape(half, tall, width) for a in (keep_a, send_a))
        part, edge = rows_back()
        back = turn(edge, -1)
        result_own, *hats = unroll(back)
        sum_a, sum_1, sum_2 = (scatter_whole(*a) for a in ((keep_a, send_a), (keep_1, send_1), (keep_2, send_2)))
        grad_wq, grad_wk, grad_wv = (sum_a[:, i : i + LANES] for i in (0, 128, 256))
        grad_wo = sum_2[:, 512:].T
        grad_wu, grad_wd = (
            jnp.concatenate((sum_1[:, i : i + 256], sum_2[:, i : i + 256]), axis=1) for i in (0, 256)
        )
        grad_wd = grad_wd.T
        pooled = lax.psum_scatter(more[0].astype(F32), AXES, scatter_dimension=0, tiled=True)[0]
        lines = lax.psum(lines, AXES)
        grad_ub = lines[4:8].reshape(FF)
        small = [lines[i] for i in (0, 1, 2, 3, 8, 9, 10, 11)]
        input_grad = call(partial(finish_kernel, False), [shape(wide, F32)], final + [VMEM], scratch=rolled, limit=16)(
            *facts, *hats, part, back, row(ln1_gain), pooled
        )[0]
    grad_gain_two, grad_shift_two, grad_obias, grad_dbias, grad_gain_one, grad_shift_one, grad_qb, grad_vb = small
    return (
        result_own,
        input_grad,
        grad_gain_one,
        grad_shift_one,
        grad_wq,
        grad_wk,
        grad_wv,
        grad_qb,
        grad_vb,
        grad_wo,
        grad_obias,
        grad_gain_two,
        grad_shift_two,
        grad_wu,
        grad_ub,
        grad_wd,
        grad_dbias,
    )


def solution(mesh):
    vector, matrix, turned = P(), P("seq", "mp"), P("mp", "seq")
    own, group = P(None, ("seq", "mp"), None), P(None, "seq", None)
    return jax.shard_map(
        per_device,
        mesh=mesh,
        in_specs=(own, group, vector, vector, vector, vector, matrix, matrix, matrix, vector, vector)
        + (turned, vector, vector, vector, matrix, vector, turned, vector),
        out_specs=(own, own, vector, vector, matrix, matrix, matrix, vector, vector, turned, vector)
        + (vector, vector, matrix, vector, turned, vector),
        check_vma=False,
    )
```

profile of v0, /device:TPU:0, one launch (start us, length us, event | category | flops | bytes accessed | tf_op | source)
XLA Modules:
  0.0 155.7 jit_solution(9719458516894731539)
XLA Ops:
  0.7 0.6 pad_add_fusion.1.place.place_ref
  1.2 3.9 %shard_map.314 = (bf16[1,64,512]{2,1,0:T(8,128)(2,1)}, bf16[1,64,1152]{2,1,0:T(8,128)(2,1)}, bf16[2,128,512]{2,1,0:T(8,128)(2,1)}) custom-call(s32[2]{0:T(128)} %pad_add_fusion.1.place.place_ref, s32[2]{0:T(128)} %offsets.19, s32[2,8]{1,0:T(2,128)} %lengths.15, bf16[2,512,512]{2,1,0:T(8,128)(2,1)} %x_ref.5, bf16[2,2048,512]{2,1,0:T(8,128)(2,1)} %cot_ref.3, ...), custom_call_target="tpu_custom_call" | custom-call | flops 1 | bytes 1 | tf_op jit(solution)/shard_map/pallas_call | solution.py:758
  5.1 5.1 %collective-permute-start.2 = (bf16[1,64,512]{2,1,0:T(8,128)(2,1)}, bf16[1,64,512]{2,1,0:T(8,128)(2,1)S(1)}, u32[]{:S(2)}, u32[]{:S(2)}) collective-permute-start(bf16[1,64,512]{2,1,0:T(8,128)(2,1)} %get-tuple-element.113), channel_id=1, source_target_pairs={{0,24},{1,25},{2,26},{3,27},{4,28},{5,29},{6,30},{7,31},{8,16},{9,... | collective-permute-start | bytes 196616 | tf_op jit(solution)/shard_map/ppermute | solution.py:709
  10.3 0.6 collective-permute-start
  10.9 0.9 constant_dynamic-update-slice_fusion.8
  11.8 4.3 %collective-permute-done = bf16[1,64,512]{2,1,0:T(8,128)(2,1)S(1)} collective-permute-done((bf16[1,64,512]{2,1,0:T(8,128)(2,1)}, bf16[1,64,512]{2,1,0:T(8,128)(2,1)S(1)}, u32[]{:S(2)}, u32[]{:S(2)}) %collective-permute-start) | collective-permute-done | bytes 65568 | tf_op jit(solution)/shard_map/ppermute | solution.py:709
  16.2 1.6 collective-permute-start.4
  17.8 2.0 %collective-permute-start.7 = (bf16[1,64,1152]{2,1,0:T(8,128)(2,1)S(1)}, bf16[1,64,1152]{2,1,0:T(8,128)(2,1)S(1)}, u32[]{:S(2)}, u32[]{:S(2)}) collective-permute-start(bf16[1,64,1152]{2,1,0:T(8,128)(2,1)S(1)} %copy-done.15), channel_id=1, source_target_pairs={{0,16},{1,17},{2,18},{3,19},{4,20},{5,21},{6,22},{7,23},{8,24},{9,... | collective-permute-start | bytes 442376 | tf_op jit(solution)/shard_map/ppermute | solution.py:681
  19.8 2.8 %collective-permute-done.4 = bf16[4,64,512]{2,1,0:T(8,128)(2,1)S(1)} collective-permute-done((bf16[4,64,512]{2,1,0:T(8,128)(2,1)S(1)}, bf16[4,64,512]{2,1,0:T(8,128)(2,1)S(1)}, u32[]{:S(2)}, u32[]{:S(2)}) %collective-permute-start.4) | collective-permute-done | bytes 262176 | tf_op jit(solution)/shard_map/ppermute | solution.py:681
  22.6 0.7 constant_dynamic-update-slice_fusion.4
  23.4 1.5 collective-permute-start.5
  24.9 0.1 add_select_fusion.1
  25.0 0.1 select_n.110
  25.1 0.1 select_n.112
  25.1 1.0 collective-permute-done.7
  26.2 0.6 collective-permute-start.8
  26.8 10.5 %collective-permute-done.3.left_ref = bf16[2,128,512]{2,1,0:T(8,128)(2,1)S(1)} collective-permute-done((bf16[2,128,512]{2,1,0:T(8,128)(2,1)S(1)}, bf16[2,128,512]{2,1,0:T(8,128)(2,1)S(1)}, u32[]{:S(2)}, u32[]{:S(2)}) %collective-permute-start.3) | collective-permute-done | bytes 262176 | tf_op jit(solution)/shard_map/ppermute | solution.py:684
  37.6 0.1 pad_maximum_fusion.2
  37.8 0.7 collective-permute-start.10
  38.6 1.6 %collective-permute-done.6.far_ref = bf16[16,64,512]{2,1,0:T(8,128)(2,1)S(1)} collective-permute-done((bf16[16,64,512]{2,1,0:T(8,128)(2,1)S(1)}, bf16[16,64,512]{2,1,0:T(8,128)(2,1)S(1)}, u32[]{:S(2)}, u32[]{:S(2)}) %collective-permute-start.6) | collective-permute-done | bytes 1048608 | tf_op jit(solution)/shard_map/ppermute | solution.py:681
  40.2 6.5 %shard_map.315 = (bf16[2,512,512]{2,1,0:T(8,128)(2,1)S(1)}, bf16[2,512,1536]{2,1,0:T(8,128)(2,1)S(1)}, bf16[2,128,1536]{2,1,0:T(8,128)(2,1)S(1)}, f32[2,128,512]{2,1,0:T(8,128)S(1)}, bf16[512,1536]{1,0:T(8,128)(2,1)S(1)}) custom-call(s32[2]{0:T(128)S(1)} %copy-done.4, s32[2]{0:T(128)S(1)} %copy-done.3, s32[2,8]{1,0:T(2,128)S(1)} %copy-done.2, ...), custom_call_target="tpu_custom_call" | custom-call | flops 1 | bytes 1 | tf_op jit(solution)/shard_map/pallas_call | solution.py:790
  46.8 0.8 collective-permute-done.10.left_ref
  47.6 2.9 %collective-permute-done.9 = bf16[4,64,1152]{2,1,0:T(8,128)(2,1)S(1)} collective-permute-done((bf16[4,64,1152]{2,1,0:T(8,128)(2,1)S(1)}, bf16[4,64,1152]{2,1,0:T(8,128)(2,1)S(1)}, u32[]{:S(2)}, u32[]{:S(2)}) %collective-permute-start.9) | collective-permute-done | bytes 589856 | tf_op jit(solution)/shard_map/ppermute | solution.py:681
  50.6 1.8 %collective-permute-start.11 = (bf16[8,64,640]{2,1,0:T(8,128)(2,1)S(1)}, bf16[8,64,640]{2,1,0:T(8,128)(2,1)S(1)}, u32[]{:S(2)}, u32[]{:S(2)}) collective-permute-start(bf16[8,64,640]{2,1,0:T(8,128)(2,1)S(1)} %slice.75), channel_id=1, source_target_pairs={{0,4},{1,3},{2,6},{3,1},{4,0},{5,7},{6,2},{7,5},{8,12},{9,11},{10,... | collective-permute-start | bytes 1966088 | tf_op jit(solution)/shard_map/ppermute | solution.py:681
  52.4 3.9 %shard_map.316 = (bf16[2,512,512]{2,1,0:T(8,128)(2,1)S(1)}, f32[2,4,4,1,256]{4,3,2,1,0:T(1,128)S(1)}) custom-call(s32[2]{0:T(128)S(1)} %copy-done.4, s32[2]{0:T(128)S(1)} %copy-done.3, s32[2,8]{1,0:T(2,128)S(1)} %copy-done.2, bf16[2,512,1536]{2,1,0:T(8,128)(2,1)S(1)} %get-tuple-element.125.qkv_ref, bf16[2,128,1536]{2,1,0:T(8,128)(2,1)S(1)} %get-tuple-element.121.skv_ref), custom_call_target="tpu_custom_call" | custom-call | flops 1 | bytes 1 | tf_op jit(solution)/shard_map/pallas_call | solution.py:653
  56.2 3.9 %shard_map.317 = (bf16[2,512,512]{2,1,0:T(8,128)(2,1)S(1)}, f32[2,4,4,1,256]{4,3,2,1,0:T(1,128)S(1)}) custom-call(s32[2]{0:T(128)S(1)} %copy-done.4, s32[2]{0:T(128)S(1)} %copy-done.3, s32[2,8]{1,0:T(2,128)S(1)} %copy-done.2, bf16[2,512,1536]{2,1,0:T(8,128)(2,1)S(1)} %get-tuple-element.125.qkv_ref, ...), custom_call_target="tpu_custom_call", output_to_operand_aliasing={{0}: (5, {}), {1}: (6, {})} | custom-call | flops 1 | bytes 1 | tf_op jit(solution)/shard_map/pallas_call | solution.py:653
  60.1 1.1 collective-permute-done.11
  61.2 0.1 pad_maximum_fusion.near_ref
  61.5 1.8 %collective-permute-start.13 = (bf16[8,64,512]{2,1,0:T(8,128)(2,1)S(1)}, bf16[8,64,512]{2,1,0:T(8,128)(2,1)S(1)}, u32[]{:S(2)}, u32[]{:S(2)}) collective-permute-start(bf16[8,64,512]{2,1,0:T(8,128)(2,1)S(1)} %slice.76), channel_id=1, source_target_pairs={{0,4},{1,3},{2,6},{3,1},{4,0},{5,7},{6,2},{7,5},{8,12},{9,11},{10,... | collective-permute-start | bytes 1572872 | tf_op jit(solution)/shard_map/ppermute | solution.py:681
  63.3 1.2 collective-permute-done.12.far_ref
  64.5 13.8 %shard_map.318 = (f32[1024,512]{1,0:T(8,128)S(1)}, bf16[1024,512]{1,0:T(8,128)(2,1)S(1)}, bf16[1024,512]{1,0:T(8,128)(2,1)S(1)}, bf16[1024,512]{1,0:T(8,128)(2,1...) custom-call(s32[2]{0:T(128)S(1)} %copy-done.4, ...), custom_call_target="tpu_custom_call" | custom-call | flops 1 | bytes 1 | tf_op jit(solution)/shard_map/pallas_call | solution.py:822
  78.4 0.1 pad_maximum_fusion.1.near_ref
  78.5 0.2 collective-permute-start.14
  78.6 0.4 collective-permute-start.15
  79.0 2.1 %collective-permute-done.14 = bf16[16,64,512]{2,1,0:T(8,128)(2,1)S(1)} collective-permute-done((bf16[16,64,512]{2,1,0:T(8,128)(2,1)S(1)}, bf16[16,64,512]{2,1,0:T(8,128)(2,1)S(1)}, u32[]{:S(2)}, u32[]{:S(2)}) %collective-permute-start.14) | collective-permute-done | bytes 1048608 | tf_op jit(solution)/shard_map/ppermute | solution.py:681
  81.2 0.3 convert_add_fusion.1
  81.6 1.8 %collective-permute-start.16 = (bf16[8,64,512]{2,1,0:T(8,128)(2,1)S(1)}, bf16[8,64,512]{2,1,0:T(8,128)(2,1)S(1)}, u32[]{:S(2)}, u32[]{:S(2)}) collective-permute-start(bf16[8,64,512]{2,1,0:T(8,128)(2,1)S(1)} %slice.103), channel_id=1, source_target_pairs={{0,4},{1,3},{2,6},{3,1},{4,0},{5,7},{6,2},{7,5},{8,12},{9,11},{10,... | collective-permute-start | bytes 1572872 | tf_op jit(solution)/shard_map/ppermute | solution.py:681
  83.4 14.5 %shard_map.319 = (bf16[2,512,512]{2,1,0:T(8,128)(2,1)S(1)}, bf16[2,512,512]{2,1,0:T(8,128)(2,1)S(1)}, bf16[2,512,512]{2,1,0:T(8,128)(2,1)S(1)}, f32[8,512]{1,0:T...) custom-call(s32[32]{0:T(128)S(1)} %get-tuple-element.226.block_of, ...), custom_call_target="tpu_custom_call" | custom-call | flops 1 | bytes 1 | tf_op jit(solution)/shard_map/pallas_call | solution.py:843
  97.9 0.2 slice_add_fusion.1
  98.2 4.2 %shard_map.320 = (bf16[2,512,1536]{2,1,0:T(8,128)(2,1)S(1)}, bf16[2,128,1536]{2,1,0:T(8,128)(2,1)S(1)}) custom-call(s32[2]{0:T(128)S(1)} %copy-done.4, s32[2]{0:T(128)S(1)} %copy-done.3, s32[2,8]{1,0:T(2,128)S(1)} %copy-done.2, bf16[2,512,1536]{2,1,0:T(8,128)(2,1)S(1)} %get-tuple-element.125.qkv_ref, bf16[2,128,1536]{2,1,0:T(8,128)(2,1)S(1)} %get-tuple-element.121.skv_ref, ...), custom_call_target="tpu_custom_call" | custom-call | flops 1 | bytes 1 | tf_op jit(solution)/shard_map/pallas_call | solution.py:653
  102.4 2.2 %collective-permute-start.18 = (bf16[4,64,512]{2,1,0:T(8,128)(2,1)S(1)}, bf16[4,64,512]{2,1,0:T(8,128)(2,1)S(1)}, u32[]{:S(2)}, u32[]{:S(2)}) collective-permute-start(bf16[4,64,512]{2,1,0:T(8,128)(2,1)S(1)} %slice.105), channel_id=1, source_target_pairs={{0,2},{1,5},{2,0},{3,7},{4,6},{5,1},{6,4},{7,3},{8,10},{9,13},{10,... | collective-permute-start | bytes 786440 | tf_op jit(solution)/shard_map/ppermute | solution.py:681
  104.6 0.3 convert_add_fusion
  104.9 1.2 collective-permute-start.20
  106.2 4.4 %shard_map.321 = (bf16[2,512,1536]{2,1,0:T(8,128)(2,1)S(1)}, bf16[2,128,1536]{2,1,0:T(8,128)(2,1)S(1)}) custom-call(s32[2]{0:T(128)S(1)} %copy-done.4, s32[2]{0:T(128)S(1)} %copy-done.3, s32[2,8]{1,0:T(2,128)S(1)} %copy-done.2, bf16[2,512,1536]{2,1,0:T(8,128)(2,1)S(1)} %get-tuple-element.125.qkv_ref, ...), custom_call_target="tpu_custom_call", output_to_operand_aliasing={{0}: (7, {}), {1}: (8, {})} | custom-call | flops 1 | bytes 1 | tf_op jit(solution)/shard_map/pallas_call | solution.py:653
  110.6 0.1 slice_add_fusion.3
  110.8 7.0 %shard_map.322 = (f32[16,512]{1,0:T(8,128)}, bf16[1024,512]{1,0:T(8,128)(2,1)S(1)}, bf16[1056,512]{1,0:T(8,128)(2,1)S(1)}) custom-call(s32[2]{0:T(128)S(1)} %copy-done.4, s32[2]{0:T(128)S(1)} %copy-done.3, s32[2,8]{1,0:T(2,128)S(1)} %copy-done.2, s32[32]{0:T(128)S(1)} %get-tuple-element.226.block_of, s32[32]{0:T(128)S(1)} %get-tuple-element.225.row_of, ...), custom_call_target="tpu_custom_call" | custom-call | flops 1 | bytes 1 | tf_op jit(solution)/shard_map/pallas_call | solution.py:870
  117.8 0.2 slice_add_fusion
  118.1 2.5 %collective-permute-start.21 = (bf16[4,64,640]{2,1,0:T(8,128)(2,1)S(1)}, bf16[4,64,640]{2,1,0:T(8,128)(2,1)S(1)}, u32[]{:S(2)}, u32[]{:S(2)}) collective-permute-start(bf16[4,64,640]{2,1,0:T(8,128)(2,1)S(1)} %slice.104), channel_id=1, source_target_pairs={{0,2},{1,5},{2,0},{3,7},{4,6},{5,1},{6,4},{7,3},{8,10},{9,13},{10,... | collective-permute-start | bytes 983048 | tf_op jit(solution)/shard_map/ppermute | solution.py:681
  120.5 0.2 shard_map.323
  120.8 2.9 %collective-permute-start.23 = (bf16[544,512]{1,0:T(8,128)(2,1)S(1)}, bf16[544,512]{1,0:T(8,128)(2,1)S(1)}, u32[]{:S(2)}, u32[]{:S(2)}) collective-permute-start(bf16[544,512]{1,0:T(8,128)(2,1)S(1)} %get-tuple-element.168.mine_ref), channel_id=1, source_target_pairs={{0,4},{1,3},{2,6},{3,1},{4,0},{5,7},{6,2},{7,5},{8,12},{9,11},{10,... | collective-permute-start | bytes 1671176 | tf_op jit(solution)/shard_map/ppermute | solution.py:681
  123.7 2.8 %shard_map.324 = (f32[2,512,512]{2,1,0:T(8,128)S(1)}, bf16[2,2,128,512]{3,2,1,0:T(8,128)(2,1)S(1)}) custom-call(bf16[2,512,1536]{2,1,0:T(8,128)(2,1)S(1)} %get-tuple-element.156.grad_ref, bf16[512,1536]{1,0:T(8,128)(2,1)S(1)} %get-tuple-element.169.w_ref, bf16[2,512,512]{2,1,0:T(8,128)(2,1)S(1)} %get-tuple-element.129.xs_ref, ...), custom_call_target="tpu_custom_call" | custom-call | flops 1 | bytes 1 | tf_op jit(solution)/shard_map/pallas_call | solution.py:893
  126.4 0.5 collective-permute-done.21
  126.9 0.1 slice_add_fusion.2
  127.1 0.5 collective-permute-start.22
  127.6 4.2 %collective-permute-done.23.got_ref = bf16[544,512]{1,0:T(8,128)(2,1)S(1)} collective-permute-done((bf16[544,512]{1,0:T(8,128)(2,1)S(1)}, bf16[544,512]{1,0:T(8,128)(2,1)S(1)}, u32[]{:S(2)}, u32[]{:S(2)}) %collective-permute-start.23) | collective-permute-done | bytes 557088 | tf_op jit(solution)/shard_map/ppermute | solution.py:681
  131.8 0.1 shard_map.325
  131.9 1.5 collective-permute-start.24
  133.4 2.1 %collective-permute-done.25 = bf16[2,64,1152]{2,1,0:T(8,128)(2,1)S(1)} collective-permute-done((bf16[2,64,1152]{2,1,0:T(8,128)(2,1)S(1)}, bf16[2,64,1152]{2,1,0:T(8,128)(2,1)S(1)}, u32[]{:S(2)}, u32[]{:S(2)}) %collective-permute-start.25) | collective-permute-done | bytes 294944 | tf_op jit(solution)/shard_map/ppermute | solution.py:681
  135.7 7.6 %collective-permute-done.24.got_ref = bf16[288,512]{1,0:T(8,128)(2,1)S(1)} collective-permute-done((bf16[288,512]{1,0:T(8,128)(2,1)S(1)}, bf16[288,512]{1,0:T(8,128)(2,1)S(1)}, u32[]{:S(2)}, u32[]{:S(2)}) %collective-permute-start.24) | collective-permute-done | bytes 294944 | tf_op jit(solution)/shard_map/ppermute | solution.py:681
  143.5 3.4 %collective-permute-start.26 = (bf16[80,512]{1,0:T(8,128)(2,1)S(1)}, bf16[80,512]{1,0:T(8,128)(2,1)S(1)}, u32[]{:S(2)}, u32[]{:S(2)}) collective-permute-start(bf16[80,512]{1,0:T(8,128)(2,1)S(1)} %get-tuple-element.181.refs_1_), channel_id=1, source_target_pairs={{0,16},{1,17},{2,18},{3,19},{4,20},{5,21},{6,22},{7,23},{8,24},{9,... | collective-permute-start | bytes 245768 | tf_op jit(solution)/shard_map/ppermute | solution.py:709
  146.9 3.0 %shard_map.327 = (bf16[2,512,512]{2,1,0:T(8,128)(2,1)}, bf16[2,512,512]{2,1,0:T(8,128)(2,1)S(1)}, f32[2,512,128]{2,1,0:T(8,128)S(1)}) custom-call(s32[2]{0:T(128)S(1)} %copy-done.3, bf16[2,512,512]{2,1,0:T(8,128)(2,1)S(1)} %get-tuple-element.143.result_ref, bf16[2,2,128,512]{3,2,1,0:T(8,128)(2,1)S(1)} %collective-permute-done.22.right_ref, ...), custom_call_target="tpu_custom_call" | custom-call | flops 1 | bytes 1 | tf_op jit(solution)/shard_map/pallas_call | solution.py:901
  149.9 0.7 shard_map.328
  150.6 1.3 collective-permute-done.26.refs_2_
  151.9 3.6 %shard_map.329 = (f32[2,512,512]{2,1,0:T(8,128)}, f32[64,128]{1,0:T(8,128)}, f32[64,128]{1,0:T(8,128)}, f32[64,128]{1,0:T(8,128)}, f32[1,2048]{1,0:T(1,128)}, /*...) custom-call(s32[2]{0:T(128)S(1)} %copy-done.4, ...), custom_call_target="tpu_custom_call" | custom-call | flops 1 | bytes 1 | tf_op jit(solution)/shard_map/pallas_call | solution.py:931
  (93 shorter events, 1.7 us)
Async XLA Ops:
  1.2 16.5 %copy-start.1 = (bf16[2,512,512]{2,1,0:T(8,128)(2,1)S(1)}, bf16[2,512,512]{2,1,0:T(8,128)(2,1)}, u32[]{:S(2)}) copy-start(bf16[2,512,512]{2,1,0:T(8,128)(2,1)} %x_ref.5) | copy-start | bytes 3145732
  5.1 12.7 %copy-start.15 = (bf16[1,64,1152]{2,1,0:T(8,128)(2,1)S(1)}, bf16[1,64,1152]{2,1,0:T(8,128)(2,1)}, u32[]{:S(2)}) copy-start(bf16[1,64,1152]{2,1,0:T(8,128)(2,1)} %get-tuple-element.118) | copy-start | bytes 442372
  5.1 11.0 %collective-permute-start.2 = (bf16[1,64,512]{2,1,0:T(8,128)(2,1)}, bf16[1,64,512]{2,1,0:T(8,128)(2,1)S(1)}, u32[]{:S(2)}, u32[]{:S(2)}) collective-permute-start(bf16[1,64,512]{2,1,0:T(8,128)(2,1)} %get-tuple-element.113), channel_id=1, source_target_pairs={{0,24},{1,25},{2,26},{3,27},{4,28},{5,29},{6,30},{7,31},{8,16},{9,... | collective-permute-start | bytes 196616 | tf_op jit(solution)/shard_map/ppermute | solution.py:709
  10.2 5.9 %collective-permute-start.1 = (bf16[1,64,512]{2,1,0:T(8,128)(2,1)}, bf16[1,64,512]{2,1,0:T(8,128)(2,1)S(1)}, u32[]{:S(2)}, u32[]{:S(2)}) collective-permute-start(bf16[1,64,512]{2,1,0:T(8,128)(2,1)} %get-tuple-element.113), channel_id=1, source_target_pairs={{0,8},{1,9},{2,10},{3,11},{4,12},{5,13},{6,14},{7,15},{8,0},{9,1},... | collective-permute-start | bytes 196616 | tf_op jit(solution)/shard_map/ppermute | solution.py:709
  10.3 5.8 %collective-permute-start = (bf16[1,64,512]{2,1,0:T(8,128)(2,1)}, bf16[1,64,512]{2,1,0:T(8,128)(2,1)S(1)}, u32[]{:S(2)}, u32[]{:S(2)}) collective-permute-start(bf16[1,64,512]{2,1,0:T(8,128)(2,1)} %get-tuple-element.113), channel_id=1, source_target_pairs={{0,16},{1,17},{2,18},{3,19},{4,20},{5,21},{6,22},{7,23},{8,24},{9,... | collective-permute-start | bytes 196616 | tf_op jit(solution)/shard_map/ppermute | solution.py:709
  16.2 1.6 %copy-start.16 = (bf16[8,64,512]{2,1,0:T(8,128)(2,1)}, bf16[8,64,512]{2,1,0:T(8,128)(2,1)S(1)}, u32[]{:S(2)}) copy-start(bf16[8,64,512]{2,1,0:T(8,128)(2,1)S(1)} %get-tuple-element.211) | copy-start | bytes 1572868
  16.2 6.4 %collective-permute-start.4 = (bf16[4,64,512]{2,1,0:T(8,128)(2,1)S(1)}, bf16[4,64,512]{2,1,0:T(8,128)(2,1)S(1)}, u32[]{:S(2)}, u32[]{:S(2)}) collective-permute-start(bf16[4,64,512]{2,1,0:T(8,128)(2,1)S(1)} %get-tuple-element.213), channel_id=1, source_target_pairs={{0,2},{1,5},{2,0},{3,7},{4,6},{5,1},{6,4},{7,3},{8,10},{9,13},{10,... | collective-permute-start | bytes 786440 | tf_op jit(solution)/shard_map/ppermute | solution.py:681
  17.8 8.3 %collective-permute-start.7 = (bf16[1,64,1152]{2,1,0:T(8,128)(2,1)S(1)}, bf16[1,64,1152]{2,1,0:T(8,128)(2,1)S(1)}, u32[]{:S(2)}, u32[]{:S(2)}) collective-permute-start(bf16[1,64,1152]{2,1,0:T(8,128)(2,1)S(1)} %copy-done.15), channel_id=1, source_target_pairs={{0,16},{1,17},{2,18},{3,19},{4,20},{5,21},{6,22},{7,23},{8,24},{9,... | collective-permute-start | bytes 442376 | tf_op jit(solution)/shard_map/ppermute | solution.py:681
  23.4 14.0 %collective-permute-start.5 = (bf16[8,64,512]{2,1,0:T(8,128)(2,1)}, bf16[8,64,512]{2,1,0:T(8,128)(2,1)S(1)}, u32[]{:S(2)}, u32[]{:S(2)}) collective-permute-start(bf16[8,64,512]{2,1,0:T(8,128)(2,1)} %get-tuple-element.209), channel_id=1, source_target_pairs={{0,4},{1,3},{2,6},{3,1},{4,0},{5,7},{6,2},{7,5},{8,12},{9,11},{10,... | collective-permute-start | bytes 1572872 | tf_op jit(solution)/shard_map/ppermute | solution.py:681
  25.1 12.2 %collective-permute-start.3 = (bf16[2,128,512]{2,1,0:T(8,128)(2,1)S(1)}, bf16[2,128,512]{2,1,0:T(8,128)(2,1)S(1)}, u32[]{:S(2)}, u32[]{:S(2)}) collective-permute-start(bf16[2,128,512]{2,1,0:T(8,128)(2,1)S(1)} %slice.58), channel_id=1, source_target_pairs={{0,1},{1,2},{2,3},{3,4},{4,5},{5,6},{6,7},{7,8},{8,9},{9,10},{10,1... | collective-permute-start | bytes 786440 | tf_op jit(solution)/shard_map/ppermute | solution.py:684
  26.2 11.6 %copy-start.17 = (bf16[2,128,512]{2,1,0:T(8,128)(2,1)S(1)}, bf16[2,128,512]{2,1,0:T(8,128)(2,1)}, u32[]{:S(2)}) copy-start(bf16[2,128,512]{2,1,0:T(8,128)(2,1)} %get-tuple-element.123) | copy-start | bytes 786436
  26.2 11.4 %collective-permute-start.8 = (bf16[2,64,1152]{2,1,0:T(8,128)(2,1)S(1)}, bf16[2,64,1152]{2,1,0:T(8,128)(2,1)S(1)}, u32[]{:S(2)}, u32[]{:S(2)}) collective-permute-start(bf16[2,64,1152]{2,1,0:T(8,128)(2,1)S(1)} %pad_maximum_fusion.3), channel_id=1, source_target_pairs={{0,8},{1,9},{2,10},{3,11},{4,12},{5,13},{6,14},{7,15},{8,0},{9,1},... | collective-permute-start | bytes 884744 | tf_op jit(solution)/shard_map/ppermute | solution.py:681
  37.4 2.8 %copy-start.2 = (s32[2,8]{1,0:T(2,128)S(1)}, s32[2,8]{1,0:T(2,128)}, u32[]{:S(2)}) copy-start(s32[2,8]{1,0:T(2,128)} %lengths.15) | copy-start | bytes 196
  37.4 2.8 %copy-start.3 = (s32[2]{0:T(128)S(1)}, s32[2]{0:T(128)}, u32[]{:S(2)}) copy-start(s32[2]{0:T(128)} %offsets.19) | copy-start | bytes 28
  37.4 2.8 %copy-start.4 = (s32[2]{0:T(128)S(1)}, s32[2]{0:T(128)}, u32[]{:S(2)}) copy-start(s32[2]{0:T(128)} %pad_add_fusion.1.place.place_ref) | copy-start | bytes 28
  37.4 2.8 %copy-start.6 = (f32[512]{0:T(512)S(1)}, f32[512]{0:T(512)}, u32[]{:S(2)}) copy-start(f32[512]{0:T(512)} %param.23) | copy-start | bytes 6148
  37.4 2.8 %copy-start.8 = (f32[512]{0:T(512)S(1)}, f32[512]{0:T(512)}, u32[]{:S(2)}) copy-start(f32[512]{0:T(512)} %param.24) | copy-start | bytes 6148
  37.4 2.8 %copy-start.12 = (f32[512]{0:T(512)S(1)}, f32[512]{0:T(512)}, u32[]{:S(2)}) copy-start(f32[512]{0:T(512)} %param.28) | copy-start | bytes 6148
  37.5 2.8 %copy-start.13 = (f32[512]{0:T(512)S(1)}, f32[512]{0:T(512)}, u32[]{:S(2)}) copy-start(f32[512]{0:T(512)} %param.29) | copy-start | bytes 6148
  37.5 2.7 %collective-permute-start.6 = (bf16[16,64,512]{2,1,0:T(8,128)(2,1)S(1)}, bf16[16,64,512]{2,1,0:T(8,128)(2,1)S(1)}, u32[]{:S(2)}, u32[]{:S(2)}) collective-permute-start(bf16[16,64,512]{2,1,0:T(8,128)(2,1)S(1)} %constant_dynamic-update-slice_fusion.9.near_ref), channel_id=1, source_target_pairs={{0,1},{1,0},{2,3},{3,2},{4,5},{5,4},{6,7},{7,6},{8,9},{9,8},{10,11... | collective-permute-start | bytes 3145736 | tf_op jit(solution)/shard_map/ppermute | solution.py:681
  37.7 12.8 %collective-permute-start.9 = (bf16[4,64,1152]{2,1,0:T(8,128)(2,1)S(1)}, bf16[4,64,1152]{2,1,0:T(8,128)(2,1)S(1)}, u32[]{:S(2)}, u32[]{:S(2)}) collective-permute-start(bf16[4,64,1152]{2,1,0:T(8,128)(2,1)S(1)} %pad_maximum_fusion.2), channel_id=1, source_target_pairs={{0,2},{1,5},{2,0},{3,7},{4,6},{5,1},{6,4},{7,3},{8,10},{9,13},{10,... | collective-permute-start | bytes 1769480 | tf_op jit(solution)/shard_map/ppermute | solution.py:681
  37.8 9.8 %collective-permute-start.10 = (bf16[2,128,512]{2,1,0:T(8,128)(2,1)S(1)}, bf16[2,128,512]{2,1,0:T(8,128)(2,1)S(1)}, u32[]{:S(2)}, u32[]{:S(2)}) collective-permute-start(bf16[2,128,512]{2,1,0:T(8,128)(2,1)S(1)} %copy-done.17), channel_id=1, source_target_pairs={{0,1},{1,2},{2,3},{3,4},{4,5},{5,6},{6,7},{7,8},{8,9},{9,10},{10,1... | collective-permute-start | bytes 786440 | tf_op jit(solution)/shard_map/ppermute | solution.py:684
  50.6 10.7 %collective-permute-start.11 = (bf16[8,64,640]{2,1,0:T(8,128)(2,1)S(1)}, bf16[8,64,640]{2,1,0:T(8,128)(2,1)S(1)}, u32[]{:S(2)}, u32[]{:S(2)}) collective-permute-start(bf16[8,64,640]{2,1,0:T(8,128)(2,1)S(1)} %slice.75), channel_id=1, source_target_pairs={{0,4},{1,3},{2,6},{3,1},{4,0},{5,7},{6,2},{7,5},{8,12},{9,11},{10,... | collective-permute-start | bytes 1966088 | tf_op jit(solution)/shard_map/ppermute | solution.py:681
  56.2 8.3 %copy-start = (bf16[2,2048,512]{2,1,0:T(8,128)(2,1)S(1)}, bf16[2,2048,512]{2,1,0:T(8,128)(2,1)}, u32[]{:S(2)}) copy-start(bf16[2,2048,512]{2,1,0:T(8,128)(2,1)} %cot_ref.3) | copy-start | bytes 12582916
  61.2 3.3 %copy-start.5 = (f32[2048]{0:T(1024)S(1)}, f32[2048]{0:T(1024)}, u32[]{:S(2)}) copy-start(f32[2048]{0:T(1024)} %param.35) | copy-start | bytes 24580
  61.2 3.3 %copy-start.7 = (f32[512]{0:T(512)S(1)}, f32[512]{0:T(512)}, u32[]{:S(2)}) copy-start(f32[512]{0:T(512)} %param.32) | copy-start | bytes 6148
  61.2 3.3 %copy-start.9 = (f32[512]{0:T(512)S(1)}, f32[512]{0:T(512)}, u32[]{:S(2)}) copy-start(f32[512]{0:T(512)} %param.31) | copy-start | bytes 6148
  61.2 3.3 %copy-start.10 = (f32[512]{0:T(512)S(1)}, f32[512]{0:T(512)}, u32[]{:S(2)}) copy-start(f32[512]{0:T(512)} %param.33) | copy-start | bytes 6148
  61.2 3.3 %copy-start.11 = (f32[512]{0:T(512)S(1)}, f32[512]{0:T(512)}, u32[]{:S(2)}) copy-start(f32[512]{0:T(512)} %param.37) | copy-start | bytes 6148
  61.4 3.1 %collective-permute-start.12 = (bf16[16,64,640]{2,1,0:T(8,128)(2,1)S(1)}, bf16[16,64,640]{2,1,0:T(8,128)(2,1)S(1)}, u32[]{:S(2)}, u32[]{:S(2)}) collective-permute-start(bf16[16,64,640]{2,1,0:T(8,128)(2,1)S(1)} %pad_maximum_fusion.near_ref), channel_id=1, source_target_pairs={{0,1},{1,0},{2,3},{3,2},{4,5},{5,4},{6,7},{7,6},{8,9},{9,8},{10,11... | collective-permute-start | bytes 3932168 | tf_op jit(solution)/shard_map/ppermute | solution.py:681
  61.5 16.8 %collective-permute-start.13 = (bf16[8,64,512]{2,1,0:T(8,128)(2,1)S(1)}, bf16[8,64,512]{2,1,0:T(8,128)(2,1)S(1)}, u32[]{:S(2)}, u32[]{:S(2)}) collective-permute-start(bf16[8,64,512]{2,1,0:T(8,128)(2,1)S(1)} %slice.76), channel_id=1, source_target_pairs={{0,4},{1,3},{2,6},{3,1},{4,0},{5,7},{6,2},{7,5},{8,12},{9,11},{10,... | collective-permute-start | bytes 1572872 | tf_op jit(solution)/shard_map/ppermute | solution.py:681
  78.5 2.7 %collective-permute-start.14 = (bf16[16,64,512]{2,1,0:T(8,128)(2,1)S(1)}, bf16[16,64,512]{2,1,0:T(8,128)(2,1)S(1)}, u32[]{:S(2)}, u32[]{:S(2)}) collective-permute-start(bf16[16,64,512]{2,1,0:T(8,128)(2,1)S(1)} %get-tuple-element.141), channel_id=1, source_target_pairs={{0,1},{1,0},{2,3},{3,2},{4,5},{5,4},{6,7},{7,6},{8,9},{9,8},{10,11... | collective-permute-start | bytes 3145736 | tf_op jit(solution)/shard_map/ppermute | solution.py:681
  78.6 4.7 %collective-permute-start.15 = (bf16[16,64,512]{2,1,0:T(8,128)(2,1)S(1)}, bf16[16,64,512]{2,1,0:T(8,128)(2,1)S(1)}, u32[]{:S(2)}, u32[]{:S(2)}) collective-permute-start(bf16[16,64,512]{2,1,0:T(8,128)(2,1)S(1)} %pad_maximum_fusion.1.near_ref), channel_id=1, source_target_pairs={{0,1},{1,0},{2,3},{3,2},{4,5},{5,4},{6,7},{7,6},{8,9},{9,8},{10,11... | collective-permute-start | bytes 3145736 | tf_op jit(solution)/shard_map/ppermute | solution.py:681
  81.6 16.3 %collective-permute-start.16 = (bf16[8,64,512]{2,1,0:T(8,128)(2,1)S(1)}, bf16[8,64,512]{2,1,0:T(8,128)(2,1)S(1)}, u32[]{:S(2)}, u32[]{:S(2)}) collective-permute-start(bf16[8,64,512]{2,1,0:T(8,128)(2,1)S(1)} %slice.103), channel_id=1, source_target_pairs={{0,4},{1,3},{2,6},{3,1},{4,0},{5,7},{6,2},{7,5},{8,12},{9,11},{10,... | collective-permute-start | bytes 1572872 | tf_op jit(solution)/shard_map/ppermute | solution.py:681
  98.1 6.5 %collective-permute-start.17 = (bf16[16,64,640]{2,1,0:T(8,128)(2,1)S(1)}, bf16[16,64,640]{2,1,0:T(8,128)(2,1)S(1)}, u32[]{:S(2)}, u32[]{:S(2)}) collective-permute-start(bf16[16,64,640]{2,1,0:T(8,128)(2,1)S(1)} %get-tuple-element.150), channel_id=1, source_target_pairs={{0,1},{1,0},{2,3},{3,2},{4,5},{5,4},{6,7},{7,6},{8,9},{9,8},{10,11... | collective-permute-start | bytes 3932168 | tf_op jit(solution)/shard_map/ppermute | solution.py:681
  102.4 8.2 %collective-permute-start.18 = (bf16[4,64,512]{2,1,0:T(8,128)(2,1)S(1)}, bf16[4,64,512]{2,1,0:T(8,128)(2,1)S(1)}, u32[]{:S(2)}, u32[]{:S(2)}) collective-permute-start(bf16[4,64,512]{2,1,0:T(8,128)(2,1)S(1)} %slice.105), channel_id=1, source_target_pairs={{0,2},{1,5},{2,0},{3,7},{4,6},{5,1},{6,4},{7,3},{8,10},{9,13},{10,... | collective-permute-start | bytes 786440 | tf_op jit(solution)/shard_map/ppermute | solution.py:681
  104.9 12.9 %collective-permute-start.20 = (bf16[8,64,640]{2,1,0:T(8,128)(2,1)S(1)}, bf16[8,64,640]{2,1,0:T(8,128)(2,1)S(1)}, u32[]{:S(2)}, u32[]{:S(2)}) collective-permute-start(bf16[8,64,640]{2,1,0:T(8,128)(2,1)S(1)} %slice.102), channel_id=1, source_target_pairs={{0,4},{1,3},{2,6},{3,1},{4,0},{5,7},{6,2},{7,5},{8,12},{9,11},{10,... | collective-permute-start | bytes 1966088 | tf_op jit(solution)/shard_map/ppermute | solution.py:681
  110.7 16.4 %copy-start.14 = (f32[4,64,512]{2,1,0:T(8,128)}, f32[4,64,512]{2,1,0:T(8,128)S(1)}, u32[]{:S(2)}) copy-start(f32[4,64,512]{2,1,0:T(8,128)S(1)} %slice_add_fusion.3) | copy-start | bytes 1572868
  117.8 2.8 %collective-permute-start.19 = (bf16[1056,512]{1,0:T(8,128)(2,1)S(1)}, bf16[1056,512]{1,0:T(8,128)(2,1)S(1)}, u32[]{:S(2)}, u32[]{:S(2)}) collective-permute-start(bf16[1056,512]{1,0:T(8,128)(2,1)S(1)} %get-tuple-element.165.mine_ref), channel_id=1, source_target_pairs={{0,1},{1,0},{2,3},{3,2},{4,5},{5,4},{6,7},{7,6},{8,9},{9,8},{10,11... | collective-permute-start | bytes 3244040 | tf_op jit(solution)/shard_map/ppermute | solution.py:681
  118.1 8.8 %collective-permute-start.21 = (bf16[4,64,640]{2,1,0:T(8,128)(2,1)S(1)}, bf16[4,64,640]{2,1,0:T(8,128)(2,1)S(1)}, u32[]{:S(2)}, u32[]{:S(2)}) collective-permute-start(bf16[4,64,640]{2,1,0:T(8,128)(2,1)S(1)} %slice.104), channel_id=1, source_target_pairs={{0,2},{1,5},{2,0},{3,7},{4,6},{5,1},{6,4},{7,3},{8,10},{9,13},{10,... | collective-permute-start | bytes 983048 | tf_op jit(solution)/shard_map/ppermute | solution.py:681
  120.8 11.0 %collective-permute-start.23 = (bf16[544,512]{1,0:T(8,128)(2,1)S(1)}, bf16[544,512]{1,0:T(8,128)(2,1)S(1)}, u32[]{:S(2)}, u32[]{:S(2)}) collective-permute-start(bf16[544,512]{1,0:T(8,128)(2,1)S(1)} %get-tuple-element.168.mine_ref), channel_id=1, source_target_pairs={{0,4},{1,3},{2,6},{3,1},{4,0},{5,7},{6,2},{7,5},{8,12},{9,11},{10,... | collective-permute-start | bytes 1671176 | tf_op jit(solution)/shard_map/ppermute | solution.py:681
  127.0 8.5 %collective-permute-start.25 = (bf16[2,64,1152]{2,1,0:T(8,128)(2,1)S(1)}, bf16[2,64,1152]{2,1,0:T(8,128)(2,1)S(1)}, u32[]{:S(2)}, u32[]{:S(2)}) collective-permute-start(bf16[2,64,1152]{2,1,0:T(8,128)(2,1)S(1)} %pad_maximum_fusion.4), channel_id=1, source_target_pairs={{0,8},{1,9},{2,10},{3,11},{4,12},{5,13},{6,14},{7,15},{8,0},{9,1},... | collective-permute-start | bytes 884744 | tf_op jit(solution)/shard_map/ppermute | solution.py:681
  127.1 8.5 %slice-start = ((f32[4,64,512]{2,1,0:T(8,128)}), f32[2,64,512]{2,1,0:T(8,128)S(1)}, s32[]{:S(2)}) async-start(f32[4,64,512]{2,1,0:T(8,128)} %copy-done.14), calls=%async_computation | async-start | bytes 524288 | tf_op jit(solution)/shard_map/slice | solution.py:720
  127.1 19.8 %collective-permute-start.22 = (bf16[2,2,128,512]{3,2,1,0:T(8,128)(2,1)S(1)}, bf16[2,2,128,512]{3,2,1,0:T(8,128)(2,1)S(1)}, u32[]{:S(2)}, u32[]{:S(2)}) collective-permute-start(bf16[2,2,128,512]{3,2,1,0:T(8,128)(2,1)S(1)} %get-tuple-element.174), channel_id=1, source_target_pairs={{0,31},{1,0},{2,1},{3,2},{4,3},{5,4},{6,5},{7,6},{8,7},{9,8},{10,9... | collective-permute-start | bytes 1572872 | tf_op jit(solution)/shard_map/ppermute | solution.py:684
  131.9 11.4 %collective-permute-start.24 = (bf16[288,512]{1,0:T(8,128)(2,1)S(1)}, bf16[288,512]{1,0:T(8,128)(2,1)S(1)}, u32[]{:S(2)}, u32[]{:S(2)}) collective-permute-start(bf16[288,512]{1,0:T(8,128)(2,1)S(1)} %get-tuple-element.178.mine_ref), channel_id=1, source_target_pairs={{0,2},{1,5},{2,0},{3,7},{4,6},{5,1},{6,4},{7,3},{8,10},{9,13},{10,... | collective-permute-start | bytes 884744 | tf_op jit(solution)/shard_map/ppermute | solution.py:681
  135.6 14.2 %collective-permute-start.27 = (bf16[1,64,1152]{2,1,0:T(8,128)(2,1)S(1)}, bf16[1,64,1152]{2,1,0:T(8,128)(2,1)S(1)}, u32[]{:S(2)}, u32[]{:S(2)}) collective-permute-start(bf16[1,64,1152]{2,1,0:T(8,128)(2,1)S(1)} %slice.107), channel_id=1, source_target_pairs={{0,16},{1,17},{2,18},{3,19},{4,20},{5,21},{6,22},{7,23},{8,24},{9,... | collective-permute-start | bytes 442376 | tf_op jit(solution)/shard_map/ppermute | solution.py:681
  143.3 7.3 %collective-permute-start.28 = (bf16[80,512]{1,0:T(8,128)(2,1)S(1)}, bf16[80,512]{1,0:T(8,128)(2,1)S(1)}, u32[]{:S(2)}, u32[]{:S(2)}) collective-permute-start(bf16[80,512]{1,0:T(8,128)(2,1)S(1)} %get-tuple-element.190), channel_id=1, source_target_pairs={{0,8},{1,9},{2,10},{3,11},{4,12},{5,13},{6,14},{7,15},{8,0},{9,1},... | collective-permute-start | bytes 245768 | tf_op jit(solution)/shard_map/ppermute | solution.py:709
  143.4 7.2 %collective-permute-start.29 = (bf16[80,512]{1,0:T(8,128)(2,1)S(1)}, bf16[80,512]{1,0:T(8,128)(2,1)S(1)}, u32[]{:S(2)}, u32[]{:S(2)}) collective-permute-start(bf16[80,512]{1,0:T(8,128)(2,1)S(1)} %get-tuple-element.192), channel_id=1, source_target_pairs={{0,24},{1,25},{2,26},{3,27},{4,28},{5,29},{6,30},{7,31},{8,16},{9,... | collective-permute-start | bytes 245768 | tf_op jit(solution)/shard_map/ppermute | solution.py:709
  143.5 8.4 %collective-permute-start.26 = (bf16[80,512]{1,0:T(8,128)(2,1)S(1)}, bf16[80,512]{1,0:T(8,128)(2,1)S(1)}, u32[]{:S(2)}, u32[]{:S(2)}) collective-permute-start(bf16[80,512]{1,0:T(8,128)(2,1)S(1)} %get-tuple-element.181.refs_1_), channel_id=1, source_target_pairs={{0,16},{1,17},{2,18},{3,19},{4,20},{5,21},{6,22},{7,23},{8,24},{9,... | collective-permute-start | bytes 245768 | tf_op jit(solution)/shard_map/ppermute | solution.py:709
where the time goes:
time: 157 us; the launch traced here: 156 us
  Pallas kernels  72.5 us (46%)
  waiting for transfers between devices  44 us (28%)
  starting transfers between devices  32.9 us (21%)
  local copies, waits for them, and re-layouts  2.55 us (2%)
  other arithmetic  2.24 us (1%)
    ppermute x21, waiting for transfers between devices, swap(): return lax.ppermute(value, AXES, pairs)  27.1 us
    ppermute x21, starting transfers between devices, swap(): return lax.ppermute(value, AXES, pairs)  22.4 us
    pallas_call x4, Pallas kernels, call_row(): call(partial(kernel, mi), outs, [SMEM] * 3 + [block(a.shape) for a in arr...  16.4 us
    pallas_call x1, Pallas kernels, per_device(): call(mlp_second_kernel, [shape(wide, BF16)] * 3 + [shape((8, D), F32)] +...  14.5 us
    pallas_call x1, Pallas kernels, per_device(): call(mlp_first_kernel, [tall_float] + [tall_low] * 4 + [shape((D, D), BF1...  13.8 us
    ppermute x3, waiting for transfers between devices, turn(): lax.ppermute(value, AXES, [(i, (i + by) % count) for i in range(count)])  11.3 us
    ppermute x6, starting transfers between devices, reach(): return lax.ppermute(value, AXES, [(i, i ^ flip) for i in range(count)])  9.29 us
    pallas_call x1, Pallas kernels, per_device(): call(partial(weights_back_kernel, apart), [shape((16, D), F32)] + [shape(...  7 us
  transfers between devices with their start and end apart: 30, of which 15 were waited for; matrix products, arithmetic and copies ran while one was open for 2% of the time, Pallas kernels for 42%

commit v1 on v0

--- a/solution.py
+++ b/solution.py
@@ -13,7 +13,7 @@
 HEAD_DIM = 64
 SPAN = 128
 LANES = 128
-STEP = 256
+STEP = 512
 EPSILON = 1e-05
 NEGATIVE = -1e30
 SCALE = 1.0 / math.sqrt(HEAD_DIM)
@@ -202,15 +202,18 @@
         rows_ref[mi, rows + summaries : rows + 2 * summaries, :] = (summed - high.astype(F32)).astype(BF16)
     pltpu.make_async_copy(w_ref, w_ref, sem.at[0]).wait()
     none = jnp.zeros((1, LANES), F32)
-    for m in range(4):
-        lanes = slice(m * LANES, (m + 1) * LANES)
-        cols = slice(m * 384, (m + 1) * 384)
+
+    def block(m, carry):
+        lanes, cols = columns(m, LANES), columns(m, 384)
         bias = jnp.concatenate((qbias[:, lanes], none, vbias[:, lanes]), axis=1)
         for mi in range(2):
             projected = dot(rows_ref[mi], w_ref[:, cols])
             qkv_ref[mi, :, cols] = (projected[:rows] + bias).astype(BF16)
             pooled = projected[rows : rows + summaries] + projected[rows + summaries :]
             skv_ref[mi, :, cols] = (pooled + roots[mi] * bias).astype(BF16)
+        return carry
+
+    lax.fori_loop(0, 4, block, 0)
 
 
 def pair_of(ref, here, pair):

time: 157 us -> 156 us (level)
  no operation moved by 1% of the time
where the time goes in v1:
time: 156 us; the launch traced here: 155 us
  Pallas kernels  72 us (46%)
  waiting for transfers between devices  43.5 us (28%)
  starting transfers between devices  32.9 us (21%)
  local copies, waits for them, and re-layouts  2.55 us (2%)
  other arithmetic  2.24 us (1%)
    ppermute x21, waiting for transfers between devices, swap(): return lax.ppermute(value, AXES, pairs)  27.1 us
    ppermute x21, starting transfers between devices, swap(): return lax.ppermute(value, AXES, pairs)  22.4 us
    pallas_call x4, Pallas kernels, call_row(): call(partial(kernel, mi), outs, [SMEM] * 3 + [block(a.shape) for a in arr...  16.4 us
    pallas_call x1, Pallas kernels, per_device(): call(mlp_second_kernel, [shape(wide, BF16)] * 3 + [shape((8, D), F32)] +...  13.8 us
    pallas_call x1, Pallas kernels, per_device(): call(mlp_first_kernel, [tall_float] + [tall_low] * 4 + [shape((D, D), BF1...  13.4 us
    ppermute x3, waiting for transfers between devices, turn(): lax.ppermute(value, AXES, [(i, (i + by) % count) for i in range(count)])  10.7 us
    ppermute x6, starting transfers between devices, reach(): return lax.ppermute(value, AXES, [(i, i ^ flip) for i in range(count)])  9.29 us
    pallas_call x1, Pallas kernels, per_device(): call(partial(project_kernel, apart), [shape(wide, BF16), shape(three, BF1...  7.07 us
  transfers between devices with their start and end apart: 30, of which 15 were waited for; matrix products, arithmetic and copies ran while one was open for 2% of the time, Pallas kernels for 42%

profile of v1, /device:TPU:0, one launch (start us, length us, event | category | flops | bytes accessed | tf_op | source)
XLA Modules:
  0.0 154.6 jit_solution(16404386068979291628)
XLA Ops:
  0.7 0.6 pad_add_fusion.1.place.place_ref
  1.2 3.9 %shard_map.314 = (bf16[1,64,512]{2,1,0:T(8,128)(2,1)}, bf16[1,64,1152]{2,1,0:T(8,128)(2,1)}, bf16[2,128,512]{2,1,0:T(8,128)(2,1)}) custom-call(s32[2]{0:T(128)} %pad_add_fusion.1.place.place_ref, s32[2]{0:T(128)} %offsets.19, s32[2,8]{1,0:T(2,128)} %lengths.15, bf16[2,512,512]{2,1,0:T(8,128)(2,1)} %x_ref.5, bf16[2,2048,512]{2,1,0:T(8,128)(2,1)} %cot_ref.3, ...), custom_call_target="tpu_custom_call" | custom-call | flops 1 | bytes 1 | tf_op jit(solution)/shard_map/pallas_call | solution.py:761
  5.1 5.1 %collective-permute-start.2 = (bf16[1,64,512]{2,1,0:T(8,128)(2,1)}, bf16[1,64,512]{2,1,0:T(8,128)(2,1)S(1)}, u32[]{:S(2)}, u32[]{:S(2)}) collective-permute-start(bf16[1,64,512]{2,1,0:T(8,128)(2,1)} %get-tuple-element.113), channel_id=1, source_target_pairs={{0,24},{1,25},{2,26},{3,27},{4,28},{5,29},{6,30},{7,31},{8,16},{9,... | collective-permute-start | bytes 196616 | tf_op jit(solution)/shard_map/ppermute | solution.py:712
  10.3 0.6 collective-permute-start
  10.9 0.9 constant_dynamic-update-slice_fusion.8
  11.8 4.3 %collective-permute-done = bf16[1,64,512]{2,1,0:T(8,128)(2,1)S(1)} collective-permute-done((bf16[1,64,512]{2,1,0:T(8,128)(2,1)}, bf16[1,64,512]{2,1,0:T(8,128)(2,1)S(1)}, u32[]{:S(2)}, u32[]{:S(2)}) %collective-permute-start) | collective-permute-done | bytes 65568 | tf_op jit(solution)/shard_map/ppermute | solution.py:712
  16.2 1.6 %collective-permute-start.4 = (bf16[4,64,512]{2,1,0:T(8,128)(2,1)S(1)}, bf16[4,64,512]{2,1,0:T(8,128)(2,1)S(1)}, u32[]{:S(2)}, u32[]{:S(2)}) collective-permute-start(bf16[4,64,512]{2,1,0:T(8,128)(2,1)S(1)} %get-tuple-element.213), channel_id=1, source_target_pairs={{0,2},{1,5},{2,0},{3,7},{4,6},{5,1},{6,4},{7,3},{8,10},{9,13},{10,... | collective-permute-start | bytes 786440 | tf_op jit(solution)/shard_map/ppermute | solution.py:684
  17.8 2.0 %collective-permute-start.7 = (bf16[1,64,1152]{2,1,0:T(8,128)(2,1)S(1)}, bf16[1,64,1152]{2,1,0:T(8,128)(2,1)S(1)}, u32[]{:S(2)}, u32[]{:S(2)}) collective-permute-start(bf16[1,64,1152]{2,1,0:T(8,128)(2,1)S(1)} %copy-done.15), channel_id=1, source_target_pairs={{0,16},{1,17},{2,18},{3,19},{4,20},{5,21},{6,22},{7,23},{8,24},{9,... | collective-permute-start | bytes 442376 | tf_op jit(solution)/shard_map/ppermute | solution.py:684
  19.8 2.8 %collective-permute-done.4 = bf16[4,64,512]{2,1,0:T(8,128)(2,1)S(1)} collective-permute-done((bf16[4,64,512]{2,1,0:T(8,128)(2,1)S(1)}, bf16[4,64,512]{2,1,0:T(8,128)(2,1)S(1)}, u32[]{:S(2)}, u32[]{:S(2)}) %collective-permute-start.4) | collective-permute-done | bytes 262176 | tf_op jit(solution)/shard_map/ppermute | solution.py:684
  22.6 0.7 constant_dynamic-update-slice_fusion.4
  23.4 1.5 collective-permute-start.5
  24.9 0.1 add_select_fusion.1
  25.0 0.1 select_n.110
  25.1 0.1 select_n.112
  25.1 1.0 collective-permute-done.7
  26.2 0.6 collective-permute-start.8
  26.8 10.5 %collective-permute-done.3.left_ref = bf16[2,128,512]{2,1,0:T(8,128)(2,1)S(1)} collective-permute-done((bf16[2,128,512]{2,1,0:T(8,128)(2,1)S(1)}, bf16[2,128,512]{2,1,0:T(8,128)(2,1)S(1)}, u32[]{:S(2)}, u32[]{:S(2)}) %collective-permute-start.3) | collective-permute-done | bytes 262176 | tf_op jit(solution)/shard_map/ppermute | solution.py:687
  37.6 0.1 pad_maximum_fusion.2
  37.8 0.7 collective-permute-start.10
  38.6 1.6 %collective-permute-done.6.far_ref = bf16[16,64,512]{2,1,0:T(8,128)(2,1)S(1)} collective-permute-done((bf16[16,64,512]{2,1,0:T(8,128)(2,1)S(1)}, bf16[16,64,512]{2,1,0:T(8,128)(2,1)S(1)}, u32[]{:S(2)}, u32[]{:S(2)}) %collective-permute-start.6) | collective-permute-done | bytes 1048608 | tf_op jit(solution)/shard_map/ppermute | solution.py:684
  40.2 7.1 %shard_map.315 = (bf16[2,512,512]{2,1,0:T(8,128)(2,1)S(1)}, bf16[2,512,1536]{2,1,0:T(8,128)(2,1)S(1)}, bf16[2,128,1536]{2,1,0:T(8,128)(2,1)S(1)}, f32[2,128,512]{2,1,0:T(8,128)S(1)}, bf16[512,1536]{1,0:T(8,128)(2,1)S(1)}) custom-call(s32[2]{0:T(128)S(1)} %copy-done.4, s32[2]{0:T(128)S(1)} %copy-done.3, s32[2,8]{1,0:T(2,128)S(1)} %copy-done.2, ...), custom_call_target="tpu_custom_call" | custom-call | flops 1 | bytes 1 | tf_op jit(solution)/shard_map/pallas_call | solution.py:793
  47.3 0.2 collective-permute-done.10.left_ref
  47.6 2.9 %collective-permute-done.9 = bf16[4,64,1152]{2,1,0:T(8,128)(2,1)S(1)} collective-permute-done((bf16[4,64,1152]{2,1,0:T(8,128)(2,1)S(1)}, bf16[4,64,1152]{2,1,0:T(8,128)(2,1)S(1)}, u32[]{:S(2)}, u32[]{:S(2)}) %collective-permute-start.9) | collective-permute-done | bytes 589856 | tf_op jit(solution)/shard_map/ppermute | solution.py:684
  50.6 1.8 %collective-permute-start.11 = (bf16[8,64,640]{2,1,0:T(8,128)(2,1)S(1)}, bf16[8,64,640]{2,1,0:T(8,128)(2,1)S(1)}, u32[]{:S(2)}, u32[]{:S(2)}) collective-permute-start(bf16[8,64,640]{2,1,0:T(8,128)(2,1)S(1)} %slice.75), channel_id=1, source_target_pairs={{0,4},{1,3},{2,6},{3,1},{4,0},{5,7},{6,2},{7,5},{8,12},{9,11},{10,... | collective-permute-start | bytes 1966088 | tf_op jit(solution)/shard_map/ppermute | solution.py:684
  52.4 3.9 %shard_map.316 = (bf16[2,512,512]{2,1,0:T(8,128)(2,1)S(1)}, f32[2,4,4,1,256]{4,3,2,1,0:T(1,128)S(1)}) custom-call(s32[2]{0:T(128)S(1)} %copy-done.4, s32[2]{0:T(128)S(1)} %copy-done.3, s32[2,8]{1,0:T(2,128)S(1)} %copy-done.2, bf16[2,512,1536]{2,1,0:T(8,128)(2,1)S(1)} %get-tuple-element.125.qkv_ref, bf16[2,128,1536]{2,1,0:T(8,128)(2,1)S(1)} %get-tuple-element.121.skv_ref), custom_call_target="tpu_custom_call" | custom-call | flops 1 | bytes 1 | tf_op jit(solution)/shard_map/pallas_call | solution.py:656
  56.2 3.9 %shard_map.317 = (bf16[2,512,512]{2,1,0:T(8,128)(2,1)S(1)}, f32[2,4,4,1,256]{4,3,2,1,0:T(1,128)S(1)}) custom-call(s32[2]{0:T(128)S(1)} %copy-done.4, s32[2]{0:T(128)S(1)} %copy-done.3, s32[2,8]{1,0:T(2,128)S(1)} %copy-done.2, bf16[2,512,1536]{2,1,0:T(8,128)(2,1)S(1)} %get-tuple-element.125.qkv_ref, ...), custom_call_target="tpu_custom_call", output_to_operand_aliasing={{0}: (5, {}), {1}: (6, {})} | custom-call | flops 1 | bytes 1 | tf_op jit(solution)/shard_map/pallas_call | solution.py:656
  60.1 1.1 collective-permute-done.11
  61.2 0.1 pad_maximum_fusion.near_ref
  61.5 1.8 %collective-permute-start.13 = (bf16[8,64,512]{2,1,0:T(8,128)(2,1)S(1)}, bf16[8,64,512]{2,1,0:T(8,128)(2,1)S(1)}, u32[]{:S(2)}, u32[]{:S(2)}) collective-permute-start(bf16[8,64,512]{2,1,0:T(8,128)(2,1)S(1)} %slice.76), channel_id=1, source_target_pairs={{0,4},{1,3},{2,6},{3,1},{4,0},{5,7},{6,2},{7,5},{8,12},{9,11},{10,... | collective-permute-start | bytes 1572872 | tf_op jit(solution)/shard_map/ppermute | solution.py:684
  63.3 1.2 collective-permute-done.12.far_ref
  64.5 13.4 %shard_map.318 = (f32[1024,512]{1,0:T(8,128)S(1)}, bf16[1024,512]{1,0:T(8,128)(2,1)S(1)}, bf16[1024,512]{1,0:T(8,128)(2,1)S(1)}, bf16[1024,512]{1,0:T(8,128)(2,1...) custom-call(s32[2]{0:T(128)S(1)} %copy-done.4, ...), custom_call_target="tpu_custom_call" | custom-call | flops 1 | bytes 1 | tf_op jit(solution)/shard_map/pallas_call | solution.py:825
  78.0 0.1 pad_maximum_fusion.1.near_ref
  78.1 0.2 collective-permute-start.14
  78.3 0.4 collective-permute-start.15
  78.7 2.1 %collective-permute-done.14 = bf16[16,64,512]{2,1,0:T(8,128)(2,1)S(1)} collective-permute-done((bf16[16,64,512]{2,1,0:T(8,128)(2,1)S(1)}, bf16[16,64,512]{2,1,0:T(8,128)(2,1)S(1)}, u32[]{:S(2)}, u32[]{:S(2)}) %collective-permute-start.14) | collective-permute-done | bytes 1048608 | tf_op jit(solution)/shard_map/ppermute | solution.py:684
  80.8 0.3 convert_add_fusion.1
  81.2 1.8 %collective-permute-start.16 = (bf16[8,64,512]{2,1,0:T(8,128)(2,1)S(1)}, bf16[8,64,512]{2,1,0:T(8,128)(2,1)S(1)}, u32[]{:S(2)}, u32[]{:S(2)}) collective-permute-start(bf16[8,64,512]{2,1,0:T(8,128)(2,1)S(1)} %slice.103), channel_id=1, source_target_pairs={{0,4},{1,3},{2,6},{3,1},{4,0},{5,7},{6,2},{7,5},{8,12},{9,11},{10,... | collective-permute-start | bytes 1572872 | tf_op jit(solution)/shard_map/ppermute | solution.py:684
  83.0 13.8 %shard_map.319 = (bf16[2,512,512]{2,1,0:T(8,128)(2,1)S(1)}, bf16[2,512,512]{2,1,0:T(8,128)(2,1)S(1)}, bf16[2,512,512]{2,1,0:T(8,128)(2,1)S(1)}, f32[8,512]{1,0:T...) custom-call(s32[32]{0:T(128)S(1)} %get-tuple-element.226.block_of, ...), custom_call_target="tpu_custom_call" | custom-call | flops 1 | bytes 1 | tf_op jit(solution)/shard_map/pallas_call | solution.py:846
  96.8 0.2 slice_add_fusion.1
  97.1 4.2 %shard_map.320 = (bf16[2,512,1536]{2,1,0:T(8,128)(2,1)S(1)}, bf16[2,128,1536]{2,1,0:T(8,128)(2,1)S(1)}) custom-call(s32[2]{0:T(128)S(1)} %copy-done.4, s32[2]{0:T(128)S(1)} %copy-done.3, s32[2,8]{1,0:T(2,128)S(1)} %copy-done.2, bf16[2,512,1536]{2,1,0:T(8,128)(2,1)S(1)} %get-tuple-element.125.qkv_ref, bf16[2,128,1536]{2,1,0:T(8,128)(2,1)S(1)} %get-tuple-element.121.skv_ref, ...), custom_call_target="tpu_custom_call" | custom-call | flops 1 | bytes 1 | tf_op jit(solution)/shard_map/pallas_call | solution.py:656
  101.3 2.2 %collective-permute-start.18 = (bf16[4,64,512]{2,1,0:T(8,128)(2,1)S(1)}, bf16[4,64,512]{2,1,0:T(8,128)(2,1)S(1)}, u32[]{:S(2)}, u32[]{:S(2)}) collective-permute-start(bf16[4,64,512]{2,1,0:T(8,128)(2,1)S(1)} %slice.105), channel_id=1, source_target_pairs={{0,2},{1,5},{2,0},{3,7},{4,6},{5,1},{6,4},{7,3},{8,10},{9,13},{10,... | collective-permute-start | bytes 786440 | tf_op jit(solution)/shard_map/ppermute | solution.py:684
  103.5 0.3 convert_add_fusion
  103.9 1.2 collective-permute-start.20
  105.1 4.4 %shard_map.321 = (bf16[2,512,1536]{2,1,0:T(8,128)(2,1)S(1)}, bf16[2,128,1536]{2,1,0:T(8,128)(2,1)S(1)}) custom-call(s32[2]{0:T(128)S(1)} %copy-done.4, s32[2]{0:T(128)S(1)} %copy-done.3, s32[2,8]{1,0:T(2,128)S(1)} %copy-done.2, bf16[2,512,1536]{2,1,0:T(8,128)(2,1)S(1)} %get-tuple-element.125.qkv_ref, ...), custom_call_target="tpu_custom_call", output_to_operand_aliasing={{0}: (7, {}), {1}: (8, {})} | custom-call | flops 1 | bytes 1 | tf_op jit(solution)/shard_map/pallas_call | solution.py:656
  109.5 0.1 slice_add_fusion.3
  109.7 7.0 %shard_map.322 = (f32[16,512]{1,0:T(8,128)}, bf16[1024,512]{1,0:T(8,128)(2,1)S(1)}, bf16[1056,512]{1,0:T(8,128)(2,1)S(1)}) custom-call(s32[2]{0:T(128)S(1)} %copy-done.4, s32[2]{0:T(128)S(1)} %copy-done.3, s32[2,8]{1,0:T(2,128)S(1)} %copy-done.2, s32[32]{0:T(128)S(1)} %get-tuple-element.226.block_of, s32[32]{0:T(128)S(1)} %get-tuple-element.225.row_of, ...), custom_call_target="tpu_custom_call" | custom-call | flops 1 | bytes 1 | tf_op jit(solution)/shard_map/pallas_call | solution.py:873
  116.7 0.2 slice_add_fusion
  117.0 2.5 %collective-permute-start.21 = (bf16[4,64,640]{2,1,0:T(8,128)(2,1)S(1)}, bf16[4,64,640]{2,1,0:T(8,128)(2,1)S(1)}, u32[]{:S(2)}, u32[]{:S(2)}) collective-permute-start(bf16[4,64,640]{2,1,0:T(8,128)(2,1)S(1)} %slice.104), channel_id=1, source_target_pairs={{0,2},{1,5},{2,0},{3,7},{4,6},{5,1},{6,4},{7,3},{8,10},{9,13},{10,... | collective-permute-start | bytes 983048 | tf_op jit(solution)/shard_map/ppermute | solution.py:684
  119.4 0.2 shard_map.323
  119.7 2.8 %collective-permute-start.23 = (bf16[544,512]{1,0:T(8,128)(2,1)S(1)}, bf16[544,512]{1,0:T(8,128)(2,1)S(1)}, u32[]{:S(2)}, u32[]{:S(2)}) collective-permute-start(bf16[544,512]{1,0:T(8,128)(2,1)S(1)} %get-tuple-element.168.mine_ref), channel_id=1, source_target_pairs={{0,4},{1,3},{2,6},{3,1},{4,0},{5,7},{6,2},{7,5},{8,12},{9,11},{10,... | collective-permute-start | bytes 1671176 | tf_op jit(solution)/shard_map/ppermute | solution.py:684
  122.5 2.8 %shard_map.324 = (f32[2,512,512]{2,1,0:T(8,128)S(1)}, bf16[2,2,128,512]{3,2,1,0:T(8,128)(2,1)S(1)}) custom-call(bf16[2,512,1536]{2,1,0:T(8,128)(2,1)S(1)} %get-tuple-element.156.grad_ref, bf16[512,1536]{1,0:T(8,128)(2,1)S(1)} %get-tuple-element.169.w_ref, bf16[2,512,512]{2,1,0:T(8,128)(2,1)S(1)} %get-tuple-element.129.xs_ref, ...), custom_call_target="tpu_custom_call" | custom-call | flops 1 | bytes 1 | tf_op jit(solution)/shard_map/pallas_call | solution.py:896
  125.3 0.5 collective-permute-done.21
  125.8 0.1 slice_add_fusion.2
  126.1 0.4 collective-permute-start.22
  126.5 4.2 %collective-permute-done.23.got_ref = bf16[544,512]{1,0:T(8,128)(2,1)S(1)} collective-permute-done((bf16[544,512]{1,0:T(8,128)(2,1)S(1)}, bf16[544,512]{1,0:T(8,128)(2,1)S(1)}, u32[]{:S(2)}, u32[]{:S(2)}) %collective-permute-start.23) | collective-permute-done | bytes 557088 | tf_op jit(solution)/shard_map/ppermute | solution.py:684
  130.6 0.1 shard_map.325
  130.8 1.6 %collective-permute-start.24 = (bf16[288,512]{1,0:T(8,128)(2,1)S(1)}, bf16[288,512]{1,0:T(8,128)(2,1)S(1)}, u32[]{:S(2)}, u32[]{:S(2)}) collective-permute-start(bf16[288,512]{1,0:T(8,128)(2,1)S(1)} %get-tuple-element.178.mine_ref), channel_id=1, source_target_pairs={{0,2},{1,5},{2,0},{3,7},{4,6},{5,1},{6,4},{7,3},{8,10},{9,13},{10,... | collective-permute-start | bytes 884744 | tf_op jit(solution)/shard_map/ppermute | solution.py:684
  132.4 2.1 %collective-permute-done.25 = bf16[2,64,1152]{2,1,0:T(8,128)(2,1)S(1)} collective-permute-done((bf16[2,64,1152]{2,1,0:T(8,128)(2,1)S(1)}, bf16[2,64,1152]{2,1,0:T(8,128)(2,1)S(1)}, u32[]{:S(2)}, u32[]{:S(2)}) %collective-permute-start.25) | collective-permute-done | bytes 294944 | tf_op jit(solution)/shard_map/ppermute | solution.py:684
  134.6 7.6 %collective-permute-done.24.got_ref = bf16[288,512]{1,0:T(8,128)(2,1)S(1)} collective-permute-done((bf16[288,512]{1,0:T(8,128)(2,1)S(1)}, bf16[288,512]{1,0:T(8,128)(2,1)S(1)}, u32[]{:S(2)}, u32[]{:S(2)}) %collective-permute-start.24) | collective-permute-done | bytes 294944 | tf_op jit(solution)/shard_map/ppermute | solution.py:684
  142.4 3.4 %collective-permute-start.26 = (bf16[80,512]{1,0:T(8,128)(2,1)S(1)}, bf16[80,512]{1,0:T(8,128)(2,1)S(1)}, u32[]{:S(2)}, u32[]{:S(2)}) collective-permute-start(bf16[80,512]{1,0:T(8,128)(2,1)S(1)} %get-tuple-element.181.refs_1_), channel_id=1, source_target_pairs={{0,16},{1,17},{2,18},{3,19},{4,20},{5,21},{6,22},{7,23},{8,24},{9,... | collective-permute-start | bytes 245768 | tf_op jit(solution)/shard_map/ppermute | solution.py:712
  145.8 3.0 %shard_map.327 = (bf16[2,512,512]{2,1,0:T(8,128)(2,1)}, bf16[2,512,512]{2,1,0:T(8,128)(2,1)S(1)}, f32[2,512,128]{2,1,0:T(8,128)S(1)}) custom-call(s32[2]{0:T(128)S(1)} %copy-done.3, bf16[2,512,512]{2,1,0:T(8,128)(2,1)S(1)} %get-tuple-element.143.result_ref, bf16[2,2,128,512]{3,2,1,0:T(8,128)(2,1)S(1)} %collective-permute-done.22.right_ref, ...), custom_call_target="tpu_custom_call" | custom-call | flops 1 | bytes 1 | tf_op jit(solution)/shard_map/pallas_call | solution.py:904
  148.8 0.7 shard_map.328
  149.5 1.3 collective-permute-done.26.refs_2_
  150.9 3.6 %shard_map.329 = (f32[2,512,512]{2,1,0:T(8,128)}, f32[64,128]{1,0:T(8,128)}, f32[64,128]{1,0:T(8,128)}, f32[64,128]{1,0:T(8,128)}, f32[1,2048]{1,0:T(1,128)}, /*...) custom-call(s32[2]{0:T(128)S(1)} %copy-done.4, ...), custom_call_target="tpu_custom_call" | custom-call | flops 1 | bytes 1 | tf_op jit(solution)/shard_map/pallas_call | solution.py:934
  (93 shorter events, 1.7 us)
Async XLA Ops:
  1.2 16.5 %copy-start.1 = (bf16[2,512,512]{2,1,0:T(8,128)(2,1)S(1)}, bf16[2,512,512]{2,1,0:T(8,128)(2,1)}, u32[]{:S(2)}) copy-start(bf16[2,512,512]{2,1,0:T(8,128)(2,1)} %x_ref.5) | copy-start | bytes 3145732
  5.1 12.7 %copy-start.15 = (bf16[1,64,1152]{2,1,0:T(8,128)(2,1)S(1)}, bf16[1,64,1152]{2,1,0:T(8,128)(2,1)}, u32[]{:S(2)}) copy-start(bf16[1,64,1152]{2,1,0:T(8,128)(2,1)} %get-tuple-element.118) | copy-start | bytes 442372
  5.1 11.0 %collective-permute-start.2 = (bf16[1,64,512]{2,1,0:T(8,128)(2,1)}, bf16[1,64,512]{2,1,0:T(8,128)(2,1)S(1)}, u32[]{:S(2)}, u32[]{:S(2)}) collective-permute-start(bf16[1,64,512]{2,1,0:T(8,128)(2,1)} %get-tuple-element.113), channel_id=1, source_target_pairs={{0,24},{1,25},{2,26},{3,27},{4,28},{5,29},{6,30},{7,31},{8,16},{9,... | collective-permute-start | bytes 196616 | tf_op jit(solution)/shard_map/ppermute | solution.py:712
  10.2 5.9 %collective-permute-start.1 = (bf16[1,64,512]{2,1,0:T(8,128)(2,1)}, bf16[1,64,512]{2,1,0:T(8,128)(2,1)S(1)}, u32[]{:S(2)}, u32[]{:S(2)}) collective-permute-start(bf16[1,64,512]{2,1,0:T(8,128)(2,1)} %get-tuple-element.113), channel_id=1, source_target_pairs={{0,8},{1,9},{2,10},{3,11},{4,12},{5,13},{6,14},{7,15},{8,0},{9,1},... | collective-permute-start | bytes 196616 | tf_op jit(solution)/shard_map/ppermute | solution.py:712
  10.3 5.8 %collective-permute-start = (bf16[1,64,512]{2,1,0:T(8,128)(2,1)}, bf16[1,64,512]{2,1,0:T(8,128)(2,1)S(1)}, u32[]{:S(2)}, u32[]{:S(2)}) collective-permute-start(bf16[1,64,512]{2,1,0:T(8,128)(2,1)} %get-tuple-element.113), channel_id=1, source_target_pairs={{0,16},{1,17},{2,18},{3,19},{4,20},{5,21},{6,22},{7,23},{8,24},{9,... | collective-permute-start | bytes 196616 | tf_op jit(solution)/shard_map/ppermute | solution.py:712
  16.2 1.6 %copy-start.16 = (bf16[8,64,512]{2,1,0:T(8,128)(2,1)}, bf16[8,64,512]{2,1,0:T(8,128)(2,1)S(1)}, u32[]{:S(2)}) copy-start(bf16[8,64,512]{2,1,0:T(8,128)(2,1)S(1)} %get-tuple-element.211) | copy-start | bytes 1572868
  16.2 6.4 %collective-permute-start.4 = (bf16[4,64,512]{2,1,0:T(8,128)(2,1)S(1)}, bf16[4,64,512]{2,1,0:T(8,128)(2,1)S(1)}, u32[]{:S(2)}, u32[]{:S(2)}) collective-permute-start(bf16[4,64,512]{2,1,0:T(8,128)(2,1)S(1)} %get-tuple-element.213), channel_id=1, source_target_pairs={{0,2},{1,5},{2,0},{3,7},{4,6},{5,1},{6,4},{7,3},{8,10},{9,13},{10,... | collective-permute-start | bytes 786440 | tf_op jit(solution)/shard_map/ppermute | solution.py:684
  17.8 8.3 %collective-permute-start.7 = (bf16[1,64,1152]{2,1,0:T(8,128)(2,1)S(1)}, bf16[1,64,1152]{2,1,0:T(8,128)(2,1)S(1)}, u32[]{:S(2)}, u32[]{:S(2)}) collective-permute-start(bf16[1,64,1152]{2,1,0:T(8,128)(2,1)S(1)} %copy-done.15), channel_id=1, source_target_pairs={{0,16},{1,17},{2,18},{3,19},{4,20},{5,21},{6,22},{7,23},{8,24},{9,... | collective-permute-start | bytes 442376 | tf_op jit(solution)/shard_map/ppermute | solution.py:684
  23.4 14.0 %collective-permute-start.5 = (bf16[8,64,512]{2,1,0:T(8,128)(2,1)}, bf16[8,64,512]{2,1,0:T(8,128)(2,1)S(1)}, u32[]{:S(2)}, u32[]{:S(2)}) collective-permute-start(bf16[8,64,512]{2,1,0:T(8,128)(2,1)} %get-tuple-element.209), channel_id=1, source_target_pairs={{0,4},{1,3},{2,6},{3,1},{4,0},{5,7},{6,2},{7,5},{8,12},{9,11},{10,... | collective-permute-start | bytes 1572872 | tf_op jit(solution)/shard_map/ppermute | solution.py:684
  25.1 12.2 %collective-permute-start.3 = (bf16[2,128,512]{2,1,0:T(8,128)(2,1)S(1)}, bf16[2,128,512]{2,1,0:T(8,128)(2,1)S(1)}, u32[]{:S(2)}, u32[]{:S(2)}) collective-permute-start(bf16[2,128,512]{2,1,0:T(8,128)(2,1)S(1)} %slice.58), channel_id=1, source_target_pairs={{0,1},{1,2},{2,3},{3,4},{4,5},{5,6},{6,7},{7,8},{8,9},{9,10},{10,1... | collective-permute-start | bytes 786440 | tf_op jit(solution)/shard_map/ppermute | solution.py:687
  26.2 11.6 %copy-start.17 = (bf16[2,128,512]{2,1,0:T(8,128)(2,1)S(1)}, bf16[2,128,512]{2,1,0:T(8,128)(2,1)}, u32[]{:S(2)}) copy-start(bf16[2,128,512]{2,1,0:T(8,128)(2,1)} %get-tuple-element.123) | copy-start | bytes 786436
  26.2 11.4 %collective-permute-start.8 = (bf16[2,64,1152]{2,1,0:T(8,128)(2,1)S(1)}, bf16[2,64,1152]{2,1,0:T(8,128)(2,1)S(1)}, u32[]{:S(2)}, u32[]{:S(2)}) collective-permute-start(bf16[2,64,1152]{2,1,0:T(8,128)(2,1)S(1)} %pad_maximum_fusion.3), channel_id=1, source_target_pairs={{0,8},{1,9},{2,10},{3,11},{4,12},{5,13},{6,14},{7,15},{8,0},{9,1},... | collective-permute-start | bytes 884744 | tf_op jit(solution)/shard_map/ppermute | solution.py:684
  37.4 2.8 %copy-start.2 = (s32[2,8]{1,0:T(2,128)S(1)}, s32[2,8]{1,0:T(2,128)}, u32[]{:S(2)}) copy-start(s32[2,8]{1,0:T(2,128)} %lengths.15) | copy-start | bytes 196
  37.4 2.8 %copy-start.3 = (s32[2]{0:T(128)S(1)}, s32[2]{0:T(128)}, u32[]{:S(2)}) copy-start(s32[2]{0:T(128)} %offsets.19) | copy-start | bytes 28
  37.4 2.8 %copy-start.4 = (s32[2]{0:T(128)S(1)}, s32[2]{0:T(128)}, u32[]{:S(2)}) copy-start(s32[2]{0:T(128)} %pad_add_fusion.1.place.place_ref) | copy-start | bytes 28
  37.4 2.8 %copy-start.6 = (f32[512]{0:T(512)S(1)}, f32[512]{0:T(512)}, u32[]{:S(2)}) copy-start(f32[512]{0:T(512)} %param.23) | copy-start | bytes 6148
  37.4 2.8 %copy-start.8 = (f32[512]{0:T(512)S(1)}, f32[512]{0:T(512)}, u32[]{:S(2)}) copy-start(f32[512]{0:T(512)} %param.24) | copy-start | bytes 6148
  37.4 2.8 %copy-start.12 = (f32[512]{0:T(512)S(1)}, f32[512]{0:T(512)}, u32[]{:S(2)}) copy-start(f32[512]{0:T(512)} %param.28) | copy-start | bytes 6148
  37.5 2.8 %copy-start.13 = (f32[512]{0:T(512)S(1)}, f32[512]{0:T(512)}, u32[]{:S(2)}) copy-start(f32[512]{0:T(512)} %param.29) | copy-start | bytes 6148
  37.5 2.7 %collective-permute-start.6 = (bf16[16,64,512]{2,1,0:T(8,128)(2,1)S(1)}, bf16[16,64,512]{2,1,0:T(8,128)(2,1)S(1)}, u32[]{:S(2)}, u32[]{:S(2)}) collective-permute-start(bf16[16,64,512]{2,1,0:T(8,128)(2,1)S(1)} %constant_dynamic-update-slice_fusion.9.near_ref), channel_id=1, source_target_pairs={{0,1},{1,0},{2,3},{3,2},{4,5},{5,4},{6,7},{7,6},{8,9},{9,8},{10,11... | collective-permute-start | bytes 3145736 | tf_op jit(solution)/shard_map/ppermute | solution.py:684
  37.7 12.8 %collective-permute-start.9 = (bf16[4,64,1152]{2,1,0:T(8,128)(2,1)S(1)}, bf16[4,64,1152]{2,1,0:T(8,128)(2,1)S(1)}, u32[]{:S(2)}, u32[]{:S(2)}) collective-permute-start(bf16[4,64,1152]{2,1,0:T(8,128)(2,1)S(1)} %pad_maximum_fusion.2), channel_id=1, source_target_pairs={{0,2},{1,5},{2,0},{3,7},{4,6},{5,1},{6,4},{7,3},{8,10},{9,13},{10,... | collective-permute-start | bytes 1769480 | tf_op jit(solution)/shard_map/ppermute | solution.py:684
  37.8 9.8 %collective-permute-start.10 = (bf16[2,128,512]{2,1,0:T(8,128)(2,1)S(1)}, bf16[2,128,512]{2,1,0:T(8,128)(2,1)S(1)}, u32[]{:S(2)}, u32[]{:S(2)}) collective-permute-start(bf16[2,128,512]{2,1,0:T(8,128)(2,1)S(1)} %copy-done.17), channel_id=1, source_target_pairs={{0,1},{1,2},{2,3},{3,4},{4,5},{5,6},{6,7},{7,8},{8,9},{9,10},{10,1... | collective-permute-start | bytes 786440 | tf_op jit(solution)/shard_map/ppermute | solution.py:687
  50.6 10.7 %collective-permute-start.11 = (bf16[8,64,640]{2,1,0:T(8,128)(2,1)S(1)}, bf16[8,64,640]{2,1,0:T(8,128)(2,1)S(1)}, u32[]{:S(2)}, u32[]{:S(2)}) collective-permute-start(bf16[8,64,640]{2,1,0:T(8,128)(2,1)S(1)} %slice.75), channel_id=1, source_target_pairs={{0,4},{1,3},{2,6},{3,1},{4,0},{5,7},{6,2},{7,5},{8,12},{9,11},{10,... | collective-permute-start | bytes 1966088 | tf_op jit(solution)/shard_map/ppermute | solution.py:684
  56.2 8.3 %copy-start = (bf16[2,2048,512]{2,1,0:T(8,128)(2,1)S(1)}, bf16[2,2048,512]{2,1,0:T(8,128)(2,1)}, u32[]{:S(2)}) copy-start(bf16[2,2048,512]{2,1,0:T(8,128)(2,1)} %cot_ref.3) | copy-start | bytes 12582916
  61.2 3.3 %copy-start.5 = (f32[2048]{0:T(1024)S(1)}, f32[2048]{0:T(1024)}, u32[]{:S(2)}) copy-start(f32[2048]{0:T(1024)} %param.35) | copy-start | bytes 24580
  61.2 3.3 %copy-start.7 = (f32[512]{0:T(512)S(1)}, f32[512]{0:T(512)}, u32[]{:S(2)}) copy-start(f32[512]{0:T(512)} %param.32) | copy-start | bytes 6148
  61.2 3.3 %copy-start.9 = (f32[512]{0:T(512)S(1)}, f32[512]{0:T(512)}, u32[]{:S(2)}) copy-start(f32[512]{0:T(512)} %param.31) | copy-start | bytes 6148
  61.2 3.3 %copy-start.10 = (f32[512]{0:T(512)S(1)}, f32[512]{0:T(512)}, u32[]{:S(2)}) copy-start(f32[512]{0:T(512)} %param.33) | copy-start | bytes 6148
  61.2 3.3 %copy-start.11 = (f32[512]{0:T(512)S(1)}, f32[512]{0:T(512)}, u32[]{:S(2)}) copy-start(f32[512]{0:T(512)} %param.37) | copy-start | bytes 6148
  61.4 3.1 %collective-permute-start.12 = (bf16[16,64,640]{2,1,0:T(8,128)(2,1)S(1)}, bf16[16,64,640]{2,1,0:T(8,128)(2,1)S(1)}, u32[]{:S(2)}, u32[]{:S(2)}) collective-permute-start(bf16[16,64,640]{2,1,0:T(8,128)(2,1)S(1)} %pad_maximum_fusion.near_ref), channel_id=1, source_target_pairs={{0,1},{1,0},{2,3},{3,2},{4,5},{5,4},{6,7},{7,6},{8,9},{9,8},{10,11... | collective-permute-start | bytes 3932168 | tf_op jit(solution)/shard_map/ppermute | solution.py:684
  61.5 16.5 %collective-permute-start.13 = (bf16[8,64,512]{2,1,0:T(8,128)(2,1)S(1)}, bf16[8,64,512]{2,1,0:T(8,128)(2,1)S(1)}, u32[]{:S(2)}, u32[]{:S(2)}) collective-permute-start(bf16[8,64,512]{2,1,0:T(8,128)(2,1)S(1)} %slice.76), channel_id=1, source_target_pairs={{0,4},{1,3},{2,6},{3,1},{4,0},{5,7},{6,2},{7,5},{8,12},{9,11},{10,... | collective-permute-start | bytes 1572872 | tf_op jit(solution)/shard_map/ppermute | solution.py:684
  78.1 2.7 %collective-permute-start.14 = (bf16[16,64,512]{2,1,0:T(8,128)(2,1)S(1)}, bf16[16,64,512]{2,1,0:T(8,128)(2,1)S(1)}, u32[]{:S(2)}, u32[]{:S(2)}) collective-permute-start(bf16[16,64,512]{2,1,0:T(8,128)(2,1)S(1)} %get-tuple-element.141), channel_id=1, source_target_pairs={{0,1},{1,0},{2,3},{3,2},{4,5},{5,4},{6,7},{7,6},{8,9},{9,8},{10,11... | collective-permute-start | bytes 3145736 | tf_op jit(solution)/shard_map/ppermute | solution.py:684
  78.3 4.7 %collective-permute-start.15 = (bf16[16,64,512]{2,1,0:T(8,128)(2,1)S(1)}, bf16[16,64,512]{2,1,0:T(8,128)(2,1)S(1)}, u32[]{:S(2)}, u32[]{:S(2)}) collective-permute-start(bf16[16,64,512]{2,1,0:T(8,128)(2,1)S(1)} %pad_maximum_fusion.1.near_ref), channel_id=1, source_target_pairs={{0,1},{1,0},{2,3},{3,2},{4,5},{5,4},{6,7},{7,6},{8,9},{9,8},{10,11... | collective-permute-start | bytes 3145736 | tf_op jit(solution)/shard_map/ppermute | solution.py:684
  81.2 15.6 %collective-permute-start.16 = (bf16[8,64,512]{2,1,0:T(8,128)(2,1)S(1)}, bf16[8,64,512]{2,1,0:T(8,128)(2,1)S(1)}, u32[]{:S(2)}, u32[]{:S(2)}) collective-permute-start(bf16[8,64,512]{2,1,0:T(8,128)(2,1)S(1)} %slice.103), channel_id=1, source_target_pairs={{0,4},{1,3},{2,6},{3,1},{4,0},{5,7},{6,2},{7,5},{8,12},{9,11},{10,... | collective-permute-start | bytes 1572872 | tf_op jit(solution)/shard_map/ppermute | solution.py:684
  97.0 6.4 %collective-permute-start.17 = (bf16[16,64,640]{2,1,0:T(8,128)(2,1)S(1)}, bf16[16,64,640]{2,1,0:T(8,128)(2,1)S(1)}, u32[]{:S(2)}, u32[]{:S(2)}) collective-permute-start(bf16[16,64,640]{2,1,0:T(8,128)(2,1)S(1)} %get-tuple-element.150), channel_id=1, source_target_pairs={{0,1},{1,0},{2,3},{3,2},{4,5},{5,4},{6,7},{7,6},{8,9},{9,8},{10,11... | collective-permute-start | bytes 3932168 | tf_op jit(solution)/shard_map/ppermute | solution.py:684
  101.3 8.2 %collective-permute-start.18 = (bf16[4,64,512]{2,1,0:T(8,128)(2,1)S(1)}, bf16[4,64,512]{2,1,0:T(8,128)(2,1)S(1)}, u32[]{:S(2)}, u32[]{:S(2)}) collective-permute-start(bf16[4,64,512]{2,1,0:T(8,128)(2,1)S(1)} %slice.105), channel_id=1, source_target_pairs={{0,2},{1,5},{2,0},{3,7},{4,6},{5,1},{6,4},{7,3},{8,10},{9,13},{10,... | collective-permute-start | bytes 786440 | tf_op jit(solution)/shard_map/ppermute | solution.py:684
  103.9 12.9 %collective-permute-start.20 = (bf16[8,64,640]{2,1,0:T(8,128)(2,1)S(1)}, bf16[8,64,640]{2,1,0:T(8,128)(2,1)S(1)}, u32[]{:S(2)}, u32[]{:S(2)}) collective-permute-start(bf16[8,64,640]{2,1,0:T(8,128)(2,1)S(1)} %slice.102), channel_id=1, source_target_pairs={{0,4},{1,3},{2,6},{3,1},{4,0},{5,7},{6,2},{7,5},{8,12},{9,11},{10,... | collective-permute-start | bytes 1966088 | tf_op jit(solution)/shard_map/ppermute | solution.py:684
  109.6 16.4 %copy-start.14 = (f32[4,64,512]{2,1,0:T(8,128)}, f32[4,64,512]{2,1,0:T(8,128)S(1)}, u32[]{:S(2)}) copy-start(f32[4,64,512]{2,1,0:T(8,128)S(1)} %slice_add_fusion.3) | copy-start | bytes 1572868
  116.7 2.8 %collective-permute-start.19 = (bf16[1056,512]{1,0:T(8,128)(2,1)S(1)}, bf16[1056,512]{1,0:T(8,128)(2,1)S(1)}, u32[]{:S(2)}, u32[]{:S(2)}) collective-permute-start(bf16[1056,512]{1,0:T(8,128)(2,1)S(1)} %get-tuple-element.165.mine_ref), channel_id=1, source_target_pairs={{0,1},{1,0},{2,3},{3,2},{4,5},{5,4},{6,7},{7,6},{8,9},{9,8},{10,11... | collective-permute-start | bytes 3244040 | tf_op jit(solution)/shard_map/ppermute | solution.py:684
  117.0 8.8 %collective-permute-start.21 = (bf16[4,64,640]{2,1,0:T(8,128)(2,1)S(1)}, bf16[4,64,640]{2,1,0:T(8,128)(2,1)S(1)}, u32[]{:S(2)}, u32[]{:S(2)}) collective-permute-start(bf16[4,64,640]{2,1,0:T(8,128)(2,1)S(1)} %slice.104), channel_id=1, source_target_pairs={{0,2},{1,5},{2,0},{3,7},{4,6},{5,1},{6,4},{7,3},{8,10},{9,13},{10,... | collective-permute-start | bytes 983048 | tf_op jit(solution)/shard_map/ppermute | solution.py:684
  119.7 11.0 %collective-permute-start.23 = (bf16[544,512]{1,0:T(8,128)(2,1)S(1)}, bf16[544,512]{1,0:T(8,128)(2,1)S(1)}, u32[]{:S(2)}, u32[]{:S(2)}) collective-permute-start(bf16[544,512]{1,0:T(8,128)(2,1)S(1)} %get-tuple-element.168.mine_ref), channel_id=1, source_target_pairs={{0,4},{1,3},{2,6},{3,1},{4,0},{5,7},{6,2},{7,5},{8,12},{9,11},{10,... | collective-permute-start | bytes 1671176 | tf_op jit(solution)/shard_map/ppermute | solution.py:684
  125.9 8.5 %collective-permute-start.25 = (bf16[2,64,1152]{2,1,0:T(8,128)(2,1)S(1)}, bf16[2,64,1152]{2,1,0:T(8,128)(2,1)S(1)}, u32[]{:S(2)}, u32[]{:S(2)}) collective-permute-start(bf16[2,64,1152]{2,1,0:T(8,128)(2,1)S(1)} %pad_maximum_fusion.4), channel_id=1, source_target_pairs={{0,8},{1,9},{2,10},{3,11},{4,12},{5,13},{6,14},{7,15},{8,0},{9,1},... | collective-permute-start | bytes 884744 | tf_op jit(solution)/shard_map/ppermute | solution.py:684
  126.0 8.4 %slice-start = ((f32[4,64,512]{2,1,0:T(8,128)}), f32[2,64,512]{2,1,0:T(8,128)S(1)}, s32[]{:S(2)}) async-start(f32[4,64,512]{2,1,0:T(8,128)} %copy-done.14), calls=%async_computation | async-start | bytes 524288 | tf_op jit(solution)/shard_map/slice | solution.py:723
  126.1 19.8 %collective-permute-start.22 = (bf16[2,2,128,512]{3,2,1,0:T(8,128)(2,1)S(1)}, bf16[2,2,128,512]{3,2,1,0:T(8,128)(2,1)S(1)}, u32[]{:S(2)}, u32[]{:S(2)}) collective-permute-start(bf16[2,2,128,512]{3,2,1,0:T(8,128)(2,1)S(1)} %get-tuple-element.174), channel_id=1, source_target_pairs={{0,31},{1,0},{2,1},{3,2},{4,3},{5,4},{6,5},{7,6},{8,7},{9,8},{10,9... | collective-permute-start | bytes 1572872 | tf_op jit(solution)/shard_map/ppermute | solution.py:687
  130.8 11.4 %collective-permute-start.24 = (bf16[288,512]{1,0:T(8,128)(2,1)S(1)}, bf16[288,512]{1,0:T(8,128)(2,1)S(1)}, u32[]{:S(2)}, u32[]{:S(2)}) collective-permute-start(bf16[288,512]{1,0:T(8,128)(2,1)S(1)} %get-tuple-element.178.mine_ref), channel_id=1, source_target_pairs={{0,2},{1,5},{2,0},{3,7},{4,6},{5,1},{6,4},{7,3},{8,10},{9,13},{10,... | collective-permute-start | bytes 884744 | tf_op jit(solution)/shard_map/ppermute | solution.py:684
  134.5 14.3 %collective-permute-start.27 = (bf16[1,64,1152]{2,1,0:T(8,128)(2,1)S(1)}, bf16[1,64,1152]{2,1,0:T(8,128)(2,1)S(1)}, u32[]{:S(2)}, u32[]{:S(2)}) collective-permute-start(bf16[1,64,1152]{2,1,0:T(8,128)(2,1)S(1)} %slice.107), channel_id=1, source_target_pairs={{0,16},{1,17},{2,18},{3,19},{4,20},{5,21},{6,22},{7,23},{8,24},{9,... | collective-permute-start | bytes 442376 | tf_op jit(solution)/shard_map/ppermute | solution.py:684
  142.3 7.3 %collective-permute-start.28 = (bf16[80,512]{1,0:T(8,128)(2,1)S(1)}, bf16[80,512]{1,0:T(8,128)(2,1)S(1)}, u32[]{:S(2)}, u32[]{:S(2)}) collective-permute-start(bf16[80,512]{1,0:T(8,128)(2,1)S(1)} %get-tuple-element.190), channel_id=1, source_target_pairs={{0,8},{1,9},{2,10},{3,11},{4,12},{5,13},{6,14},{7,15},{8,0},{9,1},... | collective-permute-start | bytes 245768 | tf_op jit(solution)/shard_map/ppermute | solution.py:712
  142.3 7.2 %collective-permute-start.29 = (bf16[80,512]{1,0:T(8,128)(2,1)S(1)}, bf16[80,512]{1,0:T(8,128)(2,1)S(1)}, u32[]{:S(2)}, u32[]{:S(2)}) collective-permute-start(bf16[80,512]{1,0:T(8,128)(2,1)S(1)} %get-tuple-element.192), channel_id=1, source_target_pairs={{0,24},{1,25},{2,26},{3,27},{4,28},{5,29},{6,30},{7,31},{8,16},{9,... | collective-permute-start | bytes 245768 | tf_op jit(solution)/shard_map/ppermute | solution.py:712
  142.4 8.4 %collective-permute-start.26 = (bf16[80,512]{1,0:T(8,128)(2,1)S(1)}, bf16[80,512]{1,0:T(8,128)(2,1)S(1)}, u32[]{:S(2)}, u32[]{:S(2)}) collective-permute-start(bf16[80,512]{1,0:T(8,128)(2,1)S(1)} %get-tuple-element.181.refs_1_), channel_id=1, source_target_pairs={{0,16},{1,17},{2,18},{3,19},{4,20},{5,21},{6,22},{7,23},{8,24},{9,... | collective-permute-start | bytes 245768 | tf_op jit(solution)/shard_map/ppermute | solution.py:712

commit v2 on v1

--- a/solution.py
+++ b/solution.py
@@ -458,7 +458,7 @@
 
 
 def weights_back_kernel(
-    apart, place, offsets, lengths, block_of, row_of, slots_ref, xs_ref, grad_ref, pooled_ref, sums_ref, w_ref,
+    apart, place_ref, offsets, lengths, block_of, row_of, slots_ref, xs_ref, grad_ref, pooled_ref, sums_ref, w_ref,
     gain, shift, small_ref, down_ref, gub1_ref, gub2_ref, line_ref, keep_ref, send_ref, *refs
 ):
     if apart:
@@ -471,7 +471,7 @@
     turned = []
     column = jnp.zeros((1, 3 * D), F32)
     for mi in range(2):
-        _, offset, ends = row_info(place, offsets, lengths, mi)
+        _, offset, ends = row_info(place_ref, offsets, lengths, mi)
         first, last = summary_range(iota((summaries, 1), 0), offset, ends)
         root = jnp.sqrt((last - first + 1).astype(F32))
         hat, _ = unit(xs_ref[mi].astype(F32))
@@ -479,6 +479,39 @@
         column += jnp.sum(grad_ref[mi].astype(F32), axis=0, keepdims=True)
         column += jnp.sum(root * pooled_ref[mi].astype(F32), axis=0, keepdims=True)
         back_ref[mi] = dot_cols(pooled_ref[mi], w_ref[...]).astype(BF16)
+    for base in range(0, stack_ref.shape[0], 32):
+        names = [slots_ref[mi : mi + 1, 16 * base : 16 * base + 512] for mi in range(2)]
+        spread = [
+            jnp.where(iota((summaries, 1), 0) == named, 1.0, 0.0).astype(BF16).T for named in names
+        ]
+        piece = (dot(spread[0], back_ref[0]) + dot(spread[1], back_ref[1])).astype(BF16)
+        for lane in range(D // LANES):
+            part = piece[:, lane * LANES : (lane + 1) * LANES]
+            stack_ref[base : base + 32, 16 * lane : 16 * lane + 16, :] = part.reshape(32, 16, LANES)
+
+    def place(d):
+        return pl.ds(pl.multiple_of(d * shard, 16), shard)
+
+    def emit_sums(d, carry):
+        for target, slot in ((keep_ref, d), (send_ref, half + d)):
+            pltpu.make_async_copy(stack_ref.at[slot], target.at[place(d), 384:512], sem.at[1]).start()
+        return carry
+
+    def emit(m):
+        def body(d, carry):
+            for target, slot in ((keep_ref, d), (send_ref, half + d)):
+
+                @pl.when(block_of[slot] == m)
+                def _():
+                    source = gwb_ref.at[pl.ds(pl.multiple_of(row_of[slot] * shard, 16), shard), m * 384 : (m + 1) * 384]
+                    pltpu.make_async_copy(source, target.at[place(d), 0:384], sem.at[0]).start()
+
+            return carry
+
+        lax.fori_loop(0, half, body, 0)
+
+    if not apart:
+        lax.fori_loop(0, half, emit_sums, 0)
     turned = jnp.concatenate(turned, axis=1)
     gain_col, shift_col = gain[...].T, shift[...].T
     grad_gain = jnp.zeros((D, 1), F32)
@@ -491,6 +524,7 @@
         grad_gain += jnp.sum(hats * w, axis=1, keepdims=True)
         grad_shift += jnp.sum(sums * w, axis=1, keepdims=True)
         gwb_ref[:, cols] = (hats * gain_col + shift_col * sums).astype(BF16)
+        emit(m)
         line_ref[10:11, lanes] = sums[:, :128]
         line_ref[11:12, lanes] = sums[:, 256:]
     line_ref[8:9, :] = grad_gain.T
@@ -501,29 +535,6 @@
         for j, ref in enumerate((gub1_ref, gub2_ref)):
             line_ref[4 + i : 5 + i, j * 256 : (j + 1) * 256] = ref[:, i * 256 : (i + 1) * 256]
     line_ref[12:16, :] = jnp.zeros((4, D), F32)
-    for base in range(0, stack_ref.shape[0], 32):
-        names = [slots_ref[mi : mi + 1, 16 * base : 16 * base + 512] for mi in range(2)]
-        spread = [
-            jnp.where(iota((summaries, 1), 0) == named, 1.0, 0.0).astype(BF16).T for named in names
-        ]
-        piece = (dot(spread[0], back_ref[0]) + dot(spread[1], back_ref[1])).astype(BF16)
-        for lane in range(D // LANES):
-            part = piece[:, lane * LANES : (lane + 1) * LANES]
-            stack_ref[base : base + 32, 16 * lane : 16 * lane + 16, :] = part.reshape(32, 16, LANES)
-
-    def emit(d, carry):
-        for target, slot in ((keep_ref, d), (send_ref, half + d)):
-            first_row = pl.multiple_of(row_of[slot] * shard, 16)
-            cols = pl.ds(pl.multiple_of(block_of[slot] * 384, 128), 384)
-            here = target.at[pl.ds(pl.multiple_of(d * shard, 16), shard), :]
-            pltpu.make_async_copy(
-                gwb_ref.at[pl.ds(first_row, shard), cols], here.at[:, 0:384], sem.at[0]
-            ).start()
-            if not apart:
-                pltpu.make_async_copy(stack_ref.at[slot], here.at[:, 384:512], sem.at[1]).start()
-        return carry
-
-    lax.fori_loop(0, half, emit, 0)
     if apart:
         pltpu.make_async_copy(stack_ref, all_ref, sem.at[1]).start()
     else:

time: 156 us -> 159 us (1.019)
  Pallas kernels: 72 us -> 74.4 us
    pallas_call x1, Pallas kernels: 6.99 us -> 9.66 us  [per_device(): call(partial(weights_back_kernel, apart), [shape((16, D), F32)] + [shape(...]
  transfers between devices with their start and end apart: 30 -> 30, of which waited for: 15 -> 16; matrix products, arithmetic and copies ran while one was open for 2% -> 2% of each run, Pallas kernels for 42% -> 43%
where the time goes in v2:
time: 159 us; the launch traced here: 157 us
  Pallas kernels  74.4 us (47%)
  waiting for transfers between devices  43.7 us (27%)
  starting transfers between devices  32.9 us (21%)
  local copies, waits for them, and re-layouts  2.55 us (2%)
  other arithmetic  2.24 us (1%)
    ppermute x21, waiting for transfers between devices, swap(): return lax.ppermute(value, AXES, pairs)  27.3 us
    ppermute x21, starting transfers between devices, swap(): return lax.ppermute(value, AXES, pairs)  22.4 us
    pallas_call x4, Pallas kernels, call_row(): call(partial(kernel, mi), outs, [SMEM] * 3 + [block(a.shape) for a in arr...  16.1 us
    pallas_call x1, Pallas kernels, per_device(): call(mlp_second_kernel, [shape(wide, BF16)] * 3 + [shape((8, D), F32)] +...  13.8 us
    pallas_call x1, Pallas kernels, per_device(): call(mlp_first_kernel, [tall_float] + [tall_low] * 4 + [shape((D, D), BF1...  13.4 us
    ppermute x3, waiting for transfers between devices, turn(): lax.ppermute(value, AXES, [(i, (i + by) % count) for i in range(count)])  10.7 us
    pallas_call x1, Pallas kernels, per_device(): call(partial(weights_back_kernel, apart), [shape((16, D), F32)] + [shape(...  9.66 us
    ppermute x6, starting transfers between devices, reach(): return lax.ppermute(value, AXES, [(i, i ^ flip) for i in range(count)])  9.29 us
  transfers between devices with their start and end apart: 30, of which 16 were waited for; matrix products, arithmetic and copies ran while one was open for 2% of the time, Pallas kernels for 43%

profile of v2, /device:TPU:0, one launch (start us, length us, event | category | flops | bytes accessed | tf_op | source)
XLA Modules:
  0.0 157.3 jit_solution(16440829000050696077)
XLA Ops:
  0.7 0.6 pad_add_fusion.1.place.place_ref
  1.2 3.9 %shard_map.314 = (bf16[1,64,512]{2,1,0:T(8,128)(2,1)}, bf16[1,64,1152]{2,1,0:T(8,128)(2,1)}, bf16[2,128,512]{2,1,0:T(8,128)(2,1)}) custom-call(s32[2]{0:T(128)} %pad_add_fusion.1.place.place_ref, s32[2]{0:T(128)} %offsets.19, s32[2,8]{1,0:T(2,128)} %lengths.15, bf16[2,512,512]{2,1,0:T(8,128)(2,1)} %x_ref.5, bf16[2,2048,512]{2,1,0:T(8,128)(2,1)} %cot_ref.3, ...), custom_call_target="tpu_custom_call" | custom-call | flops 1 | bytes 1 | tf_op jit(solution)/shard_map/pallas_call | solution.py:772
  5.1 5.1 %collective-permute-start.2 = (bf16[1,64,512]{2,1,0:T(8,128)(2,1)}, bf16[1,64,512]{2,1,0:T(8,128)(2,1)S(1)}, u32[]{:S(2)}, u32[]{:S(2)}) collective-permute-start(bf16[1,64,512]{2,1,0:T(8,128)(2,1)} %get-tuple-element.113), channel_id=1, source_target_pairs={{0,24},{1,25},{2,26},{3,27},{4,28},{5,29},{6,30},{7,31},{8,16},{9,... | collective-permute-start | bytes 196616 | tf_op jit(solution)/shard_map/ppermute | solution.py:723
  10.3 0.6 collective-permute-start
  10.9 0.9 constant_dynamic-update-slice_fusion.8
  11.8 4.3 %collective-permute-done = bf16[1,64,512]{2,1,0:T(8,128)(2,1)S(1)} collective-permute-done((bf16[1,64,512]{2,1,0:T(8,128)(2,1)}, bf16[1,64,512]{2,1,0:T(8,128)(2,1)S(1)}, u32[]{:S(2)}, u32[]{:S(2)}) %collective-permute-start) | collective-permute-done | bytes 65568 | tf_op jit(solution)/shard_map/ppermute | solution.py:723
  16.2 1.6 collective-permute-start.4
  17.8 2.0 %collective-permute-start.7 = (bf16[1,64,1152]{2,1,0:T(8,128)(2,1)S(1)}, bf16[1,64,1152]{2,1,0:T(8,128)(2,1)S(1)}, u32[]{:S(2)}, u32[]{:S(2)}) collective-permute-start(bf16[1,64,1152]{2,1,0:T(8,128)(2,1)S(1)} %copy-done.15), channel_id=1, source_target_pairs={{0,16},{1,17},{2,18},{3,19},{4,20},{5,21},{6,22},{7,23},{8,24},{9,... | collective-permute-start | bytes 442376 | tf_op jit(solution)/shard_map/ppermute | solution.py:695
  19.8 2.8 %collective-permute-done.4 = bf16[4,64,512]{2,1,0:T(8,128)(2,1)S(1)} collective-permute-done((bf16[4,64,512]{2,1,0:T(8,128)(2,1)S(1)}, bf16[4,64,512]{2,1,0:T(8,128)(2,1)S(1)}, u32[]{:S(2)}, u32[]{:S(2)}) %collective-permute-start.4) | collective-permute-done | bytes 262176 | tf_op jit(solution)/shard_map/ppermute | solution.py:695
  22.6 0.7 constant_dynamic-update-slice_fusion.4
  23.4 1.5 collective-permute-start.5
  24.9 0.1 add_select_fusion.1
  25.0 0.1 select_n.110
  25.1 0.1 select_n.112
  25.1 1.0 collective-permute-done.7
  26.2 0.6 collective-permute-start.8
  26.8 10.5 %collective-permute-done.3.left_ref = bf16[2,128,512]{2,1,0:T(8,128)(2,1)S(1)} collective-permute-done((bf16[2,128,512]{2,1,0:T(8,128)(2,1)S(1)}, bf16[2,128,512]{2,1,0:T(8,128)(2,1)S(1)}, u32[]{:S(2)}, u32[]{:S(2)}) %collective-permute-start.3) | collective-permute-done | bytes 262176 | tf_op jit(solution)/shard_map/ppermute | solution.py:698
  37.6 0.1 pad_maximum_fusion.2
  37.8 0.7 collective-permute-start.10
  38.6 1.6 %collective-permute-done.6.far_ref = bf16[16,64,512]{2,1,0:T(8,128)(2,1)S(1)} collective-permute-done((bf16[16,64,512]{2,1,0:T(8,128)(2,1)S(1)}, bf16[16,64,512]{2,1,0:T(8,128)(2,1)S(1)}, u32[]{:S(2)}, u32[]{:S(2)}) %collective-permute-start.6) | collective-permute-done | bytes 1048608 | tf_op jit(solution)/shard_map/ppermute | solution.py:695
  40.2 7.1 %shard_map.315 = (bf16[2,512,512]{2,1,0:T(8,128)(2,1)S(1)}, bf16[2,512,1536]{2,1,0:T(8,128)(2,1)S(1)}, bf16[2,128,1536]{2,1,0:T(8,128)(2,1)S(1)}, f32[2,128,512]{2,1,0:T(8,128)S(1)}, bf16[512,1536]{1,0:T(8,128)(2,1)S(1)}) custom-call(s32[2]{0:T(128)S(1)} %copy-done.4, s32[2]{0:T(128)S(1)} %copy-done.3, s32[2,8]{1,0:T(2,128)S(1)} %copy-done.2, ...), custom_call_target="tpu_custom_call" | custom-call | flops 1 | bytes 1 | tf_op jit(solution)/shard_map/pallas_call | solution.py:804
  47.3 0.2 collective-permute-done.10.left_ref
  47.6 2.9 %collective-permute-done.9 = bf16[4,64,1152]{2,1,0:T(8,128)(2,1)S(1)} collective-permute-done((bf16[4,64,1152]{2,1,0:T(8,128)(2,1)S(1)}, bf16[4,64,1152]{2,1,0:T(8,128)(2,1)S(1)}, u32[]{:S(2)}, u32[]{:S(2)}) %collective-permute-start.9) | collective-permute-done | bytes 589856 | tf_op jit(solution)/shard_map/ppermute | solution.py:695
  50.6 1.8 %collective-permute-start.11 = (bf16[8,64,640]{2,1,0:T(8,128)(2,1)S(1)}, bf16[8,64,640]{2,1,0:T(8,128)(2,1)S(1)}, u32[]{:S(2)}, u32[]{:S(2)}) collective-permute-start(bf16[8,64,640]{2,1,0:T(8,128)(2,1)S(1)} %slice.75), channel_id=1, source_target_pairs={{0,4},{1,3},{2,6},{3,1},{4,0},{5,7},{6,2},{7,5},{8,12},{9,11},{10,... | collective-permute-start | bytes 1966088 | tf_op jit(solution)/shard_map/ppermute | solution.py:695
  52.4 3.9 %shard_map.316 = (bf16[2,512,512]{2,1,0:T(8,128)(2,1)S(1)}, f32[2,4,4,1,256]{4,3,2,1,0:T(1,128)S(1)}) custom-call(s32[2]{0:T(128)S(1)} %copy-done.4, s32[2]{0:T(128)S(1)} %copy-done.3, s32[2,8]{1,0:T(2,128)S(1)} %copy-done.2, bf16[2,512,1536]{2,1,0:T(8,128)(2,1)S(1)} %get-tuple-element.125.qkv_ref, bf16[2,128,1536]{2,1,0:T(8,128)(2,1)S(1)} %get-tuple-element.121.skv_ref), custom_call_target="tpu_custom_call" | custom-call | flops 1 | bytes 1 | tf_op jit(solution)/shard_map/pallas_call | solution.py:667
  56.2 3.9 %shard_map.317 = (bf16[2,512,512]{2,1,0:T(8,128)(2,1)S(1)}, f32[2,4,4,1,256]{4,3,2,1,0:T(1,128)S(1)}) custom-call(s32[2]{0:T(128)S(1)} %copy-done.4, s32[2]{0:T(128)S(1)} %copy-done.3, s32[2,8]{1,0:T(2,128)S(1)} %copy-done.2, bf16[2,512,1536]{2,1,0:T(8,128)(2,1)S(1)} %get-tuple-element.125.qkv_ref, ...), custom_call_target="tpu_custom_call", output_to_operand_aliasing={{0}: (5, {}), {1}: (6, {})} | custom-call | flops 1 | bytes 1 | tf_op jit(solution)/shard_map/pallas_call | solution.py:667
  60.1 1.1 collective-permute-done.11
  61.2 0.1 pad_maximum_fusion.near_ref
  61.5 1.8 %collective-permute-start.13 = (bf16[8,64,512]{2,1,0:T(8,128)(2,1)S(1)}, bf16[8,64,512]{2,1,0:T(8,128)(2,1)S(1)}, u32[]{:S(2)}, u32[]{:S(2)}) collective-permute-start(bf16[8,64,512]{2,1,0:T(8,128)(2,1)S(1)} %slice.76), channel_id=1, source_target_pairs={{0,4},{1,3},{2,6},{3,1},{4,0},{5,7},{6,2},{7,5},{8,12},{9,11},{10,... | collective-permute-start | bytes 1572872 | tf_op jit(solution)/shard_map/ppermute | solution.py:695
  63.3 1.2 collective-permute-done.12.far_ref
  64.5 13.4 %shard_map.318 = (f32[1024,512]{1,0:T(8,128)S(1)}, bf16[1024,512]{1,0:T(8,128)(2,1)S(1)}, bf16[1024,512]{1,0:T(8,128)(2,1)S(1)}, bf16[1024,512]{1,0:T(8,128)(2,1...) custom-call(s32[2]{0:T(128)S(1)} %copy-done.4, ...), custom_call_target="tpu_custom_call" | custom-call | flops 1 | bytes 1 | tf_op jit(solution)/shard_map/pallas_call | solution.py:836
  78.0 0.1 pad_maximum_fusion.1.near_ref
  78.1 0.2 collective-permute-start.14
  78.3 0.4 collective-permute-start.15
  78.7 2.1 %collective-permute-done.14 = bf16[16,64,512]{2,1,0:T(8,128)(2,1)S(1)} collective-permute-done((bf16[16,64,512]{2,1,0:T(8,128)(2,1)S(1)}, bf16[16,64,512]{2,1,0:T(8,128)(2,1)S(1)}, u32[]{:S(2)}, u32[]{:S(2)}) %collective-permute-start.14) | collective-permute-done | bytes 1048608 | tf_op jit(solution)/shard_map/ppermute | solution.py:695
  80.8 0.3 convert_add_fusion.1
  81.2 1.8 %collective-permute-start.16 = (bf16[8,64,512]{2,1,0:T(8,128)(2,1)S(1)}, bf16[8,64,512]{2,1,0:T(8,128)(2,1)S(1)}, u32[]{:S(2)}, u32[]{:S(2)}) collective-permute-start(bf16[8,64,512]{2,1,0:T(8,128)(2,1)S(1)} %slice.103), channel_id=1, source_target_pairs={{0,4},{1,3},{2,6},{3,1},{4,0},{5,7},{6,2},{7,5},{8,12},{9,11},{10,... | collective-permute-start | bytes 1572872 | tf_op jit(solution)/shard_map/ppermute | solution.py:695
  83.0 13.8 %shard_map.319 = (bf16[2,512,512]{2,1,0:T(8,128)(2,1)S(1)}, bf16[2,512,512]{2,1,0:T(8,128)(2,1)S(1)}, bf16[2,512,512]{2,1,0:T(8,128)(2,1)S(1)}, f32[8,512]{1,0:T...) custom-call(s32[32]{0:T(128)S(1)} %get-tuple-element.226.block_of, ...), custom_call_target="tpu_custom_call" | custom-call | flops 1 | bytes 1 | tf_op jit(solution)/shard_map/pallas_call | solution.py:857
  96.8 0.2 slice_add_fusion.1
  97.1 4.2 %shard_map.320 = (bf16[2,512,1536]{2,1,0:T(8,128)(2,1)S(1)}, bf16[2,128,1536]{2,1,0:T(8,128)(2,1)S(1)}) custom-call(s32[2]{0:T(128)S(1)} %copy-done.4, s32[2]{0:T(128)S(1)} %copy-done.3, s32[2,8]{1,0:T(2,128)S(1)} %copy-done.2, bf16[2,512,1536]{2,1,0:T(8,128)(2,1)S(1)} %get-tuple-element.125.qkv_ref, bf16[2,128,1536]{2,1,0:T(8,128)(2,1)S(1)} %get-tuple-element.121.skv_ref, ...), custom_call_target="tpu_custom_call" | custom-call | flops 1 | bytes 1 | tf_op jit(solution)/shard_map/pallas_call | solution.py:667
  101.3 2.2 %collective-permute-start.18 = (bf16[4,64,512]{2,1,0:T(8,128)(2,1)S(1)}, bf16[4,64,512]{2,1,0:T(8,128)(2,1)S(1)}, u32[]{:S(2)}, u32[]{:S(2)}) collective-permute-start(bf16[4,64,512]{2,1,0:T(8,128)(2,1)S(1)} %slice.105), channel_id=1, source_target_pairs={{0,2},{1,5},{2,0},{3,7},{4,6},{5,1},{6,4},{7,3},{8,10},{9,13},{10,... | collective-permute-start | bytes 786440 | tf_op jit(solution)/shard_map/ppermute | solution.py:695
  103.5 0.3 convert_add_fusion
  103.9 1.2 collective-permute-start.20
  105.1 4.2 %shard_map.321 = (bf16[2,512,1536]{2,1,0:T(8,128)(2,1)S(1)}, bf16[2,128,1536]{2,1,0:T(8,128)(2,1)S(1)}) custom-call(s32[2]{0:T(128)S(1)} %copy-done.4, s32[2]{0:T(128)S(1)} %copy-done.3, s32[2,8]{1,0:T(2,128)S(1)} %copy-done.2, bf16[2,512,1536]{2,1,0:T(8,128)(2,1)S(1)} %get-tuple-element.125.qkv_ref, ...), custom_call_target="tpu_custom_call", output_to_operand_aliasing={{0}: (7, {}), {1}: (8, {})} | custom-call | flops 1 | bytes 1 | tf_op jit(solution)/shard_map/pallas_call | solution.py:667
  109.3 0.3 collective-permute-done.18
  109.7 9.7 %shard_map.322 = (f32[16,512]{1,0:T(8,128)}, bf16[1024,512]{1,0:T(8,128)(2,1)S(1)}, bf16[1056,512]{1,0:T(8,128)(2,1)S(1)}) custom-call(s32[2]{0:T(128)S(1)} %copy-done.4, s32[2]{0:T(128)S(1)} %copy-done.3, s32[2,8]{1,0:T(2,128)S(1)} %copy-done.2, s32[32]{0:T(128)S(1)} %get-tuple-element.226.block_of, s32[32]{0:T(128)S(1)} %get-tuple-element.225.row_of, ...), custom_call_target="tpu_custom_call" | custom-call | flops 1 | bytes 1 | tf_op jit(solution)/shard_map/pallas_call | solution.py:884
  119.4 0.2 slice_add_fusion
  119.6 2.5 %collective-permute-start.21 = (bf16[4,64,640]{2,1,0:T(8,128)(2,1)S(1)}, bf16[4,64,640]{2,1,0:T(8,128)(2,1)S(1)}, u32[]{:S(2)}, u32[]{:S(2)}) collective-permute-start(bf16[4,64,640]{2,1,0:T(8,128)(2,1)S(1)} %slice.104), channel_id=1, source_target_pairs={{0,2},{1,5},{2,0},{3,7},{4,6},{5,1},{6,4},{7,3},{8,10},{9,13},{10,... | collective-permute-start | bytes 983048 | tf_op jit(solution)/shard_map/ppermute | solution.py:695
  122.1 0.2 shard_map.323
  122.4 2.9 %collective-permute-start.23 = (bf16[544,512]{1,0:T(8,128)(2,1)S(1)}, bf16[544,512]{1,0:T(8,128)(2,1)S(1)}, u32[]{:S(2)}, u32[]{:S(2)}) collective-permute-start(bf16[544,512]{1,0:T(8,128)(2,1)S(1)} %get-tuple-element.168.mine_ref), channel_id=1, source_target_pairs={{0,4},{1,3},{2,6},{3,1},{4,0},{5,7},{6,2},{7,5},{8,12},{9,11},{10,... | collective-permute-start | bytes 1671176 | tf_op jit(solution)/shard_map/ppermute | solution.py:695
  125.2 2.8 %shard_map.324 = (f32[2,512,512]{2,1,0:T(8,128)S(1)}, bf16[2,2,128,512]{3,2,1,0:T(8,128)(2,1)S(1)}) custom-call(bf16[2,512,1536]{2,1,0:T(8,128)(2,1)S(1)} %get-tuple-element.156.grad_ref, bf16[512,1536]{1,0:T(8,128)(2,1)S(1)} %get-tuple-element.169.w_ref, bf16[2,512,512]{2,1,0:T(8,128)(2,1)S(1)} %get-tuple-element.129.xs_ref, ...), custom_call_target="tpu_custom_call" | custom-call | flops 1 | bytes 1 | tf_op jit(solution)/shard_map/pallas_call | solution.py:907
  128.0 0.5 collective-permute-done.21
  128.4 0.1 slice_add_fusion.2
  128.7 0.4 collective-permute-start.22
  129.2 4.2 %collective-permute-done.23.got_ref = bf16[544,512]{1,0:T(8,128)(2,1)S(1)} collective-permute-done((bf16[544,512]{1,0:T(8,128)(2,1)S(1)}, bf16[544,512]{1,0:T(8,128)(2,1)S(1)}, u32[]{:S(2)}, u32[]{:S(2)}) %collective-permute-start.23) | collective-permute-done | bytes 557088 | tf_op jit(solution)/shard_map/ppermute | solution.py:695
  133.3 0.1 shard_map.325
  133.5 1.5 collective-permute-start.24
  135.0 2.1 %collective-permute-done.25 = bf16[2,64,1152]{2,1,0:T(8,128)(2,1)S(1)} collective-permute-done((bf16[2,64,1152]{2,1,0:T(8,128)(2,1)S(1)}, bf16[2,64,1152]{2,1,0:T(8,128)(2,1)S(1)}, u32[]{:S(2)}, u32[]{:S(2)}) %collective-permute-start.25) | collective-permute-done | bytes 294944 | tf_op jit(solution)/shard_map/ppermute | solution.py:695
  137.3 7.6 %collective-permute-done.24.got_ref = bf16[288,512]{1,0:T(8,128)(2,1)S(1)} collective-permute-done((bf16[288,512]{1,0:T(8,128)(2,1)S(1)}, bf16[288,512]{1,0:T(8,128)(2,1)S(1)}, u32[]{:S(2)}, u32[]{:S(2)}) %collective-permute-start.24) | collective-permute-done | bytes 294944 | tf_op jit(solution)/shard_map/ppermute | solution.py:695
  145.1 3.4 %collective-permute-start.26 = (bf16[80,512]{1,0:T(8,128)(2,1)S(1)}, bf16[80,512]{1,0:T(8,128)(2,1)S(1)}, u32[]{:S(2)}, u32[]{:S(2)}) collective-permute-start(bf16[80,512]{1,0:T(8,128)(2,1)S(1)} %get-tuple-element.181.refs_1_), channel_id=1, source_target_pairs={{0,16},{1,17},{2,18},{3,19},{4,20},{5,21},{6,22},{7,23},{8,24},{9,... | collective-permute-start | bytes 245768 | tf_op jit(solution)/shard_map/ppermute | solution.py:723
  148.5 3.0 %shard_map.327 = (bf16[2,512,512]{2,1,0:T(8,128)(2,1)}, bf16[2,512,512]{2,1,0:T(8,128)(2,1)S(1)}, f32[2,512,128]{2,1,0:T(8,128)S(1)}) custom-call(s32[2]{0:T(128)S(1)} %copy-done.3, bf16[2,512,512]{2,1,0:T(8,128)(2,1)S(1)} %get-tuple-element.143.result_ref, bf16[2,2,128,512]{3,2,1,0:T(8,128)(2,1)S(1)} %collective-permute-done.22.right_ref, ...), custom_call_target="tpu_custom_call" | custom-call | flops 1 | bytes 1 | tf_op jit(solution)/shard_map/pallas_call | solution.py:915
  151.5 0.7 shard_map.328
  152.2 1.3 collective-permute-done.26.refs_2_
  153.5 3.6 %shard_map.329 = (f32[2,512,512]{2,1,0:T(8,128)}, f32[64,128]{1,0:T(8,128)}, f32[64,128]{1,0:T(8,128)}, f32[64,128]{1,0:T(8,128)}, f32[1,2048]{1,0:T(1,128)}, /*...) custom-call(s32[2]{0:T(128)S(1)} %copy-done.4, ...), custom_call_target="tpu_custom_call" | custom-call | flops 1 | bytes 1 | tf_op jit(solution)/shard_map/pallas_call | solution.py:945
  (93 shorter events, 1.7 us)
Async XLA Ops:
  1.2 16.5 %copy-start.1 = (bf16[2,512,512]{2,1,0:T(8,128)(2,1)S(1)}, bf16[2,512,512]{2,1,0:T(8,128)(2,1)}, u32[]{:S(2)}) copy-start(bf16[2,512,512]{2,1,0:T(8,128)(2,1)} %x_ref.5) | copy-start | bytes 3145732
  5.1 12.7 %copy-start.15 = (bf16[1,64,1152]{2,1,0:T(8,128)(2,1)S(1)}, bf16[1,64,1152]{2,1,0:T(8,128)(2,1)}, u32[]{:S(2)}) copy-start(bf16[1,64,1152]{2,1,0:T(8,128)(2,1)} %get-tuple-element.118) | copy-start | bytes 442372
  5.1 11.0 %collective-permute-start.2 = (bf16[1,64,512]{2,1,0:T(8,128)(2,1)}, bf16[1,64,512]{2,1,0:T(8,128)(2,1)S(1)}, u32[]{:S(2)}, u32[]{:S(2)}) collective-permute-start(bf16[1,64,512]{2,1,0:T(8,128)(2,1)} %get-tuple-element.113), channel_id=1, source_target_pairs={{0,24},{1,25},{2,26},{3,27},{4,28},{5,29},{6,30},{7,31},{8,16},{9,... | collective-permute-start | bytes 196616 | tf_op jit(solution)/shard_map/ppermute | solution.py:723
  10.2 5.9 %collective-permute-start.1 = (bf16[1,64,512]{2,1,0:T(8,128)(2,1)}, bf16[1,64,512]{2,1,0:T(8,128)(2,1)S(1)}, u32[]{:S(2)}, u32[]{:S(2)}) collective-permute-start(bf16[1,64,512]{2,1,0:T(8,128)(2,1)} %get-tuple-element.113), channel_id=1, source_target_pairs={{0,8},{1,9},{2,10},{3,11},{4,12},{5,13},{6,14},{7,15},{8,0},{9,1},... | collective-permute-start | bytes 196616 | tf_op jit(solution)/shard_map/ppermute | solution.py:723
  10.3 5.8 %collective-permute-start = (bf16[1,64,512]{2,1,0:T(8,128)(2,1)}, bf16[1,64,512]{2,1,0:T(8,128)(2,1)S(1)}, u32[]{:S(2)}, u32[]{:S(2)}) collective-permute-start(bf16[1,64,512]{2,1,0:T(8,128)(2,1)} %get-tuple-element.113), channel_id=1, source_target_pairs={{0,16},{1,17},{2,18},{3,19},{4,20},{5,21},{6,22},{7,23},{8,24},{9,... | collective-permute-start | bytes 196616 | tf_op jit(solution)/shard_map/ppermute | solution.py:723
  16.2 1.6 copy-start.16
  16.2 6.4 %collective-permute-start.4 = (bf16[4,64,512]{2,1,0:T(8,128)(2,1)S(1)}, bf16[4,64,512]{2,1,0:T(8,128)(2,1)S(1)}, u32[]{:S(2)}, u32[]{:S(2)}) collective-permute-start(bf16[4,64,512]{2,1,0:T(8,128)(2,1)S(1)} %get-tuple-element.213), channel_id=1, source_target_pairs={{0,2},{1,5},{2,0},{3,7},{4,6},{5,1},{6,4},{7,3},{8,10},{9,13},{10,... | collective-permute-start | bytes 786440 | tf_op jit(solution)/shard_map/ppermute | solution.py:695
  17.8 8.3 %collective-permute-start.7 = (bf16[1,64,1152]{2,1,0:T(8,128)(2,1)S(1)}, bf16[1,64,1152]{2,1,0:T(8,128)(2,1)S(1)}, u32[]{:S(2)}, u32[]{:S(2)}) collective-permute-start(bf16[1,64,1152]{2,1,0:T(8,128)(2,1)S(1)} %copy-done.15), channel_id=1, source_target_pairs={{0,16},{1,17},{2,18},{3,19},{4,20},{5,21},{6,22},{7,23},{8,24},{9,... | collective-permute-start | bytes 442376 | tf_op jit(solution)/shard_map/ppermute | solution.py:695
  23.4 14.0 %collective-permute-start.5 = (bf16[8,64,512]{2,1,0:T(8,128)(2,1)}, bf16[8,64,512]{2,1,0:T(8,128)(2,1)S(1)}, u32[]{:S(2)}, u32[]{:S(2)}) collective-permute-start(bf16[8,64,512]{2,1,0:T(8,128)(2,1)} %get-tuple-element.209), channel_id=1, source_target_pairs={{0,4},{1,3},{2,6},{3,1},{4,0},{5,7},{6,2},{7,5},{8,12},{9,11},{10,... | collective-permute-start | bytes 1572872 | tf_op jit(solution)/shard_map/ppermute | solution.py:695
  25.1 12.2 %collective-permute-start.3 = (bf16[2,128,512]{2,1,0:T(8,128)(2,1)S(1)}, bf16[2,128,512]{2,1,0:T(8,128)(2,1)S(1)}, u32[]{:S(2)}, u32[]{:S(2)}) collective-permute-start(bf16[2,128,512]{2,1,0:T(8,128)(2,1)S(1)} %slice.58), channel_id=1, source_target_pairs={{0,1},{1,2},{2,3},{3,4},{4,5},{5,6},{6,7},{7,8},{8,9},{9,10},{10,1... | collective-permute-start | bytes 786440 | tf_op jit(solution)/shard_map/ppermute | solution.py:698
  26.2 11.6 %copy-start.17 = (bf16[2,128,512]{2,1,0:T(8,128)(2,1)S(1)}, bf16[2,128,512]{2,1,0:T(8,128)(2,1)}, u32[]{:S(2)}) copy-start(bf16[2,128,512]{2,1,0:T(8,128)(2,1)} %get-tuple-element.123) | copy-start | bytes 786436
  26.2 11.4 %collective-permute-start.8 = (bf16[2,64,1152]{2,1,0:T(8,128)(2,1)S(1)}, bf16[2,64,1152]{2,1,0:T(8,128)(2,1)S(1)}, u32[]{:S(2)}, u32[]{:S(2)}) collective-permute-start(bf16[2,64,1152]{2,1,0:T(8,128)(2,1)S(1)} %pad_maximum_fusion.3), channel_id=1, source_target_pairs={{0,8},{1,9},{2,10},{3,11},{4,12},{5,13},{6,14},{7,15},{8,0},{9,1},... | collective-permute-start | bytes 884744 | tf_op jit(solution)/shard_map/ppermute | solution.py:695
  37.4 2.8 %copy-start.2 = (s32[2,8]{1,0:T(2,128)S(1)}, s32[2,8]{1,0:T(2,128)}, u32[]{:S(2)}) copy-start(s32[2,8]{1,0:T(2,128)} %lengths.15) | copy-start | bytes 196
  37.4 2.8 %copy-start.3 = (s32[2]{0:T(128)S(1)}, s32[2]{0:T(128)}, u32[]{:S(2)}) copy-start(s32[2]{0:T(128)} %offsets.19) | copy-start | bytes 28
  37.4 2.8 %copy-start.4 = (s32[2]{0:T(128)S(1)}, s32[2]{0:T(128)}, u32[]{:S(2)}) copy-start(s32[2]{0:T(128)} %pad_add_fusion.1.place.place_ref) | copy-start | bytes 28
  37.4 2.8 %copy-start.6 = (f32[512]{0:T(512)S(1)}, f32[512]{0:T(512)}, u32[]{:S(2)}) copy-start(f32[512]{0:T(512)} %param.23) | copy-start | bytes 6148
  37.4 2.8 %copy-start.8 = (f32[512]{0:T(512)S(1)}, f32[512]{0:T(512)}, u32[]{:S(2)}) copy-start(f32[512]{0:T(512)} %param.24) | copy-start | bytes 6148
  37.4 2.8 %copy-start.12 = (f32[512]{0:T(512)S(1)}, f32[512]{0:T(512)}, u32[]{:S(2)}) copy-start(f32[512]{0:T(512)} %param.28) | copy-start | bytes 6148
  37.5 2.8 %copy-start.13 = (f32[512]{0:T(512)S(1)}, f32[512]{0:T(512)}, u32[]{:S(2)}) copy-start(f32[512]{0:T(512)} %param.29) | copy-start | bytes 6148
  37.5 2.7 %collective-permute-start.6 = (bf16[16,64,512]{2,1,0:T(8,128)(2,1)S(1)}, bf16[16,64,512]{2,1,0:T(8,128)(2,1)S(1)}, u32[]{:S(2)}, u32[]{:S(2)}) collective-permute-start(bf16[16,64,512]{2,1,0:T(8,128)(2,1)S(1)} %constant_dynamic-update-slice_fusion.9.near_ref), channel_id=1, source_target_pairs={{0,1},{1,0},{2,3},{3,2},{4,5},{5,4},{6,7},{7,6},{8,9},{9,8},{10,11... | collective-permute-start | bytes 3145736 | tf_op jit(solution)/shard_map/ppermute | solution.py:695
  37.7 12.8 %collective-permute-start.9 = (bf16[4,64,1152]{2,1,0:T(8,128)(2,1)S(1)}, bf16[4,64,1152]{2,1,0:T(8,128)(2,1)S(1)}, u32[]{:S(2)}, u32[]{:S(2)}) collective-permute-start(bf16[4,64,1152]{2,1,0:T(8,128)(2,1)S(1)} %pad_maximum_fusion.2), channel_id=1, source_target_pairs={{0,2},{1,5},{2,0},{3,7},{4,6},{5,1},{6,4},{7,3},{8,10},{9,13},{10,... | collective-permute-start | bytes 1769480 | tf_op jit(solution)/shard_map/ppermute | solution.py:695
  37.8 9.8 %collective-permute-start.10 = (bf16[2,128,512]{2,1,0:T(8,128)(2,1)S(1)}, bf16[2,128,512]{2,1,0:T(8,128)(2,1)S(1)}, u32[]{:S(2)}, u32[]{:S(2)}) collective-permute-start(bf16[2,128,512]{2,1,0:T(8,128)(2,1)S(1)} %copy-done.17), channel_id=1, source_target_pairs={{0,1},{1,2},{2,3},{3,4},{4,5},{5,6},{6,7},{7,8},{8,9},{9,10},{10,1... | collective-permute-start | bytes 786440 | tf_op jit(solution)/shard_map/ppermute | solution.py:698
  50.6 10.7 %collective-permute-start.11 = (bf16[8,64,640]{2,1,0:T(8,128)(2,1)S(1)}, bf16[8,64,640]{2,1,0:T(8,128)(2,1)S(1)}, u32[]{:S(2)}, u32[]{:S(2)}) collective-permute-start(bf16[8,64,640]{2,1,0:T(8,128)(2,1)S(1)} %slice.75), channel_id=1, source_target_pairs={{0,4},{1,3},{2,6},{3,1},{4,0},{5,7},{6,2},{7,5},{8,12},{9,11},{10,... | collective-permute-start | bytes 1966088 | tf_op jit(solution)/shard_map/ppermute | solution.py:695
  56.2 8.3 %copy-start = (bf16[2,2048,512]{2,1,0:T(8,128)(2,1)S(1)}, bf16[2,2048,512]{2,1,0:T(8,128)(2,1)}, u32[]{:S(2)}) copy-start(bf16[2,2048,512]{2,1,0:T(8,128)(2,1)} %cot_ref.3) | copy-start | bytes 12582916
  61.2 3.3 %copy-start.5 = (f32[2048]{0:T(1024)S(1)}, f32[2048]{0:T(1024)}, u32[]{:S(2)}) copy-start(f32[2048]{0:T(1024)} %param.35) | copy-start | bytes 24580
  61.2 3.3 %copy-start.7 = (f32[512]{0:T(512)S(1)}, f32[512]{0:T(512)}, u32[]{:S(2)}) copy-start(f32[512]{0:T(512)} %param.32) | copy-start | bytes 6148
  61.2 3.3 %copy-start.9 = (f32[512]{0:T(512)S(1)}, f32[512]{0:T(512)}, u32[]{:S(2)}) copy-start(f32[512]{0:T(512)} %param.31) | copy-start | bytes 6148
  61.2 3.3 %copy-start.10 = (f32[512]{0:T(512)S(1)}, f32[512]{0:T(512)}, u32[]{:S(2)}) copy-start(f32[512]{0:T(512)} %param.33) | copy-start | bytes 6148
  61.2 3.3 %copy-start.11 = (f32[512]{0:T(512)S(1)}, f32[512]{0:T(512)}, u32[]{:S(2)}) copy-start(f32[512]{0:T(512)} %param.37) | copy-start | bytes 6148
  61.4 3.1 %collective-permute-start.12 = (bf16[16,64,640]{2,1,0:T(8,128)(2,1)S(1)}, bf16[16,64,640]{2,1,0:T(8,128)(2,1)S(1)}, u32[]{:S(2)}, u32[]{:S(2)}) collective-permute-start(bf16[16,64,640]{2,1,0:T(8,128)(2,1)S(1)} %pad_maximum_fusion.near_ref), channel_id=1, source_target_pairs={{0,1},{1,0},{2,3},{3,2},{4,5},{5,4},{6,7},{7,6},{8,9},{9,8},{10,11... | collective-permute-start | bytes 3932168 | tf_op jit(solution)/shard_map/ppermute | solution.py:695
  61.5 16.5 %collective-permute-start.13 = (bf16[8,64,512]{2,1,0:T(8,128)(2,1)S(1)}, bf16[8,64,512]{2,1,0:T(8,128)(2,1)S(1)}, u32[]{:S(2)}, u32[]{:S(2)}) collective-permute-start(bf16[8,64,512]{2,1,0:T(8,128)(2,1)S(1)} %slice.76), channel_id=1, source_target_pairs={{0,4},{1,3},{2,6},{3,1},{4,0},{5,7},{6,2},{7,5},{8,12},{9,11},{10,... | collective-permute-start | bytes 1572872 | tf_op jit(solution)/shard_map/ppermute | solution.py:695
  78.1 2.7 %collective-permute-start.14 = (bf16[16,64,512]{2,1,0:T(8,128)(2,1)S(1)}, bf16[16,64,512]{2,1,0:T(8,128)(2,1)S(1)}, u32[]{:S(2)}, u32[]{:S(2)}) collective-permute-start(bf16[16,64,512]{2,1,0:T(8,128)(2,1)S(1)} %get-tuple-element.141), channel_id=1, source_target_pairs={{0,1},{1,0},{2,3},{3,2},{4,5},{5,4},{6,7},{7,6},{8,9},{9,8},{10,11... | collective-permute-start | bytes 3145736 | tf_op jit(solution)/shard_map/ppermute | solution.py:695
  78.3 4.7 %collective-permute-start.15 = (bf16[16,64,512]{2,1,0:T(8,128)(2,1)S(1)}, bf16[16,64,512]{2,1,0:T(8,128)(2,1)S(1)}, u32[]{:S(2)}, u32[]{:S(2)}) collective-permute-start(bf16[16,64,512]{2,1,0:T(8,128)(2,1)S(1)} %pad_maximum_fusion.1.near_ref), channel_id=1, source_target_pairs={{0,1},{1,0},{2,3},{3,2},{4,5},{5,4},{6,7},{7,6},{8,9},{9,8},{10,11... | collective-permute-start | bytes 3145736 | tf_op jit(solution)/shard_map/ppermute | solution.py:695
  81.2 15.6 %collective-permute-start.16 = (bf16[8,64,512]{2,1,0:T(8,128)(2,1)S(1)}, bf16[8,64,512]{2,1,0:T(8,128)(2,1)S(1)}, u32[]{:S(2)}, u32[]{:S(2)}) collective-permute-start(bf16[8,64,512]{2,1,0:T(8,128)(2,1)S(1)} %slice.103), channel_id=1, source_target_pairs={{0,4},{1,3},{2,6},{3,1},{4,0},{5,7},{6,2},{7,5},{8,12},{9,11},{10,... | collective-permute-start | bytes 1572872 | tf_op jit(solution)/shard_map/ppermute | solution.py:695
  97.0 6.4 %collective-permute-start.17 = (bf16[16,64,640]{2,1,0:T(8,128)(2,1)S(1)}, bf16[16,64,640]{2,1,0:T(8,128)(2,1)S(1)}, u32[]{:S(2)}, u32[]{:S(2)}) collective-permute-start(bf16[16,64,640]{2,1,0:T(8,128)(2,1)S(1)} %get-tuple-element.150), channel_id=1, source_target_pairs={{0,1},{1,0},{2,3},{3,2},{4,5},{5,4},{6,7},{7,6},{8,9},{9,8},{10,11... | collective-permute-start | bytes 3932168 | tf_op jit(solution)/shard_map/ppermute | solution.py:695
  101.3 8.2 %collective-permute-start.18 = (bf16[4,64,512]{2,1,0:T(8,128)(2,1)S(1)}, bf16[4,64,512]{2,1,0:T(8,128)(2,1)S(1)}, u32[]{:S(2)}, u32[]{:S(2)}) collective-permute-start(bf16[4,64,512]{2,1,0:T(8,128)(2,1)S(1)} %slice.105), channel_id=1, source_target_pairs={{0,2},{1,5},{2,0},{3,7},{4,6},{5,1},{6,4},{7,3},{8,10},{9,13},{10,... | collective-permute-start | bytes 786440 | tf_op jit(solution)/shard_map/ppermute | solution.py:695
  103.9 15.5 %collective-permute-start.20 = (bf16[8,64,640]{2,1,0:T(8,128)(2,1)S(1)}, bf16[8,64,640]{2,1,0:T(8,128)(2,1)S(1)}, u32[]{:S(2)}, u32[]{:S(2)}) collective-permute-start(bf16[8,64,640]{2,1,0:T(8,128)(2,1)S(1)} %slice.102), channel_id=1, source_target_pairs={{0,4},{1,3},{2,6},{3,1},{4,0},{5,7},{6,2},{7,5},{8,12},{9,11},{10,... | collective-permute-start | bytes 1966088 | tf_op jit(solution)/shard_map/ppermute | solution.py:695
  109.6 19.1 %copy-start.14 = (f32[4,64,512]{2,1,0:T(8,128)}, f32[4,64,512]{2,1,0:T(8,128)S(1)}, u32[]{:S(2)}) copy-start(f32[4,64,512]{2,1,0:T(8,128)S(1)} %slice_add_fusion.3) | copy-start | bytes 1572868
  119.3 2.8 %collective-permute-start.19 = (bf16[1056,512]{1,0:T(8,128)(2,1)S(1)}, bf16[1056,512]{1,0:T(8,128)(2,1)S(1)}, u32[]{:S(2)}, u32[]{:S(2)}) collective-permute-start(bf16[1056,512]{1,0:T(8,128)(2,1)S(1)} %get-tuple-element.165.mine_ref), channel_id=1, source_target_pairs={{0,1},{1,0},{2,3},{3,2},{4,5},{5,4},{6,7},{7,6},{8,9},{9,8},{10,11... | collective-permute-start | bytes 3244040 | tf_op jit(solution)/shard_map/ppermute | solution.py:695
  119.6 8.8 %collective-permute-start.21 = (bf16[4,64,640]{2,1,0:T(8,128)(2,1)S(1)}, bf16[4,64,640]{2,1,0:T(8,128)(2,1)S(1)}, u32[]{:S(2)}, u32[]{:S(2)}) collective-permute-start(bf16[4,64,640]{2,1,0:T(8,128)(2,1)S(1)} %slice.104), channel_id=1, source_target_pairs={{0,2},{1,5},{2,0},{3,7},{4,6},{5,1},{6,4},{7,3},{8,10},{9,13},{10,... | collective-permute-start | bytes 983048 | tf_op jit(solution)/shard_map/ppermute | solution.py:695
  122.4 11.0 %collective-permute-start.23 = (bf16[544,512]{1,0:T(8,128)(2,1)S(1)}, bf16[544,512]{1,0:T(8,128)(2,1)S(1)}, u32[]{:S(2)}, u32[]{:S(2)}) collective-permute-start(bf16[544,512]{1,0:T(8,128)(2,1)S(1)} %get-tuple-element.168.mine_ref), channel_id=1, source_target_pairs={{0,4},{1,3},{2,6},{3,1},{4,0},{5,7},{6,2},{7,5},{8,12},{9,11},{10,... | collective-permute-start | bytes 1671176 | tf_op jit(solution)/shard_map/ppermute | solution.py:695
  128.6 8.5 %collective-permute-start.25 = (bf16[2,64,1152]{2,1,0:T(8,128)(2,1)S(1)}, bf16[2,64,1152]{2,1,0:T(8,128)(2,1)S(1)}, u32[]{:S(2)}, u32[]{:S(2)}) collective-permute-start(bf16[2,64,1152]{2,1,0:T(8,128)(2,1)S(1)} %pad_maximum_fusion.4), channel_id=1, source_target_pairs={{0,8},{1,9},{2,10},{3,11},{4,12},{5,13},{6,14},{7,15},{8,0},{9,1},... | collective-permute-start | bytes 884744 | tf_op jit(solution)/shard_map/ppermute | solution.py:695
  128.7 8.4 %slice-start = ((f32[4,64,512]{2,1,0:T(8,128)}), f32[2,64,512]{2,1,0:T(8,128)S(1)}, s32[]{:S(2)}) async-start(f32[4,64,512]{2,1,0:T(8,128)} %copy-done.14), calls=%async_computation | async-start | bytes 524288 | tf_op jit(solution)/shard_map/slice | solution.py:734
  128.7 19.8 %collective-permute-start.22 = (bf16[2,2,128,512]{3,2,1,0:T(8,128)(2,1)S(1)}, bf16[2,2,128,512]{3,2,1,0:T(8,128)(2,1)S(1)}, u32[]{:S(2)}, u32[]{:S(2)}) collective-permute-start(bf16[2,2,128,512]{3,2,1,0:T(8,128)(2,1)S(1)} %get-tuple-element.174), channel_id=1, source_target_pairs={{0,31},{1,0},{2,1},{3,2},{4,3},{5,4},{6,5},{7,6},{8,7},{9,8},{10,9... | collective-permute-start | bytes 1572872 | tf_op jit(solution)/shard_map/ppermute | solution.py:698
  133.5 11.4 %collective-permute-start.24 = (bf16[288,512]{1,0:T(8,128)(2,1)S(1)}, bf16[288,512]{1,0:T(8,128)(2,1)S(1)}, u32[]{:S(2)}, u32[]{:S(2)}) collective-permute-start(bf16[288,512]{1,0:T(8,128)(2,1)S(1)} %get-tuple-element.178.mine_ref), channel_id=1, source_target_pairs={{0,2},{1,5},{2,0},{3,7},{4,6},{5,1},{6,4},{7,3},{8,10},{9,13},{10,... | collective-permute-start | bytes 884744 | tf_op jit(solution)/shard_map/ppermute | solution.py:695
  137.2 14.3 %collective-permute-start.27 = (bf16[1,64,1152]{2,1,0:T(8,128)(2,1)S(1)}, bf16[1,64,1152]{2,1,0:T(8,128)(2,1)S(1)}, u32[]{:S(2)}, u32[]{:S(2)}) collective-permute-start(bf16[1,64,1152]{2,1,0:T(8,128)(2,1)S(1)} %slice.107), channel_id=1, source_target_pairs={{0,16},{1,17},{2,18},{3,19},{4,20},{5,21},{6,22},{7,23},{8,24},{9,... | collective-permute-start | bytes 442376 | tf_op jit(solution)/shard_map/ppermute | solution.py:695
  144.9 7.3 %collective-permute-start.28 = (bf16[80,512]{1,0:T(8,128)(2,1)S(1)}, bf16[80,512]{1,0:T(8,128)(2,1)S(1)}, u32[]{:S(2)}, u32[]{:S(2)}) collective-permute-start(bf16[80,512]{1,0:T(8,128)(2,1)S(1)} %get-tuple-element.190), channel_id=1, source_target_pairs={{0,8},{1,9},{2,10},{3,11},{4,12},{5,13},{6,14},{7,15},{8,0},{9,1},... | collective-permute-start | bytes 245768 | tf_op jit(solution)/shard_map/ppermute | solution.py:723
  145.0 7.2 %collective-permute-start.29 = (bf16[80,512]{1,0:T(8,128)(2,1)S(1)}, bf16[80,512]{1,0:T(8,128)(2,1)S(1)}, u32[]{:S(2)}, u32[]{:S(2)}) collective-permute-start(bf16[80,512]{1,0:T(8,128)(2,1)S(1)} %get-tuple-element.192), channel_id=1, source_target_pairs={{0,24},{1,25},{2,26},{3,27},{4,28},{5,29},{6,30},{7,31},{8,16},{9,... | collective-permute-start | bytes 245768 | tf_op jit(solution)/shard_map/ppermute | solution.py:723
  145.1 8.4 %collective-permute-start.26 = (bf16[80,512]{1,0:T(8,128)(2,1)S(1)}, bf16[80,512]{1,0:T(8,128)(2,1)S(1)}, u32[]{:S(2)}, u32[]{:S(2)}) collective-permute-start(bf16[80,512]{1,0:T(8,128)(2,1)S(1)} %get-tuple-element.181.refs_1_), channel_id=1, source_target_pairs={{0,16},{1,17},{2,18},{3,19},{4,20},{5,21},{6,22},{7,23},{8,24},{9,... | collective-permute-start | bytes 245768 | tf_op jit(solution)/shard_map/ppermute | solution.py:723
